TPU v7x, 128 devices: a whole 4x4x4 slice. The times are simulated.
128 devices in a mesh: chan: 32 (over x, z_lo, y), sub: 4 (over z_hi, core).
Axes of the slice: x: 4, y: 4, z: 4 (z_hi: 2, z_lo: 2; z = z_hi * 2 + z_lo), core: 2. Of those that a mesh axis runs over, the one named last changes fastest.
Arguments:
- traces: bfloat16 [16384, 16384], P(('chan', 'sub')), may hold values from -6 to 6
- fan_mask: int32 [512, 16384], P('chan'), may hold values from 0 to 1, as said below
- band_edges: int32 [66], replicated, may hold values from 0 to 511, as said below
Outputs:
- cepstra: float32 [16, 64, 16384], P(None, None, ('chan', 'sub'))
Inputs may be any that keep to these rules, and one draw needn't show every extreme that they name: `fan_mask`: 0 or 1 for each frequency bin and wavenumber index. `band_edges`: strictly increasing; the first is 0 and the last is 511.
All inputs are finite; a program needn't handle non-finite values.
Results may differ from a plain program's by a relative error of at most 0.006.
Values may be sent and summed in bfloat16 or wider, within the bound.
No kernel may reach another device: no remote copies, remote signals or barrier semaphores. Data moves between devices by JAX's collectives and lax.ppermute only.
A program may use at most 128 MiB of HBM per device.

v0:
```python
import math

import jax
import jax.numpy as jnp
from jax import lax
from jax.sharding import PartitionSpec as P

NCH = 16384
N1 = 128
N2 = 128
FLEN = 1024
NF = 512
NB = 64
FRAMES = 16


energy_floor = 0.05


def time_table(frame_len, bin_count):
    sample_index = jnp.arange(frame_len, dtype=jnp.int32)
    freq_index = jnp.arange(bin_count, dtype=jnp.int32)
    hann_window = 0.5 - 0.5 * jnp.cos(2.0 * math.pi / frame_len * sample_index.astype(jnp.float32))
    phases = (
        2.0
        * math.pi
        / frame_len
        * (freq_index[:, None] * sample_index[None, :] % frame_len).astype(jnp.float32)
    )
    factor = (0.375 * frame_len) ** (-0.5)
    real_part = jnp.cos(phases) * hann_window[None, :] * factor
    imag_part = -jnp.sin(phases) * hann_window[None, :] * factor
    return jnp.stack([real_part, imag_part], axis=0).astype(jnp.bfloat16)


def dft_block(out_index, in_index, length, sign_value):
    phases = (
        2.0
        * math.pi
        / length
        * (out_index[:, None] * in_index[None, :] % length).astype(jnp.float32)
    )
    factor = length ** (-0.5)
    real_part = jnp.cos(phases) * factor
    imag_part = sign_value * jnp.sin(phases) * factor
    top_half = jnp.stack([real_part, -imag_part], axis=1)
    bottom = jnp.stack([imag_part, real_part], axis=1)
    return jnp.stack([top_half, bottom], axis=0).astype(jnp.bfloat16)


def twiddle(out_index, in_index, total_len, sign_value):
    phases = (
        2.0
        * math.pi
        / total_len
        * (out_index[:, None] * in_index[None, :] % total_len).astype(jnp.float32)
    )
    return (jnp.cos(phases), sign_value * jnp.sin(phases))


def rotate(values, cos_part, sin_part):
    real_part = values[0] * cos_part - values[1] * sin_part
    imag_part = values[0] * sin_part + values[1] * cos_part
    return jnp.stack([real_part, imag_part], axis=0)


def spread_order(chan_count, sub_count, per_block):
    ordering = jnp.arange(chan_count * sub_count * per_block, dtype=jnp.int32)
    outer_part = ordering // (chan_count * per_block)
    remainder = ordering % (chan_count * per_block)
    return (remainder // per_block * sub_count + outer_part) * per_block + remainder % per_block


def band_weights(band_edges, bin_count):
    bounds = band_edges.astype(jnp.float32)
    freq_value = jnp.arange(bin_count, dtype=jnp.int32).astype(jnp.float32)[None, :]
    lower_edge = bounds[:-2, None]
    middle = bounds[1:-1, None]
    upper_edge = bounds[2:, None]
    rising = (freq_value - lower_edge) / (middle - lower_edge)
    falling = (upper_edge - freq_value) / (upper_edge - middle)
    return jnp.maximum(jnp.minimum(rising, falling), 0.0).astype(jnp.bfloat16)


def cosine_table(band_count):
    ordering = jnp.arange(band_count, dtype=jnp.int32)
    phases = (
        math.pi
        / (2 * band_count)
        * (ordering[:, None] * (2 * ordering[None, :] + 1) % (4 * band_count)).astype(jnp.float32)
    )
    weight = jnp.where(ordering == 0, (1.0 / band_count) ** 0.5, (2.0 / band_count) ** 0.5)
    return jnp.cos(phases) * weight[:, None]


def power_from(values):
    real_part = values[0].astype(jnp.float32)
    imag_part = values[1].astype(jnp.float32)
    return (real_part * real_part + imag_part * imag_part).astype(jnp.bfloat16)


def received_power(returned):
    return power_from(returned)


def shards(traces, fan_mask, band_edges):
    chan_count = lax.axis_size("chan")
    sub_count = lax.axis_size("sub")
    sub_place = lax.axis_index("sub")
    channels = traces.shape[0]
    per_block = channels // N1
    freq_rows = fan_mask.shape[0]
    frame_rows = traces.reshape(channels, FRAMES, FLEN)
    table_time = time_table(FLEN, NF)
    first_index = jnp.arange(N1, dtype=jnp.int32)
    second_index = jnp.arange(N2, dtype=jnp.int32)
    spread_index = spread_order(chan_count, sub_count, per_block)
    first_table = dft_block(second_index, spread_index, N2, -1.0)
    second_table = dft_block(first_index, first_index, N1, -1.0)
    third_table = dft_block(first_index, first_index, N1, 1.0)
    fourth_table = dft_block(second_index, second_index, N2, 1.0)
    fwd_cos, fwd_sin = twiddle(second_index, first_index, NCH, -1.0)
    inv_cos, inv_sin = twiddle(second_index, first_index, NCH, 1.0)
    weights = band_weights(band_edges, NF)
    cosine = cosine_table(NB)
    spectrum = jnp.einsum(
        "xft,cmt->xcfm", table_time, frame_rows, preferred_element_type=jnp.float32
    ).astype(jnp.bfloat16)
    spectrum = spectrum.reshape(2, channels, NF * FRAMES)
    by_freq = lax.all_to_all(spectrum, "chan", split_axis=2, concat_axis=1, tiled=True)
    rows_here = by_freq.shape[2]
    by_freq = by_freq.reshape(2, chan_count * per_block, N1, rows_here)
    inner_share = N1 // sub_count
    outer_share = N2 // sub_count
    fwd_cos_part = lax.dynamic_slice_in_dim(fwd_cos, sub_place * inner_share, inner_share, 1)
    fwd_sin_part = lax.dynamic_slice_in_dim(fwd_sin, sub_place * inner_share, inner_share, 1)
    inv_cos_part = lax.dynamic_slice_in_dim(inv_cos, sub_place * outer_share, outer_share, 0)
    inv_sin_part = lax.dynamic_slice_in_dim(inv_sin, sub_place * outer_share, outer_share, 0)
    summed = jnp.einsum(
        "ykxc,xcvr->ykvr",
        first_table,
        lax.all_to_all(by_freq, "sub", split_axis=2, concat_axis=1, tiled=True),
        preferred_element_type=jnp.float32,
    )
    section_one = rotate(summed, fwd_cos_part[:, :, None], fwd_sin_part[:, :, None]).astype(
        jnp.bfloat16
    )
    section_two = jnp.einsum(
        "ykxc,xucr->yukr",
        second_table,
        lax.all_to_all(section_one, "sub", split_axis=1, concat_axis=2, tiled=True),
        preferred_element_type=jnp.float32,
    ).astype(jnp.bfloat16)
    mask_block = lax.dynamic_slice_in_dim(
        fan_mask.reshape(freq_rows, N1, N2), sub_place * outer_share, outer_share, 2
    )
    mask_rows = jnp.broadcast_to(
        jnp.transpose(mask_block, (2, 1, 0))[:, :, :, None], (outer_share, N1, freq_rows, FRAMES)
    )
    mask_rows = mask_rows.reshape(outer_share, N1, freq_rows * FRAMES)
    kept_cells = jnp.where(mask_rows[None] > 0, section_two, jnp.zeros_like(section_two))
    inverse_sum = jnp.einsum(
        "ycxk,xukr->yucr", third_table, kept_cells, preferred_element_type=jnp.float32
    )
    section_three = rotate(inverse_sum, inv_cos_part[:, :, None], inv_sin_part[:, :, None]).astype(
        jnp.bfloat16
    )
    filtered = jnp.einsum(
        "ydxu,xuvr->ydvr",
        fourth_table,
        lax.all_to_all(section_three, "sub", split_axis=2, concat_axis=1, tiled=True),
        preferred_element_type=jnp.float32,
    ).astype(jnp.bfloat16)
    returned = lax.all_to_all(
        lax.all_to_all(filtered, "chan", split_axis=1, concat_axis=3, tiled=True),
        "sub",
        split_axis=1,
        concat_axis=2,
        tiled=True,
    )
    returned = returned.reshape(returned.shape[0], channels, NF, FRAMES)
    power = received_power(returned)
    energy = jnp.einsum("bf,cfm->mbc", weights, power, preferred_element_type=jnp.float32)
    logs = jnp.log(jnp.maximum(energy, energy_floor))
    return jnp.einsum("qb,mbc->mqc", cosine, logs, precision=lax.Precision.HIGHEST)


def solution(mesh):
    in_specs = (P(("chan", "sub"), None), P("chan", None), P())
    out_specs = P(None, None, ("chan", "sub"))
    return jax.shard_map(shards, mesh=mesh, in_specs=in_specs, out_specs=out_specs, check_vma=False)
```

profile of v0, /device:TPU:1, one launch (start us, length us, event | category | flops | bytes accessed | tf_op | source)
XLA Modules:
  0.0 484.1 jit_solution(4365405582803618030)
XLA Ops:
  0.0 8.8 %multiply_convert_fusion.1 = (bf16[1,512,1024]{2,1,0:T(8,128)(2,1)S(1)}, bf16[1,512,1024]{2,1,0:T(8,128)(2,1)S(1)}) fusion(f32[1024]{0:T(1024)S(1)} %multiply_subtract_fusion), kind=kLoop, calls=%fused_computation.36 | loop fusion | flops 11010048 | bytes 2101248 | tf_op jit(solution)/shard_map/convert.12
  8.9 6.4 %convert_bitcast_fusion = bf16[2,128,512,16]{1,2,3,0:T(8,128)(2,1)S(1)} fusion(bf16[16,16,8,1024]{3,2,1,0:T(8,128)(2,1)} %bitcast.144, bf16[1,512,1024]{2,1,0:T(8,128)(2,1)S(1)} %get-tuple-element.16, bf16[1,512,1024]{2,1,0:T(8,128)(2,1)S(1)} %get-tuple-element.15), kind=kOutput, calls=%fused_computation.19 | convolution fusion | flops 4301258752 | bytes 10485760 | tf_op jit(solution)/shard_map/xft,cmt->xcfm/dot_general | solution.py:126
  15.3 2.7 copy.42
  18.0 35.5 %copy.43 = bf16[2,128,8192]{1,0,2:T(2,128)(2,1)S(1)} copy(bf16[2,128,8192]{1,2,0:T(8,128)(2,1)S(1)} %bitcast.135) | data formatting | bytes 8388608 | tf_op jit(solution)/shard_map/reshape | solution.py:129
  53.5 57.6 %all_to_all.96 = bf16[2,128,8192]{1,0,2:T(2,128)(2,1)} all-to-all(bf16[2,128,8192]{1,0,2:T(2,128)(2,1)S(1)} %copy.43), channel_id=1, replica_groups=mesh['chan'=32,'sub'=4] {'chan'}, dimensions={2} | all-to-all | bytes 8388608 | tf_op jit(solution)/shard_map/all_to_all | solution.py:130
  111.1 8.3 %copy.44 = bf16[2,128,32,256]{3,2,0,1:T(8,128)(2,1)} copy(bf16[2,128,32,256]{1,0,3,2:T(2,128)(2,1)} %bitcast.136) | data formatting | bytes 8388608 | tf_op jit(solution)/shard_map/all_to_all | solution.py:130
  119.4 8.1 %all-to-all-start.1 = ((bf16[2,32,128,256]{3,1,0,2:T(8,128)(2,1)}), bf16[2,32,128,256]{3,1,0,2:T(8,128)(2,1)}, u32[]{:S(2)}, u32[]{:S(2)}) async-start(bf16[2,32,128,256]{3,1,0,2:T(8,128)(2,1)} %bitcast.133), calls=%async_computation.1 | async-start | bytes 8388608 | tf_op jit(solution)/shard_map/all_to_all | solution.py:142
  127.5 0.3 fusion.86
  127.8 0.3 fusion.87
  128.1 0.3 negate_convert_fusion.1
  128.4 47.9 %all-to-all-done.1 = bf16[2,32,128,256]{3,1,0,2:T(8,128)(2,1)} async-done(((bf16[2,32,128,256]{3,1,0,2:T(8,128)(2,1)}), bf16[2,32,128,256]{3,1,0,2:T(8,128)(2,1)}, u32[]{:S(2)}, u32[]{:S(2)}) %all-to-all-start.1) | async-done | bytes 4194336 | tf_op jit(solution)/shard_map/all_to_all | solution.py:142
  176.3 2.6 copy.46
  179.0 1.3 convolution_bitcast_fusion
  180.2 1.4 subtract_convert_fusion.1
  181.7 0.4 pad_maximum_fusion
  182.1 4.4 copy.47
  186.5 6.0 %all-to-all-start.2 = ((bf16[2,128,32,256]{3,2,0,1:T(8,128)(2,1)}), bf16[2,128,32,256]{3,2,0,1:T(8,128)(2,1)}, u32[]{:S(2)}, u32[]{:S(2)}) async-start(bf16[2,128,32,256]{3,2,0,1:T(8,128)(2,1)} %copy.47), calls=%async_computation.2 | async-start | bytes 8388608 | tf_op jit(solution)/shard_map/all_to_all | solution.py:151
  192.6 0.2 copy.75
  192.8 0.3 fusion.37
  193.1 0.4 copy.40
  193.5 0.1 constant_dynamic-slice_fusion
  193.6 0.1 copy.52
  193.7 0.3 multiply_convert_fusion.5
  194.0 0.3 negate_convert_fusion
  194.3 0.3 multiply_convert_fusion.3
  194.6 46.8 %all-to-all-done.2 = bf16[2,128,32,256]{3,2,0,1:T(8,128)(2,1)} async-done(((bf16[2,128,32,256]{3,2,0,1:T(8,128)(2,1)}), bf16[2,128,32,256]{3,2,0,1:T(8,128)(2,1)}, u32[]{:S(2)}, u32[]{:S(2)}) %all-to-all-start.2) | async-done | bytes 4194336 | tf_op jit(solution)/shard_map/all_to_all | solution.py:151
  241.4 4.8 copy.49
  246.2 0.3 broadcast_in_dim.15
  246.5 7.9 %fusion.10 = f32[2,32,128,256]{2,3,0,1:T(8,128)} fusion(pred[32,128,256]{1,2,0:T(8,128)(4,1)S(1)} %bitcast.143, bf16[2,32,128,256,1]{3,2,1,0,4:T(8,128)(2,1)} %bitcast.140, bf16[1,128,2,128]{3,1,2,0:T(8,128)(2,1)S(1)} %get-tuple-element.10, bf16[1,128,2,128]{3,1,2,0:T(8,128)(2,1)S(1)} %get-tuple-element.11, ...), kind=kOutput, calls=%fused_computation.21 | convolution fusion | flops 2152202240 | bytes 13893632 | tf_op jit(solution)/shard_map/ycxk,xukr->yucr/dot_general | solution.py:162
  254.5 4.8 subtract_convert_fusion
  259.3 2.3 pad_maximum_fusion.1
  261.6 11.3 %copy.53 = bf16[2,32,128,256]{3,0,1,2:T(2,128)(2,1)} copy(bf16[2,32,128,256]{2,3,0,1:T(8,128)(2,1)} %pad_maximum_fusion.1) | data formatting | bytes 8388608 | tf_op jit(solution)/shard_map/stack | solution.py:64
  272.9 53.5 %all_to_all.97 = bf16[2,32,128,256]{3,0,1,2:T(2,128)(2,1)S(1)} all-to-all(bf16[2,32,128,256]{3,0,1,2:T(2,128)(2,1)} %copy.53), channel_id=1, replica_groups=mesh['chan'=32,'sub'=4] {'sub'}, dimensions={2} | all-to-all | bytes 8388608 | tf_op jit(solution)/shard_map/all_to_all | solution.py:171
  326.4 2.4 copy.54
  328.8 2.4 copy.55
  331.2 1.3 bitcast_convert_fusion
  332.5 2.4 copy.56
  334.9 52.4 %all_to_all.98 = bf16[2,128,32,256]{3,2,0,1:T(8,128)(2,1)S(1)} all-to-all(bf16[2,128,32,256]{3,2,0,1:T(8,128)(2,1)S(1)} %copy.56), channel_id=1, replica_groups=mesh['chan'=32,'sub'=4] {'chan'}, dimensions={1} | all-to-all | bytes 8388608 | tf_op jit(solution)/shard_map/all_to_all | solution.py:175
  387.3 4.6 copy.97
  391.9 7.4 %all_to_all.88 = bf16[2,4,32,8192]{3,2,1,0:T(8,128)(2,1)} reshape(bf16[2,4,32,32,256]{4,3,2,1,0:T(8,128)(2,1)} %bitcast.139) | data formatting | bytes 8388608 | tf_op jit(solution)/shard_map/all_to_all | solution.py:175
  399.3 4.6 copy.58
  403.9 8.0 %all-to-all-start.5 = ((bf16[2,4,32,8192]{3,2,0,1:T(8,128)(2,1)}), bf16[2,4,32,8192]{3,2,0,1:T(8,128)(2,1)}, u32[]{:S(2)}, u32[]{:S(2)}) async-start(bf16[2,4,32,8192]{3,2,0,1:T(8,128)(2,1)} %copy.58), calls=%async_computation.5 | async-start | bytes 8388608 | tf_op jit(solution)/shard_map/all_to_all | solution.py:174
  412.0 48.8 %all-to-all-done.5 = bf16[2,4,32,8192]{3,2,0,1:T(8,128)(2,1)} async-done(((bf16[2,4,32,8192]{3,2,0,1:T(8,128)(2,1)}), bf16[2,4,32,8192]{3,2,0,1:T(8,128)(2,1)}, u32[]{:S(2)}, u32[]{:S(2)}) %all-to-all-start.5) | async-done | bytes 4194336 | tf_op jit(solution)/shard_map/all_to_all | solution.py:174
  460.8 3.0 add_convert_fusion
  463.8 8.4 %copy.59 = bf16[1,4,32,8192]{2,1,3,0:T(4,128)(2,1)} copy(bf16[1,4,32,8192]{3,2,0,1:T(8,128)(2,1)S(1)} %add_convert_fusion) | data formatting | bytes 4194304 | tf_op jit(solution)/shard_map/convert_element_type | solution.py:99
  472.2 9.5 %convert_element_type.168 = bf16[128,512,16]{0,2,1:T(8,128)(2,1)S(1)} reshape(bf16[1,4,32,8192]{2,1,3,0:T(4,128)(2,1)} %copy.59) | data formatting | bytes 4194304 | tf_op jit(solution)/shard_map/convert_element_type | solution.py:99
  481.7 0.6 fusion.34
  482.3 1.5 convolution_bitcast_fusion.1
  (15 shorter events, 0.2 us)
Async XLA Ops:
  119.4 56.9 %all-to-all-start.1 = ((bf16[2,32,128,256]{3,1,0,2:T(8,128)(2,1)}), bf16[2,32,128,256]{3,1,0,2:T(8,128)(2,1)}, u32[]{:S(2)}, u32[]{:S(2)}) async-start(bf16[2,32,128,256]{3,1,0,2:T(8,128)(2,1)} %bitcast.133), calls=%async_computation.1 | async-start | bytes 8388608 | tf_op jit(solution)/shard_map/all_to_all | solution.py:142
  186.5 6.1 %copy-start = (s32[16,16384]{1,0:T(8,128)S(1)}, s32[16,16384]{1,0:T(8,128)}, u32[]{:S(2)}) copy-start(s32[16,16384]{1,0:T(8,128)} %param.4) | copy-start | bytes 3145732
  186.5 54.9 %all-to-all-start.2 = ((bf16[2,128,32,256]{3,2,0,1:T(8,128)(2,1)}), bf16[2,128,32,256]{3,2,0,1:T(8,128)(2,1)}, u32[]{:S(2)}, u32[]{:S(2)}) async-start(bf16[2,128,32,256]{3,2,0,1:T(8,128)(2,1)} %copy.47), calls=%async_computation.2 | async-start | bytes 8388608 | tf_op jit(solution)/shard_map/all_to_all | solution.py:151
  403.9 8.0 %copy-start.1 = (s32[66]{0:T(128)S(1)}, s32[66]{0:T(128)}, u32[]{:S(2)}) copy-start(s32[66]{0:T(128)} %param.5) | copy-start | bytes 796
  403.9 56.9 %all-to-all-start.5 = ((bf16[2,4,32,8192]{3,2,0,1:T(8,128)(2,1)}), bf16[2,4,32,8192]{3,2,0,1:T(8,128)(2,1)}, u32[]{:S(2)}, u32[]{:S(2)}) async-start(bf16[2,4,32,8192]{3,2,0,1:T(8,128)(2,1)} %copy.58), calls=%async_computation.5 | async-start | bytes 8388608 | tf_op jit(solution)/shard_map/all_to_all | solution.py:174
where the time goes:
time: 491 us; the launch traced here: 484 us
  blocking collectives  163 us (33%)
  waiting for transfers between devices  144 us (29%)
  local copies, waits for them, and re-layouts  113 us (23%)
  other arithmetic  22.9 us (5%)
  starting transfers between devices  22.1 us (5%)
  matrix products  19 us (4%)
    all_to_all x1, blocking collectives, shards(): lax.all_to_all(spectrum, 'chan', split_axis=2, concat_axis=1, tiled=True)  57.6 us
    all_to_all x1, blocking collectives, shards(): lax.all_to_all(section_three, 'sub', split_axis=2, concat_axis=1, tiled=T...  53.5 us
    all_to_all x1, blocking collectives, shards(): lax.all_to_all(filtered, 'chan', split_axis=1, concat_axis=3, tiled=True)  52.4 us
    all_to_all x1, waiting for transfers between devices, shards(): lax.all_to_all(lax.all_to_all(filtered, 'chan', split_axis=1, concat_axis...  48.8 us
    all_to_all x1, waiting for transfers between devices, shards(): lax.all_to_all(by_freq, 'sub', split_axis=2, concat_axis=1, tiled=True)  47.9 us
    all_to_all x1, waiting for transfers between devices, shards(): lax.all_to_all(section_one, 'sub', split_axis=1, concat_axis=2, tiled=True)  46.8 us
    reshape x1, local copies, waits for them, and re-layouts, shards(): spectrum = spectrum.reshape(2, channels, NF * FRAMES)  35.5 us
    convert_element_type x2, local copies, waits for them, and re-layouts, power_from(): return (real_part * real_part + imag_part * imag_part).astype(jnp.bfloat16)  17.9 us
  transfers between devices with their start and end apart: 3, of which 3 were waited for; matrix products, arithmetic and copies ran while one was open for 1% of the time, Pallas kernels for 0%

commit v1 on v0

v1 whole, which is shorter than its diff:
```python
import functools
import math

import jax
import jax.numpy as jnp
import ml_dtypes
import numpy as np
from jax import lax
from jax.experimental import pallas as pl
from jax.experimental.pallas import tpu as pltpu
from jax.sharding import PartitionSpec as P

NCH = 16384
N1 = 128
N2 = 128
FLEN = 1024
NF = 512
NB = 64
FRAMES = 16
HALF = FRAMES // 2

energy_floor = 0.05


def time_table(devices):
    bins = NF // devices
    t = np.arange(FLEN)
    f = np.arange(NF)
    hann = 0.5 - 0.5 * np.cos(2.0 * math.pi * t / FLEN)
    phases = 2.0 * math.pi / FLEN * ((f[:, None] * t[None, :]) % FLEN)
    factor = (0.375 * FLEN) ** -0.5
    table = np.stack([np.cos(phases), -np.sin(phases)], axis=0) * (hann * factor)
    table = table.reshape(2, devices, bins, FLEN).transpose(1, 0, 2, 3)
    return table.reshape(2 * NF, FLEN).astype(ml_dtypes.bfloat16)


def dft_parts(length, sign):
    n = np.arange(length)
    phases = 2.0 * math.pi / length * ((n[:, None] * n[None, :]) % length)
    factor = length**-0.5
    return np.cos(phases) * factor, sign * np.sin(phases) * factor


def left_table(length, sign):
    re, im = dft_parts(length, sign)
    return np.block([[re, -im], [im, re]]).astype(ml_dtypes.bfloat16)


def right_table(length, sign):
    re, im = dft_parts(length, sign)
    return np.block([[re, im], [-im, re]]).astype(ml_dtypes.bfloat16)


def twiddle(sign):
    q = np.arange(N2)
    a = np.arange(N1)
    phases = 2.0 * math.pi / NCH * ((q[:, None] * a[None, :]) % NCH)
    return np.stack([np.cos(phases), sign * np.sin(phases)]).astype(np.float32)


def cosine_table():
    j = np.arange(NB)
    phases = math.pi / (2 * NB) * ((j[:, None] * (2 * j[None, :] + 1)) % (4 * NB))
    weight = np.where(j == 0, (1.0 / NB) ** 0.5, (2.0 / NB) ** 0.5)
    return (np.cos(phases) * weight[:, None]).astype(np.float32)


def band_weights(band_edges):
    bounds = band_edges.astype(jnp.float32)
    freq = jnp.arange(NF, dtype=jnp.int32).astype(jnp.float32)[None, :]
    low, middle, high = bounds[:-2, None], bounds[1:-1, None], bounds[2:, None]
    rising = (freq - low) / (middle - low)
    falling = (high - freq) / (high - middle)
    return jnp.maximum(jnp.minimum(rising, falling), 0.0).astype(jnp.bfloat16)


def spectrum_kernel(devices, table_ref, low_ref, high_ref, out_ref):
    rows = 2 * NF // devices
    low, high = low_ref[...], high_ref[...]
    samples = jnp.concatenate(
        [low[:, :FLEN], low[:, FLEN:], high[:, :FLEN], high[:, FLEN:]], axis=0
    )
    step = 256
    for start in range(0, 2 * NF, step):
        part = lax.dot_general(
            table_ref[start : start + step, :],
            samples,
            (((1,), (1,)), ((), ())),
            preferred_element_type=jnp.float32,
        )
        part = part.reshape(step // rows, rows, 4 * N1)
        both = jnp.concatenate([part[:, :, : 2 * N1], part[:, :, 2 * N1 :]], axis=1)
        out_ref[start // rows : (start + step) // rows] = both.astype(jnp.bfloat16)


def sections_kernel(
    bins,
    cells_ref,
    first_ref,
    second_ref,
    third_ref,
    fourth_ref,
    forward_ref,
    inverse_ref,
    mask_ref,
    power_ref,
    cells_f32,
    power_f32,
):
    rows = 4 * bins
    dot = functools.partial(jnp.dot, preferred_element_type=jnp.float32)
    bf16 = jnp.bfloat16
    for m in range(2):
        part = cells_ref[:, :, m * N1 : (m + 1) * N1].astype(jnp.float32)
        cells_f32[m] = part.reshape(N2 * rows, N1)
    fwd_cos, fwd_sin = forward_ref[0], forward_ref[1]
    inv_cos, inv_sin = inverse_ref[0], inverse_ref[1]
    for m in range(2):
        for half in range(2):
            for pair in range(bins // 2):
                bin_pair = (2 * pair, 2 * pair + 1)

                def cell(x, f):
                    at = half * 2 * bins + x * bins + f
                    return cells_f32[m, pl.ds(at, N2, stride=rows), :].astype(bf16)

                cells = jnp.concatenate(
                    [
                        jnp.concatenate([cell(x, f) for f in bin_pair], axis=1)
                        for x in range(2)
                    ],
                    axis=0,
                )
                summed = dot(first_ref[...], cells)
                rotated = []
                for i in range(2):
                    re = summed[:N2, i * N1 : (i + 1) * N1]
                    im = summed[N2:, i * N1 : (i + 1) * N1]
                    rotated.append(
                        jnp.concatenate(
                            [
                                (re * fwd_cos - im * fwd_sin).astype(bf16),
                                (re * fwd_sin + im * fwd_cos).astype(bf16),
                            ],
                            axis=1,
                        )
                    )
                section = dot(jnp.concatenate(rotated, axis=0), second_ref[...]).astype(bf16)
                masks = []
                for f in bin_pair:
                    mask = mask_ref[f]
                    masks.append(jnp.concatenate([mask, mask], axis=1))
                kept = section * jnp.concatenate(masks, axis=0)
                back = dot(kept, third_ref[...])
                re_parts, im_parts = [], []
                for i in range(2):
                    re = back[i * N2 : (i + 1) * N2, :N1]
                    im = back[i * N2 : (i + 1) * N2, N1:]
                    re_parts.append((re * inv_cos - im * inv_sin).astype(bf16))
                    im_parts.append((re * inv_sin + im * inv_cos).astype(bf16))
                turned = jnp.concatenate(
                    [
                        jnp.concatenate(re_parts, axis=1),
                        jnp.concatenate(im_parts, axis=1),
                    ],
                    axis=0,
                )
                filtered = dot(fourth_ref[...], turned).astype(bf16).astype(jnp.float32)
                re, im = filtered[:N2], filtered[N2:]
                power = re * re + im * im
                for i, f in enumerate(bin_pair):
                    at = m * 2 * bins + half * bins + f
                    power_f32[pl.ds(at, N2, stride=rows), :] = power[:, i * N1 : (i + 1) * N1]
    power_ref[...] = power_f32[...].reshape(N2, rows, N1).astype(bf16)


def cepstra_kernel(bins, power_ref, weights_ref, cosine_ref, out_ref, power_f32):
    rows = 4 * bins
    power_f32[...] = power_ref[...].astype(jnp.float32).reshape(N2 * rows, N1)
    columns = []
    for half in range(2):
        for m in range(2):
            at = m * 2 * bins + half * bins
            columns.append(
                jnp.concatenate(
                    [
                        power_f32[pl.ds(at + f, N2, stride=rows), :].astype(jnp.bfloat16)
                        for f in range(bins)
                    ],
                    axis=0,
                )
            )
    power = jnp.concatenate(columns, axis=1)
    energy = jnp.dot(weights_ref[...], power, preferred_element_type=jnp.float32)
    logs = jnp.log(jnp.maximum(energy, energy_floor))
    cepstra = jnp.dot(
        cosine_ref[...],
        logs,
        precision=lax.Precision.HIGHEST,
        preferred_element_type=jnp.float32,
    )
    for half in range(2):
        for m in range(2):
            at = (half * 2 + m) * N1
            out_ref[half, m] = cepstra[:, at : at + N1]


def whole(shape):
    return pl.BlockSpec(shape, lambda i: (0,) * len(shape))


VMEM_LIMIT = 48 * 1024 * 1024


def shards(traces, fan_mask, band_edges):
    axes = ("chan", "sub")
    devices = lax.axis_size("chan") * lax.axis_size("sub")
    sub_count = lax.axis_size("sub")
    bins = NF // devices
    rows = 4 * bins
    bf16 = jnp.bfloat16
    params = pltpu.CompilerParams(vmem_limit_bytes=VMEM_LIMIT)

    spectrum = pl.pallas_call(
        functools.partial(spectrum_kernel, devices),
        grid=(HALF // 2,),
        in_specs=[
            whole((2 * NF, FLEN)),
            pl.BlockSpec((N1, 2 * FLEN), lambda i: (0, i)),
            pl.BlockSpec((N1, 2 * FLEN), lambda i: (0, i + HALF // 2)),
        ],
        out_specs=pl.BlockSpec((devices, rows, 2 * N1), lambda i: (0, 0, i)),
        out_shape=jax.ShapeDtypeStruct((devices, rows, HALF * N1), bf16),
        compiler_params=params,
        name="spectrum",
    )(jnp.asarray(time_table(devices)), traces, traces)

    cells = lax.all_to_all(spectrum, axes, split_axis=0, concat_axis=0, tiled=True)

    mask = lax.dynamic_slice_in_dim(fan_mask, lax.axis_index("sub") * bins, bins, 0)
    mask = jnp.transpose(mask.reshape(bins, N1, N2), (0, 2, 1))
    mask = (mask > 0).astype(bf16)

    power = pl.pallas_call(
        functools.partial(sections_kernel, bins),
        grid=(HALF // 2,),
        in_specs=[
            pl.BlockSpec((N2, rows, 2 * N1), lambda i: (0, 0, i)),
            whole((2 * N2, 2 * N2)),
            whole((2 * N1, 2 * N1)),
            whole((2 * N1, 2 * N1)),
            whole((2 * N2, 2 * N2)),
            whole((2, N2, N1)),
            whole((2, N2, N1)),
            whole((bins, N2, N1)),
        ],
        out_specs=pl.BlockSpec((N2, rows, N1), lambda i: (0, 0, i)),
        out_shape=jax.ShapeDtypeStruct((N2, rows, HALF // 2 * N1), bf16),
        scratch_shapes=[
            pltpu.VMEM((2, N2 * rows, N1), jnp.float32),
            pltpu.VMEM((N2 * rows, N1), jnp.float32),
        ],
        compiler_params=params,
        name="sections",
    )(
        cells,
        jnp.asarray(left_table(N2, -1.0)),
        jnp.asarray(right_table(N1, -1.0)),
        jnp.asarray(right_table(N1, 1.0)),
        jnp.asarray(left_table(N2, 1.0)),
        jnp.asarray(twiddle(-1.0)),
        jnp.asarray(twiddle(1.0)),
        mask,
    )

    returned = lax.all_to_all(power, axes, split_axis=0, concat_axis=0, tiled=True)

    weights = band_weights(band_edges).reshape(NB, devices, bins)
    weights = jnp.transpose(weights, (0, 2, 1)).reshape(NB, NF)
    cepstra = pl.pallas_call(
        functools.partial(cepstra_kernel, bins),
        grid=(HALF // 2,),
        in_specs=[
            pl.BlockSpec((devices, rows, N1), lambda i: (0, 0, i)),
            whole((NB, NF)),
            whole((NB, NB)),
        ],
        out_specs=pl.BlockSpec((2, 2, NB, N1), lambda i: (0, i, 0, 0)),
        out_shape=jax.ShapeDtypeStruct((2, HALF, NB, N1), jnp.float32),
        scratch_shapes=[pltpu.VMEM((devices * rows, N1), jnp.float32)],
        compiler_params=params,
        name="cepstra",
    )(returned, weights, jnp.asarray(cosine_table()))
    return cepstra.reshape(FRAMES, NB, N1)


def solution(mesh):
    in_specs = (P(("chan", "sub"), None), P("chan", None), P())
    out_specs = P(None, None, ("chan", "sub"))
    return jax.shard_map(shards, mesh=mesh, in_specs=in_specs, out_specs=out_specs, check_vma=False)
```

time: 491 us -> 133 us (0.27); the launches traced: 484 us -> 132 us
  blocking collectives: 163 us -> 0 us
  local copies, waits for them, and re-layouts: 113 us -> 1.77 us
  waiting for transfers between devices: 144 us -> 80.2 us
  Pallas kernels: 0 us -> 29.4 us
  other arithmetic: 22.9 us -> 1.34 us
  matrix products: 19 us -> 0 us
    all_to_all x3 -> x0, blocking collectives: 163 us -> none  [the longest x1 57.6 us: shards(): lax.all_to_all(spectrum, 'chan', split_axis=2, concat_axis=1, tiled=True)]
    all_to_all x3 -> x2, waiting for transfers between devices: 144 us -> 80.2 us  [the longest x1 50.9 us: shards(): lax.all_to_all(spectrum, axes, split_axis=0, concat_axis=0, tiled=True)]
    all_to_all x8 -> x0, local copies, waits for them, and re-layouts: 37.2 us -> none  [the longest x3 16.6 us: shards(): lax.all_to_all(filtered, 'chan', split_axis=1, concat_axis=3, tiled=True)]
    reshape x1 -> x0, local copies, waits for them, and re-layouts: 35.5 us -> none  [shards(): spectrum = spectrum.reshape(2, channels, NF * FRAMES)]
    pallas_call x0 -> x3, Pallas kernels: none -> 29.4 us  [the longest x1 17.5 us: shards(): pl.pallas_call(functools.partial(sections_kernel, bins), grid=(HALF // 2,...]
    convert_element_type x4 -> x1, local copies, waits for them, and re-layouts: 23 us -> 0.13 us  [shards(): mask = (mask > 0).astype(bf16)]
    another operation x11 -> x0, other arithmetic: 19 us -> none
    dot_general x6 -> x0, matrix products: 19 us -> none  [the longest x1 7.91 us: shards(): jnp.einsum('ycxk,xukr->yucr', third_table, kept_cells, preferred_element_...]
  transfers between devices with their start and end apart: 3 -> 2, of which waited for: 3 -> 2; matrix products, arithmetic and copies ran while one was open for 1% -> 1% of each run, Pallas kernels for 0% -> 0%
where the time goes in v1:
time: 133 us; the launch traced here: 132 us
  waiting for transfers between devices  80.2 us (60%)
  Pallas kernels  29.4 us (22%)
  starting transfers between devices  19.6 us (15%)
  local copies, waits for them, and re-layouts  1.77 us (1%)
  other arithmetic  1.34 us (1%)
    all_to_all x1, waiting for transfers between devices, shards(): lax.all_to_all(spectrum, axes, split_axis=0, concat_axis=0, tiled=True)  50.9 us
    all_to_all x1, waiting for transfers between devices, shards(): lax.all_to_all(power, axes, split_axis=0, concat_axis=0, tiled=True)  29.3 us
    pallas_call x1, Pallas kernels, shards(): pl.pallas_call(functools.partial(sections_kernel, bins), grid=(HALF // 2,...  17.5 us
    all_to_all x1, starting transfers between devices, shards(): lax.all_to_all(spectrum, axes, split_axis=0, concat_axis=0, tiled=True)  12 us
    pallas_call x1, Pallas kernels, shards(): pl.pallas_call(functools.partial(spectrum_kernel, devices), grid=(HALF //...  7.85 us
    all_to_all x1, starting transfers between devices, shards(): lax.all_to_all(power, axes, split_axis=0, concat_axis=0, tiled=True)  7.61 us
    pallas_call x1, Pallas kernels, shards(): pl.pallas_call(functools.partial(cepstra_kernel, bins), grid=(HALF // 2,)...  4.01 us
  transfers between devices with their start and end apart: 2, of which 2 were waited for; matrix products, arithmetic and copies ran while one was open for 1% of the time, Pallas kernels for 0%

profile of v1, /device:TPU:1, one launch (start us, length us, event | category | flops | bytes accessed | tf_op | source)
XLA Modules:
  0.0 132.3 jit_solution(10295549924126542332)
XLA Ops:
  0.0 0.0 copy-start
  0.0 1.6 %copy-done = bf16[1024,1024]{1,0:T(8,128)(2,1)S(1)} copy-done((bf16[1024,1024]{1,0:T(8,128)(2,1)S(1)}, bf16[1024,1024]{1,0:T(8,128)(2,1)}, u32[]{:S(2)}) %copy-start) | copy-done | bytes 2097176
  1.6 7.8 %spectrum.1 = bf16[128,16,1024]{2,1,0:T(8,128)(2,1)} custom-call(bf16[1024,1024]{1,0:T(8,128)(2,1)S(1)} %copy-done, bf16[128,16384]{1,0:T(8,128)(2,1)} %high_ref.1, bf16[128,16384]{1,0:T(8,128)(2,1)} %high_ref.1), custom_call_target="tpu_custom_call" | custom-call | tf_op jit(solution)/shard_map/spectrum/pallas_call | solution.py:224
  9.4 0.0 copy-start.1
  9.4 0.0 copy-start.2
  9.4 0.0 copy-start.3
  9.5 0.0 copy-start.4
  9.5 12.0 %all-to-all-start = ((bf16[128,16,1024]{2,1,0:T(8,128)(2,1)}), bf16[128,16,1024]{2,1,0:T(8,128)(2,1)}, u32[]{:S(2)}, u32[]{:S(2)}) async-start(bf16[128,16,1024]{2,1,0:T(8,128)(2,1)} %spectrum.1), calls=%async_computation | async-start | bytes 8388608 | tf_op jit(solution)/shard_map/all_to_all | solution.py:238
  21.4 1.1 fusion.1
  22.6 0.1 copy.12
  22.7 50.9 %all-to-all-done.cells_ref = bf16[128,16,1024]{2,1,0:T(8,128)(2,1)} async-done(((bf16[128,16,1024]{2,1,0:T(8,128)(2,1)}), bf16[128,16,1024]{2,1,0:T(8,128)(2,1)}, u32[]{:S(2)}, u32[]{:S(2)}) %all-to-all-start) | async-done | bytes 4194336 | tf_op jit(solution)/shard_map/all_to_all | solution.py:238
  73.6 0.0 copy-done.1
  73.6 0.0 copy-done.2
  73.6 0.0 copy-done.3
  73.6 0.0 copy-done.4
  73.7 0.0 copy-start.6
  73.7 0.0 copy-start.5
  73.7 17.5 %sections.1 = bf16[128,16,512]{2,1,0:T(8,128)(2,1)} custom-call(bf16[128,16,1024]{2,1,0:T(8,128)(2,1)} %all-to-all-done.cells_ref, bf16[256,256]{1,0:T(8,128)(2,1)S(1)} %copy-done.1, bf16[256,256]{1,0:T(8,128)(2,1)S(1)} %copy-done.2, bf16[256,256]{1,0:T(8,128)(2,1)S(1)} %copy-done.1, bf16[256,256]{1,0:T(8,128)(2,1)S(1)} %copy-done.2, ...), custom_call_target="tpu_custom_call" | custom-call | tf_op jit(solution)/shard_map/sections/pallas_call | solution.py:244
  91.2 7.6 %all-to-all-start.1 = ((bf16[128,16,512]{2,1,0:T(8,128)(2,1)}), bf16[128,16,512]{2,1,0:T(8,128)(2,1)S(1)}, u32[]{:S(2)}, u32[]{:S(2)}) async-start(bf16[128,16,512]{2,1,0:T(8,128)(2,1)} %sections.1), calls=%async_computation.1 | async-start | bytes 4194304 | tf_op jit(solution)/shard_map/all_to_all | solution.py:276
  98.8 0.0 copy-done.6
  98.9 0.1 fusion.2
  98.9 0.1 maximum_convert_fusion.weights_ref
  99.1 29.3 %all-to-all-done.1.power_ref = bf16[128,16,512]{2,1,0:T(8,128)(2,1)S(1)} async-done(((bf16[128,16,512]{2,1,0:T(8,128)(2,1)}), bf16[128,16,512]{2,1,0:T(8,128)(2,1)S(1)}, u32[]{:S(2)}, u32[]{:S(2)}) %all-to-all-start.1) | async-done | bytes 2097184 | tf_op jit(solution)/shard_map/all_to_all | solution.py:276
  128.3 0.0 copy-done.5
  128.3 4.0 %cepstra.1 = f32[2,8,64,128]{3,2,1,0:T(8,128)} custom-call(bf16[128,16,512]{2,1,0:T(8,128)(2,1)S(1)} %all-to-all-done.1.power_ref, bf16[64,512]{1,0:T(8,128)(2,1)S(1)} %maximum_convert_fusion.weights_ref, f32[64,64]{1,0:T(8,128)S(1)} %copy-done.5), custom_call_target="tpu_custom_call" | custom-call | tf_op jit(solution)/shard_map/cepstra/pallas_call | solution.py:280
  (3 shorter events, 0.0 us)
Async XLA Ops:
  0.0 1.6 %copy-start = (bf16[1024,1024]{1,0:T(8,128)(2,1)S(1)}, bf16[1024,1024]{1,0:T(8,128)(2,1)}, u32[]{:S(2)}) copy-start(bf16[1024,1024]{1,0:T(8,128)(2,1)} %constant.26.clone.table_ref) | copy-start | bytes 6291460
  9.4 64.2 %copy-start.1 = (bf16[256,256]{1,0:T(8,128)(2,1)S(1)}, bf16[256,256]{1,0:T(8,128)(2,1)}, u32[]{:S(2)}) copy-start(bf16[256,256]{1,0:T(8,128)(2,1)} %constant.27.clone.first_ref.third_ref) | copy-start | bytes 393220
  9.4 64.2 %copy-start.2 = (bf16[256,256]{1,0:T(8,128)(2,1)S(1)}, bf16[256,256]{1,0:T(8,128)(2,1)}, u32[]{:S(2)}) copy-start(bf16[256,256]{1,0:T(8,128)(2,1)} %constant.28.clone.second_ref.fourth_ref) | copy-start | bytes 393220
  9.4 64.2 %copy-start.3 = (f32[2,128,128]{2,1,0:T(8,128)S(1)}, f32[2,128,128]{2,1,0:T(8,128)}, u32[]{:S(2)}) copy-start(f32[2,128,128]{2,1,0:T(8,128)} %constant.29.clone.forward_ref) | copy-start | bytes 393220
  9.5 64.2 %copy-start.4 = (f32[2,128,128]{2,1,0:T(8,128)S(1)}, f32[2,128,128]{2,1,0:T(8,128)}, u32[]{:S(2)}) copy-start(f32[2,128,128]{2,1,0:T(8,128)} %constant.30.clone.inverse_ref) | copy-start | bytes 393220
  9.5 64.2 %all-to-all-start = ((bf16[128,16,1024]{2,1,0:T(8,128)(2,1)}), bf16[128,16,1024]{2,1,0:T(8,128)(2,1)}, u32[]{:S(2)}, u32[]{:S(2)}) async-start(bf16[128,16,1024]{2,1,0:T(8,128)(2,1)} %spectrum.1), calls=%async_computation | async-start | bytes 8388608 | tf_op jit(solution)/shard_map/all_to_all | solution.py:238
  73.7 25.2 %copy-start.6 = (s32[66]{0:T(128)S(1)}, s32[66]{0:T(128)}, u32[]{:S(2)}) copy-start(s32[66]{0:T(128)} %param.13) | copy-start | bytes 796
  73.7 54.7 %copy-start.5 = (f32[64,64]{1,0:T(8,128)S(1)}, f32[64,64]{1,0:T(8,128)}, u32[]{:S(2)}) copy-start(f32[64,64]{1,0:T(8,128)} %constant.31.clone.cosine_ref) | copy-start | bytes 49156
  91.2 37.1 %all-to-all-start.1 = ((bf16[128,16,512]{2,1,0:T(8,128)(2,1)}), bf16[128,16,512]{2,1,0:T(8,128)(2,1)S(1)}, u32[]{:S(2)}, u32[]{:S(2)}) async-start(bf16[128,16,512]{2,1,0:T(8,128)(2,1)} %sections.1), calls=%async_computation.1 | async-start | bytes 4194304 | tf_op jit(solution)/shard_map/all_to_all | solution.py:276

commit v2 on v1

v2 whole, which is shorter than its diff:
```python
import functools
import math

import jax
import jax.numpy as jnp
import ml_dtypes
import numpy as np
from jax import lax
from jax.experimental import pallas as pl
from jax.experimental.pallas import tpu as pltpu
from jax.sharding import PartitionSpec as P

NCH = 16384
N1 = 128
N2 = 128
FLEN = 1024
NF = 512
NB = 64
FRAMES = 16
HALF = FRAMES // 2

energy_floor = 0.05


def time_table(devices):
    bins = NF // devices
    t = np.arange(FLEN)
    f = np.arange(NF)
    hann = 0.5 - 0.5 * np.cos(2.0 * math.pi * t / FLEN)
    phases = 2.0 * math.pi / FLEN * ((f[:, None] * t[None, :]) % FLEN)
    factor = (0.375 * FLEN) ** -0.5
    table = np.stack([np.cos(phases), -np.sin(phases)], axis=0) * (hann * factor)
    table = table.reshape(2, devices, bins, FLEN).transpose(1, 0, 2, 3)
    return table.reshape(2 * NF, FLEN).astype(ml_dtypes.bfloat16)


def dft_parts(length, sign):
    n = np.arange(length)
    phases = 2.0 * math.pi / length * ((n[:, None] * n[None, :]) % length)
    factor = length**-0.5
    return np.cos(phases) * factor, sign * np.sin(phases) * factor


def left_table(length, sign):
    re, im = dft_parts(length, sign)
    return np.block([[re, -im], [im, re]]).astype(ml_dtypes.bfloat16)


def right_table(length, sign):
    re, im = dft_parts(length, sign)
    return np.block([[re, im], [-im, re]]).astype(ml_dtypes.bfloat16)


def twiddle(sign):
    q = np.arange(N2)
    a = np.arange(N1)
    phases = 2.0 * math.pi / NCH * ((q[:, None] * a[None, :]) % NCH)
    return np.stack([np.cos(phases), sign * np.sin(phases)]).astype(np.float32)


def cosine_table():
    j = np.arange(NB)
    phases = math.pi / (2 * NB) * ((j[:, None] * (2 * j[None, :] + 1)) % (4 * NB))
    weight = np.where(j == 0, (1.0 / NB) ** 0.5, (2.0 / NB) ** 0.5)
    return (np.cos(phases) * weight[:, None]).astype(np.float32)


def band_weights(band_edges):
    bounds = band_edges.astype(jnp.float32)
    freq = jnp.arange(NF, dtype=jnp.int32).astype(jnp.float32)[None, :]
    low, middle, high = bounds[:-2, None], bounds[1:-1, None], bounds[2:, None]
    rising = (freq - low) / (middle - low)
    falling = (high - freq) / (high - middle)
    return jnp.maximum(jnp.minimum(rising, falling), 0.0).astype(jnp.bfloat16)


def row_order(bins):
    rows = 4 * bins
    group = 256 // rows
    order = np.zeros((256, 256))
    for r in range(rows):
        for b in range(group):
            order[r * group + b, b * rows + r] = 1.0
    return order.astype(ml_dtypes.bfloat16)


def spectrum_kernel(
    devices, chunks, parts, table_hbm, traces_hbm, out_hbm, table, traces, out, table_sem, traces_sem, out_sem
):
    rows = 2 * NF // devices
    height = 2 * NF // parts
    owners = devices // parts
    width = 2 * FLEN

    def table_copy(j):
        at = pl.ds(j * height, height)
        return pltpu.make_async_copy(table_hbm.at[at], table.at[at], table_sem.at[j])

    def traces_copy(i, half):
        at = pl.ds((half * chunks + i) * width, width)
        return pltpu.make_async_copy(
            traces_hbm.at[:, at], traces.at[i, half], traces_sem.at[i, half]
        )

    def out_copy(i, j):
        at = (pl.ds(j * owners, owners), slice(None), pl.ds(i * 2 * N1, 2 * N1))
        return pltpu.make_async_copy(out.at[at], out_hbm.at[at], out_sem.at[i, j])

    traces_copy(0, 0).start()
    table_copy(0).start()
    traces_copy(0, 1).start()
    for j in range(1, parts):
        table_copy(j).start()
    for i in range(1, chunks):
        for half in range(2):
            traces_copy(i, half).start()
    for i in range(chunks):
        for half in range(2):
            traces_copy(i, half).wait()
        low, high = traces[i, 0], traces[i, 1]
        samples = jnp.concatenate(
            [low[:, :FLEN], low[:, FLEN:], high[:, :FLEN], high[:, FLEN:]], axis=0
        )
        for j in range(parts):
            if i == 0:
                table_copy(j).wait()
            part = lax.dot_general(
                table[j * height : (j + 1) * height, :],
                samples,
                (((1,), (1,)), ((), ())),
                preferred_element_type=jnp.float32,
            )
            part = part.reshape(owners, rows, 4 * N1)
            both = jnp.concatenate([part[:, :, : 2 * N1], part[:, :, 2 * N1 :]], axis=1)
            out[j * owners : (j + 1) * owners, :, i * 2 * N1 : (i + 1) * 2 * N1] = both.astype(
                jnp.bfloat16
            )
            out_copy(i, j).start()
    for i in range(chunks):
        for j in range(parts):
            out_copy(i, j).wait()


def sections_kernel(
    bins,
    cells_ref,
    order_ref,
    first_ref,
    second_ref,
    third_ref,
    fourth_ref,
    forward_ref,
    inverse_ref,
    mask_ref,
    power_ref,
    cells,
    turned,
    kept,
    back,
    power_f32,
):
    rows = 4 * bins
    group = 256 // rows
    count = 4 * bins
    step = 2
    bf16 = jnp.bfloat16
    dot = functools.partial(jnp.dot, preferred_element_type=jnp.float32)
    for g in range(N2 // group):
        ordered = cells_ref[g * group : (g + 1) * group].reshape(256, 2 * N1)
        ordered = dot(order_ref[...], ordered).astype(bf16)
        for r in range(rows):
            half, x, f = r // (2 * bins), r // bins % 2, r % bins
            for m in range(2):
                n = (m * 2 + half) * bins + f
                cells[
                    x * N2 + g * group : x * N2 + (g + 1) * group, n * N1 : (n + 1) * N1
                ] = ordered[r * group : (r + 1) * group, m * N1 : (m + 1) * N1]
    fwd_cos, fwd_sin = forward_ref[0], forward_ref[1]
    for n0 in range(0, count, step):
        summed = dot(first_ref[...], cells[:, n0 * N1 : (n0 + step) * N1])
        for i in range(step):
            n = n0 + i
            re = summed[:N2, i * N1 : (i + 1) * N1]
            im = summed[N2:, i * N1 : (i + 1) * N1]
            turned[n * N2 : (n + 1) * N2, :N1] = (re * fwd_cos - im * fwd_sin).astype(bf16)
            turned[n * N2 : (n + 1) * N2, N1:] = (re * fwd_sin + im * fwd_cos).astype(bf16)
    for n0 in range(0, count, step):
        section = dot(turned[n0 * N2 : (n0 + step) * N2, :], second_ref[...]).astype(bf16)
        for i in range(step):
            n = n0 + i
            mask = mask_ref[n % bins]
            for x in range(2):
                kept[n * N2 : (n + 1) * N2, x * N1 : (x + 1) * N1] = (
                    section[i * N2 : (i + 1) * N2, x * N1 : (x + 1) * N1] * mask
                )
    inv_cos, inv_sin = inverse_ref[0], inverse_ref[1]
    for n0 in range(0, count, step):
        summed = dot(kept[n0 * N2 : (n0 + step) * N2, :], third_ref[...])
        for i in range(step):
            n = n0 + i
            re = summed[i * N2 : (i + 1) * N2, :N1]
            im = summed[i * N2 : (i + 1) * N2, N1:]
            back[:N2, n * N1 : (n + 1) * N1] = (re * inv_cos - im * inv_sin).astype(bf16)
            back[N2:, n * N1 : (n + 1) * N1] = (re * inv_sin + im * inv_cos).astype(bf16)
    for n0 in range(0, count, step):
        filtered = dot(fourth_ref[...], back[:, n0 * N1 : (n0 + step) * N1])
        filtered = filtered.astype(bf16).astype(jnp.float32)
        power = filtered[:N2] * filtered[:N2] + filtered[N2:] * filtered[N2:]
        for i in range(step):
            power_f32[pl.ds(n0 + i, N2, stride=rows), :] = power[:, i * N1 : (i + 1) * N1]
    power_ref[...] = power_f32[...].reshape(N2, rows, N1).astype(bf16)


def cepstra_kernel(power_ref, weights_ref, cosine_ref, out_ref):
    sources, rows, lanes = power_ref.shape
    power = power_ref[...].reshape(sources * rows, lanes)
    energy = jnp.dot(weights_ref[...], power, preferred_element_type=jnp.float32)
    logs = jnp.log(jnp.maximum(energy, energy_floor))
    for k in range(4):
        cepstra = jnp.dot(
            cosine_ref[...],
            logs[k * NB : (k + 1) * NB],
            precision=lax.Precision.HIGHEST,
            preferred_element_type=jnp.float32,
        )
        m, half = k // 2, k % 2
        for i in range(lanes // N1):
            out_ref[half, 2 * i + m] = cepstra[:, i * N1 : (i + 1) * N1]


def whole(shape):
    return pl.BlockSpec(shape, lambda i: (0,) * len(shape))


VMEM_LIMIT = 48 * 1024 * 1024


def shards(traces, fan_mask, band_edges):
    axes = ("chan", "sub")
    devices = lax.axis_size("chan") * lax.axis_size("sub")
    sub_count = lax.axis_size("sub")
    bins = NF // devices
    rows = 4 * bins
    bf16 = jnp.bfloat16
    params = pltpu.CompilerParams(vmem_limit_bytes=VMEM_LIMIT)

    chunks, parts = HALF // 2, 4
    spectrum = pl.pallas_call(
        functools.partial(spectrum_kernel, devices, chunks, parts),
        in_specs=[pl.BlockSpec(memory_space=pl.ANY)] * 2,
        out_specs=pl.BlockSpec(memory_space=pl.ANY),
        out_shape=jax.ShapeDtypeStruct((devices, rows, HALF * N1), bf16),
        scratch_shapes=[
            pltpu.VMEM((2 * NF, FLEN), bf16),
            pltpu.VMEM((chunks, 2, N1, 2 * FLEN), bf16),
            pltpu.VMEM((devices, rows, HALF * N1), bf16),
            pltpu.SemaphoreType.DMA((parts,)),
            pltpu.SemaphoreType.DMA((chunks, 2)),
            pltpu.SemaphoreType.DMA((chunks, parts)),
        ],
        compiler_params=params,
        name="spectrum",
    )(jnp.asarray(time_table(devices)), traces)

    cells = lax.all_to_all(spectrum, axes, split_axis=0, concat_axis=0, tiled=True)

    mask = lax.dynamic_slice_in_dim(fan_mask, lax.axis_index("sub") * bins, bins, 0)
    mask = jnp.transpose(mask.reshape(bins, N1, N2), (0, 2, 1))
    mask = (mask > 0).astype(bf16)

    power = pl.pallas_call(
        functools.partial(sections_kernel, bins),
        grid=(HALF // 2,),
        in_specs=[
            pl.BlockSpec((N2, rows, 2 * N1), lambda i: (0, 0, i)),
            whole((256, 256)),
            whole((2 * N2, 2 * N2)),
            whole((2 * N1, 2 * N1)),
            whole((2 * N1, 2 * N1)),
            whole((2 * N2, 2 * N2)),
            whole((2, N2, N1)),
            whole((2, N2, N1)),
            whole((bins, N2, N1)),
        ],
        out_specs=pl.BlockSpec((N2, rows, N1), lambda i: (0, 0, i)),
        out_shape=jax.ShapeDtypeStruct((N2, rows, HALF // 2 * N1), bf16),
        scratch_shapes=[
            pltpu.VMEM((2 * N2, rows * N1), bf16),
            pltpu.VMEM((rows * N2, 2 * N1), bf16),
            pltpu.VMEM((rows * N2, 2 * N1), bf16),
            pltpu.VMEM((2 * N2, rows * N1), bf16),
            pltpu.VMEM((N2 * rows, N1), jnp.float32),
        ],
        compiler_params=params,
        name="sections",
    )(
        cells,
        jnp.asarray(row_order(bins)),
        jnp.asarray(left_table(N2, -1.0)),
        jnp.asarray(right_table(N1, -1.0)),
        jnp.asarray(right_table(N1, 1.0)),
        jnp.asarray(left_table(N2, 1.0)),
        jnp.asarray(twiddle(-1.0)),
        jnp.asarray(twiddle(1.0)),
        mask,
    )

    returned = lax.all_to_all(power, axes, split_axis=0, concat_axis=0, tiled=True)

    weights = band_weights(band_edges).reshape(1, NB, devices, 1, bins)
    same = jnp.eye(4, dtype=bool)[:, None, None, :, None]
    weights = jnp.where(same, weights, jnp.zeros((), bf16)).reshape(4 * NB, devices * rows)
    cepstra = pl.pallas_call(
        cepstra_kernel,
        in_specs=[pl.BlockSpec(memory_space=pltpu.VMEM)] * 3,
        out_specs=pl.BlockSpec(memory_space=pltpu.VMEM),
        out_shape=jax.ShapeDtypeStruct((2, HALF, NB, N1), jnp.float32),
        compiler_params=params,
        name="cepstra",
    )(returned, weights, jnp.asarray(cosine_table()))
    return cepstra.reshape(FRAMES, NB, N1)


def solution(mesh):
    in_specs = (P(("chan", "sub"), None), P("chan", None), P())
    out_specs = P(None, None, ("chan", "sub"))
    return jax.shard_map(shards, mesh=mesh, in_specs=in_specs, out_specs=out_specs, check_vma=False)
```

time: 133 us -> 124 us (0.932)
  Pallas kernels: 29.4 us -> 20.6 us
  waiting for transfers between devices: 80.2 us -> 72 us
  local copies, waits for them, and re-layouts: 1.77 us -> 7.77 us
  other arithmetic: 1.34 us -> 3.52 us
    all_to_all x1, waiting for transfers between devices: 29.3 us -> 21.1 us  [shards(): lax.all_to_all(power, axes, split_axis=0, concat_axis=0, tiled=True)]
    pallas_call x1, Pallas kernels: 17.5 us -> 10.5 us  [shards(): pl.pallas_call(functools.partial(sections_kernel, bins), grid=(HALF // 2,...]
    select_n x0 -> x2, local copies, waits for them, and re-layouts: none -> 5.85 us  [shards(): jnp.where(same, weights, jnp.zeros((), bf16))]
    select_n x0 -> x1, other arithmetic: none -> 2.17 us  [shards(): jnp.where(same, weights, jnp.zeros((), bf16))]
    pallas_call x2, Pallas kernels: 11.9 us -> 10.1 us  [the longest x1 8.03 us: shards(): pl.pallas_call(functools.partial(spectrum_kernel, devices, chunks, parts)...]
  transfers between devices with their start and end apart: 2 -> 2, of which waited for: 2 -> 2; matrix products, arithmetic and copies ran while one was open for 1% -> 8% of each run, Pallas kernels for 0% -> 0%
where the time goes in v2:
time: 124 us
  waiting for transfers between devices  72 us (58%)
  Pallas kernels  20.6 us (17%)
  starting transfers between devices  19.6 us (16%)
  local copies, waits for them, and re-layouts  7.77 us (6%)
  other arithmetic  3.52 us (3%)
    all_to_all x1, waiting for transfers between devices, shards(): lax.all_to_all(spectrum, axes, split_axis=0, concat_axis=0, tiled=True)  50.9 us
    all_to_all x1, waiting for transfers between devices, shards(): lax.all_to_all(power, axes, split_axis=0, concat_axis=0, tiled=True)  21.1 us
    all_to_all x1, starting transfers between devices, shards(): lax.all_to_all(spectrum, axes, split_axis=0, concat_axis=0, tiled=True)  12 us
    pallas_call x1, Pallas kernels, shards(): pl.pallas_call(functools.partial(sections_kernel, bins), grid=(HALF // 2,...  10.5 us
    pallas_call x1, Pallas kernels, shards(): pl.pallas_call(functools.partial(spectrum_kernel, devices, chunks, parts)...  8.03 us
    all_to_all x1, starting transfers between devices, shards(): lax.all_to_all(power, axes, split_axis=0, concat_axis=0, tiled=True)  7.61 us
    select_n x2, local copies, waits for them, and re-layouts, shards(): jnp.where(same, weights, jnp.zeros((), bf16))  5.85 us
  transfers between devices with their start and end apart: 2, of which 2 were waited for; matrix products, arithmetic and copies ran while one was open for 8% of the time, Pallas kernels for 0%

profile of v2, /device:TPU:1, one launch (start us, length us, event | category | flops | bytes accessed | tf_op | source)
XLA Modules:
  0.0 123.7 jit_solution(18170507550874946724)
XLA Ops:
  0.0 0.0 copy-start
  0.0 1.6 %copy-done = bf16[1024,1024]{1,0:T(8,128)(2,1)S(1)} copy-done((bf16[1024,1024]{1,0:T(8,128)(2,1)S(1)}, bf16[1024,1024]{1,0:T(8,128)(2,1)}, u32[]{:S(2)}) %copy-start) | copy-done | bytes 2097176
  1.6 8.0 %spectrum.1 = bf16[128,16,1024]{2,1,0:T(8,128)(2,1)} custom-call(bf16[1024,1024]{1,0:T(8,128)(2,1)S(1)} %copy-done, bf16[128,16384]{1,0:T(8,128)(2,1)} %traces_hbm.1), custom_call_target="tpu_custom_call" | custom-call | tf_op jit(solution)/shard_map/spectrum/pallas_call | solution.py:248
  9.6 0.0 copy-start.1
  9.6 0.0 copy-start.2
  9.7 0.0 copy-start.3
  9.7 0.0 copy-start.4
  9.7 0.0 copy-start.5
  9.7 12.0 %all-to-all-start = ((bf16[128,16,1024]{2,1,0:T(8,128)(2,1)}), bf16[128,16,1024]{2,1,0:T(8,128)(2,1)}, u32[]{:S(2)}, u32[]{:S(2)}) async-start(bf16[128,16,1024]{2,1,0:T(8,128)(2,1)} %spectrum.1), calls=%async_computation | async-start | bytes 8388608 | tf_op jit(solution)/shard_map/all_to_all | solution.py:265
  21.7 1.1 fusion.1
  22.9 0.1 copy.15
  23.0 50.9 %all-to-all-done.cells_ref = bf16[128,16,1024]{2,1,0:T(8,128)(2,1)} async-done(((bf16[128,16,1024]{2,1,0:T(8,128)(2,1)}), bf16[128,16,1024]{2,1,0:T(8,128)(2,1)}, u32[]{:S(2)}, u32[]{:S(2)}) %all-to-all-start) | async-done | bytes 4194336 | tf_op jit(solution)/shard_map/all_to_all | solution.py:265
  73.9 0.0 copy-done.1
  73.9 0.0 copy-done.2
  73.9 0.0 copy-done.3
  73.9 0.0 copy-done.4
  74.0 0.0 copy-done.5
  74.0 10.5 %sections.1 = bf16[128,16,512]{2,1,0:T(8,128)(2,1)} custom-call(bf16[128,16,1024]{2,1,0:T(8,128)(2,1)} %all-to-all-done.cells_ref, bf16[256,256]{1,0:T(8,128)(2,1)S(1)} %copy-done.3, bf16[256,256]{1,0:T(8,128)(2,1)S(1)} %copy-done.1, bf16[256,256]{1,0:T(8,128)(2,1)S(1)} %copy-done.2, bf16[256,256]{1,0:T(8,128)(2,1)S(1)} %copy-done.1, ...), custom_call_target="tpu_custom_call" | custom-call | tf_op jit(solution)/shard_map/sections/pallas_call | solution.py:271
  84.5 0.0 copy-start.7
  84.5 7.6 %all-to-all-start.1 = ((bf16[128,16,512]{2,1,0:T(8,128)(2,1)}), bf16[128,16,512]{2,1,0:T(8,128)(2,1)S(1)}, u32[]{:S(2)}, u32[]{:S(2)}) async-start(bf16[128,16,512]{2,1,0:T(8,128)(2,1)} %sections.1), calls=%async_computation.1 | async-start | bytes 4194304 | tf_op jit(solution)/shard_map/all_to_all | solution.py:308
  92.1 0.0 copy-done.7
  92.1 0.1 fusion.2
  92.2 0.1 maximum_convert_fusion
  92.3 0.1 copy.16
  92.5 2.2 %broadcast_select_fusion = bf16[4,64,128,4,4]{1,0,4,3,2:T(4,128)(2,1)} fusion(pred[4,4]{0,1:T(4,128)(4,1)S(1)} %iota_compare_fusion, bf16[64,128,4]{0,2,1:T(4,128)(2,1)S(1)} %copy.16), kind=kLoop, calls=%fused_computation | loop fusion | flops 524288 | bytes 1114128 | tf_op jit(solution)/shard_map/jit(_where)/select_n | solution.py:312
  94.7 0.0 copy-start.6
  94.7 4.4 %select_n.13 = bf16[256,2048]{0,1:T(8,128)(2,1)} reshape(bf16[4,64,128,4,4]{1,0,4,3,2:T(4,128)(2,1)} %broadcast_select_fusion) | data formatting | bytes 2097152 | tf_op jit(solution)/shard_map/jit(_where)/select_n | solution.py:312
  99.0 1.5 %copy.17.weights_ref = bf16[256,2048]{1,0:T(8,128)(2,1)S(1)} copy(bf16[256,2048]{0,1:T(8,128)(2,1)} %select_n.13) | data formatting | bytes 2097152 | tf_op jit(solution)/shard_map/jit(_where)/select_n | solution.py:312
  100.5 21.1 %all-to-all-done.1.power_ref = bf16[128,16,512]{2,1,0:T(8,128)(2,1)S(1)} async-done(((bf16[128,16,512]{2,1,0:T(8,128)(2,1)}), bf16[128,16,512]{2,1,0:T(8,128)(2,1)S(1)}, u32[]{:S(2)}, u32[]{:S(2)}) %all-to-all-start.1) | async-done | bytes 2097184 | tf_op jit(solution)/shard_map/all_to_all | solution.py:308
  121.6 0.0 copy-done.6
  121.6 2.1 %cepstra.1 = f32[2,8,64,128]{3,2,1,0:T(8,128)} custom-call(bf16[128,16,512]{2,1,0:T(8,128)(2,1)S(1)} %all-to-all-done.1.power_ref, bf16[256,2048]{1,0:T(8,128)(2,1)S(1)} %copy.17.weights_ref, f32[64,64]{1,0:T(8,128)S(1)} %copy-done.6), custom_call_target="tpu_custom_call" | custom-call | tf_op jit(solution)/shard_map/cepstra/pallas_call | solution.py:313
  (4 shorter events, 0.0 us)
Async XLA Ops:
  0.0 1.6 %copy-start = (bf16[1024,1024]{1,0:T(8,128)(2,1)S(1)}, bf16[1024,1024]{1,0:T(8,128)(2,1)}, u32[]{:S(2)}) copy-start(bf16[1024,1024]{1,0:T(8,128)(2,1)} %constant.30.clone.table_hbm) | copy-start | bytes 6291460
  9.6 64.3 %copy-start.1 = (bf16[256,256]{1,0:T(8,128)(2,1)S(1)}, bf16[256,256]{1,0:T(8,128)(2,1)}, u32[]{:S(2)}) copy-start(bf16[256,256]{1,0:T(8,128)(2,1)} %constant.32.clone.first_ref.third_ref) | copy-start | bytes 393220
  9.6 64.3 %copy-start.2 = (bf16[256,256]{1,0:T(8,128)(2,1)S(1)}, bf16[256,256]{1,0:T(8,128)(2,1)}, u32[]{:S(2)}) copy-start(bf16[256,256]{1,0:T(8,128)(2,1)} %constant.33.clone.second_ref.fourth_ref) | copy-start | bytes 393220
  9.7 64.3 %copy-start.3 = (bf16[256,256]{1,0:T(8,128)(2,1)S(1)}, bf16[256,256]{1,0:T(8,128)(2,1)}, u32[]{:S(2)}) copy-start(bf16[256,256]{1,0:T(8,128)(2,1)} %constant.31.clone.order_ref) | copy-start | bytes 393220
  9.7 64.3 %copy-start.4 = (f32[2,128,128]{2,1,0:T(8,128)S(1)}, f32[2,128,128]{2,1,0:T(8,128)}, u32[]{:S(2)}) copy-start(f32[2,128,128]{2,1,0:T(8,128)} %constant.34.clone.forward_ref) | copy-start | bytes 393220
  9.7 64.3 %copy-start.5 = (f32[2,128,128]{2,1,0:T(8,128)S(1)}, f32[2,128,128]{2,1,0:T(8,128)}, u32[]{:S(2)}) copy-start(f32[2,128,128]{2,1,0:T(8,128)} %constant.35.clone.inverse_ref) | copy-start | bytes 393220
  9.7 64.2 %all-to-all-start = ((bf16[128,16,1024]{2,1,0:T(8,128)(2,1)}), bf16[128,16,1024]{2,1,0:T(8,128)(2,1)}, u32[]{:S(2)}, u32[]{:S(2)}) async-start(bf16[128,16,1024]{2,1,0:T(8,128)(2,1)} %spectrum.1), calls=%async_computation | async-start | bytes 8388608 | tf_op jit(solution)/shard_map/all_to_all | solution.py:265
  84.5 7.6 %copy-start.7 = (s32[66]{0:T(128)S(1)}, s32[66]{0:T(128)}, u32[]{:S(2)}) copy-start(s32[66]{0:T(128)} %param.14) | copy-start | bytes 796
  84.5 37.1 %all-to-all-start.1 = ((bf16[128,16,512]{2,1,0:T(8,128)(2,1)}), bf16[128,16,512]{2,1,0:T(8,128)(2,1)S(1)}, u32[]{:S(2)}, u32[]{:S(2)}) async-start(bf16[128,16,512]{2,1,0:T(8,128)(2,1)} %sections.1), calls=%async_computation.1 | async-start | bytes 4194304 | tf_op jit(solution)/shard_map/all_to_all | solution.py:308
  94.7 26.9 %copy-start.6 = (f32[64,64]{1,0:T(8,128)S(1)}, f32[64,64]{1,0:T(8,128)}, u32[]{:S(2)}) copy-start(f32[64,64]{1,0:T(8,128)} %constant.36.clone.cosine_ref) | copy-start | bytes 49156

commit v3 on v2

--- a/solution.py
+++ b/solution.py
@@ -74,23 +74,26 @@
     return jnp.maximum(jnp.minimum(rising, falling), 0.0).astype(jnp.bfloat16)
 
 
-def row_order(bins):
-    rows = 4 * bins
-    group = 256 // rows
-    order = np.zeros((256, 256))
-    for r in range(rows):
-        for b in range(group):
-            order[r * group + b, b * rows + r] = 1.0
-    return order.astype(ml_dtypes.bfloat16)
-
-
 def spectrum_kernel(
-    devices, chunks, parts, table_hbm, traces_hbm, out_hbm, table, traces, out, table_sem, traces_sem, out_sem
+    devices,
+    chunks,
+    parts,
+    table_hbm,
+    traces_hbm,
+    out_hbm,
+    table,
+    traces,
+    out,
+    table_sem,
+    traces_sem,
+    out_sem,
 ):
     rows = 2 * NF // devices
     height = 2 * NF // parts
     owners = devices // parts
-    width = 2 * FLEN
+    frames = HALF // chunks
+    width = frames * FLEN
+    lanes = frames * N1
 
     def table_copy(j):
         at = pl.ds(j * height, height)
@@ -103,7 +106,7 @@
         )
 
     def out_copy(i, j):
-        at = (pl.ds(j * owners, owners), slice(None), pl.ds(i * 2 * N1, 2 * N1))
+        at = (pl.ds(j * owners, owners), slice(None), pl.ds(i * lanes, lanes))
         return pltpu.make_async_copy(out.at[at], out_hbm.at[at], out_sem.at[i, j])
 
     traces_copy(0, 0).start()
@@ -117,9 +120,13 @@
     for i in range(chunks):
         for half in range(2):
             traces_copy(i, half).wait()
-        low, high = traces[i, 0], traces[i, 1]
         samples = jnp.concatenate(
-            [low[:, :FLEN], low[:, FLEN:], high[:, :FLEN], high[:, FLEN:]], axis=0
+            [
+                traces[i, half, :, m * FLEN : (m + 1) * FLEN]
+                for half in range(2)
+                for m in range(frames)
+            ],
+            axis=0,
         )
         for j in range(parts):
             if i == 0:
@@ -130,9 +137,9 @@
                 (((1,), (1,)), ((), ())),
                 preferred_element_type=jnp.float32,
             )
-            part = part.reshape(owners, rows, 4 * N1)
-            both = jnp.concatenate([part[:, :, : 2 * N1], part[:, :, 2 * N1 :]], axis=1)
-            out[j * owners : (j + 1) * owners, :, i * 2 * N1 : (i + 1) * 2 * N1] = both.astype(
+            part = part.reshape(owners, rows, 2 * lanes)
+            both = jnp.concatenate([part[:, :, :lanes], part[:, :, lanes:]], axis=1)
+            out[j * owners : (j + 1) * owners, :, i * lanes : (i + 1) * lanes] = both.astype(
                 jnp.bfloat16
             )
             out_copy(i, j).start()
@@ -144,7 +151,6 @@
 def sections_kernel(
     bins,
     cells_ref,
-    order_ref,
     first_ref,
     second_ref,
     third_ref,
@@ -157,24 +163,24 @@
     turned,
     kept,
     back,
-    power_f32,
+    power_rows,
 ):
     rows = 4 * bins
-    group = 256 // rows
+    group = 16
     count = 4 * bins
     step = 2
     bf16 = jnp.bfloat16
     dot = functools.partial(jnp.dot, preferred_element_type=jnp.float32)
     for g in range(N2 // group):
-        ordered = cells_ref[g * group : (g + 1) * group].reshape(256, 2 * N1)
-        ordered = dot(order_ref[...], ordered).astype(bf16)
-        for r in range(rows):
-            half, x, f = r // (2 * bins), r // bins % 2, r % bins
-            for m in range(2):
+        for m in range(2):
+            block = cells_ref[g * group : (g + 1) * group, :, m * N1 : (m + 1) * N1]
+            block = jnp.swapaxes(block, 0, 1)
+            for r in range(rows):
+                half, x, f = r // (2 * bins), r // bins % 2, r % bins
                 n = (m * 2 + half) * bins + f
                 cells[
                     x * N2 + g * group : x * N2 + (g + 1) * group, n * N1 : (n + 1) * N1
-                ] = ordered[r * group : (r + 1) * group, m * N1 : (m + 1) * N1]
+                ] = block[r]
     fwd_cos, fwd_sin = forward_ref[0], forward_ref[1]
     for n0 in range(0, count, step):
         summed = dot(first_ref[...], cells[:, n0 * N1 : (n0 + step) * N1])
@@ -207,8 +213,8 @@
         filtered = filtered.astype(bf16).astype(jnp.float32)
         power = filtered[:N2] * filtered[:N2] + filtered[N2:] * filtered[N2:]
         for i in range(step):
-            power_f32[pl.ds(n0 + i, N2, stride=rows), :] = power[:, i * N1 : (i + 1) * N1]
-    power_ref[...] = power_f32[...].reshape(N2, rows, N1).astype(bf16)
+            power_rows[n0 + i] = power[:, i * N1 : (i + 1) * N1].astype(bf16)
+    power_ref[...] = jnp.swapaxes(power_rows[...], 0, 1)
 
 
 def cepstra_kernel(power_ref, weights_ref, cosine_ref, out_ref):
@@ -244,15 +250,15 @@
     bf16 = jnp.bfloat16
     params = pltpu.CompilerParams(vmem_limit_bytes=VMEM_LIMIT)
 
-    chunks, parts = HALF // 2, 4
+    chunks, parts = 2, 2
     spectrum = pl.pallas_call(
         functools.partial(spectrum_kernel, devices, chunks, parts),
-        in_specs=[pl.BlockSpec(memory_space=pl.ANY)] * 2,
-        out_specs=pl.BlockSpec(memory_space=pl.ANY),
+        in_specs=[pl.BlockSpec(memory_space=pltpu.HBM)] * 2,
+        out_specs=pl.BlockSpec(memory_space=pltpu.HBM),
         out_shape=jax.ShapeDtypeStruct((devices, rows, HALF * N1), bf16),
         scratch_shapes=[
             pltpu.VMEM((2 * NF, FLEN), bf16),
-            pltpu.VMEM((chunks, 2, N1, 2 * FLEN), bf16),
+            pltpu.VMEM((chunks, 2, N1, HALF // chunks * FLEN), bf16),
             pltpu.VMEM((devices, rows, HALF * N1), bf16),
             pltpu.SemaphoreType.DMA((parts,)),
             pltpu.SemaphoreType.DMA((chunks, 2)),
@@ -273,7 +279,6 @@
         grid=(HALF // 2,),
         in_specs=[
             pl.BlockSpec((N2, rows, 2 * N1), lambda i: (0, 0, i)),
-            whole((256, 256)),
             whole((2 * N2, 2 * N2)),
             whole((2 * N1, 2 * N1)),
             whole((2 * N1, 2 * N1)),
@@ -289,13 +294,12 @@
             pltpu.VMEM((rows * N2, 2 * N1), bf16),
             pltpu.VMEM((rows * N2, 2 * N1), bf16),
             pltpu.VMEM((2 * N2, rows * N1), bf16),
-            pltpu.VMEM((N2 * rows, N1), jnp.float32),
+            pltpu.VMEM((rows, N2, N1), bf16),
         ],
         compiler_params=params,
         name="sections",
     )(
         cells,
-        jnp.asarray(row_order(bins)),
         jnp.asarray(left_table(N2, -1.0)),
         jnp.asarray(right_table(N1, -1.0)),
         jnp.asarray(right_table(N1, 1.0)),

time: 124 us -> 123 us (level)
  Pallas kernels: 20.6 us -> 19.2 us
where the time goes in v3:
time: 123 us; the launch traced here: 122 us
  waiting for transfers between devices  72 us (59%)
  starting transfers between devices  19.6 us (16%)
  Pallas kernels  19.2 us (16%)
  local copies, waits for them, and re-layouts  7.75 us (6%)
  other arithmetic  3.52 us (3%)
    all_to_all x1, waiting for transfers between devices, shards(): lax.all_to_all(spectrum, axes, split_axis=0, concat_axis=0, tiled=True)  50.9 us
    all_to_all x1, waiting for transfers between devices, shards(): lax.all_to_all(power, axes, split_axis=0, concat_axis=0, tiled=True)  21.1 us
    all_to_all x1, starting transfers between devices, shards(): lax.all_to_all(spectrum, axes, split_axis=0, concat_axis=0, tiled=True)  12 us
    pallas_call x1, Pallas kernels, shards(): pl.pallas_call(functools.partial(sections_kernel, bins), grid=(HALF // 2,...  9.39 us
    pallas_call x1, Pallas kernels, shards(): pl.pallas_call(functools.partial(spectrum_kernel, devices, chunks, parts)...  7.77 us
    all_to_all x1, starting transfers between devices, shards(): lax.all_to_all(power, axes, split_axis=0, concat_axis=0, tiled=True)  7.61 us
    select_n x2, local copies, waits for them, and re-layouts, shards(): jnp.where(same, weights, jnp.zeros((), bf16))  5.84 us
  transfers between devices with their start and end apart: 2, of which 2 were waited for; matrix products, arithmetic and copies ran while one was open for 8% of the time, Pallas kernels for 0%

profile of v3, /device:TPU:1, one launch (start us, length us, event | category | flops | bytes accessed | tf_op | source)
XLA Modules:
  0.0 122.2 jit_solution(406830235466346520)
XLA Ops:
  0.0 0.0 copy-start
  0.0 1.6 %copy-done = bf16[1024,1024]{1,0:T(8,128)(2,1)S(1)} copy-done((bf16[1024,1024]{1,0:T(8,128)(2,1)S(1)}, bf16[1024,1024]{1,0:T(8,128)(2,1)}, u32[]{:S(2)}) %copy-start) | copy-done | bytes 2097176
  1.6 7.8 %spectrum.1 = bf16[128,16,1024]{2,1,0:T(8,128)(2,1)} custom-call(bf16[1024,1024]{1,0:T(8,128)(2,1)S(1)} %copy-done, bf16[128,16384]{1,0:T(8,128)(2,1)} %traces_hbm.1), custom_call_target="tpu_custom_call" | custom-call | tf_op jit(solution)/shard_map/spectrum/pallas_call | solution.py:254
  9.4 0.0 copy-start.1
  9.4 0.0 copy-start.2
  9.4 0.0 copy-start.3
  9.4 0.0 copy-start.4
  9.4 12.0 %all-to-all-start = ((bf16[128,16,1024]{2,1,0:T(8,128)(2,1)}), bf16[128,16,1024]{2,1,0:T(8,128)(2,1)}, u32[]{:S(2)}, u32[]{:S(2)}) async-start(bf16[128,16,1024]{2,1,0:T(8,128)(2,1)} %spectrum.1), calls=%async_computation | async-start | bytes 8388608 | tf_op jit(solution)/shard_map/all_to_all | solution.py:271
  21.4 1.1 fusion.1
  22.6 0.1 copy.14
  22.7 50.9 %all-to-all-done.cells_ref = bf16[128,16,1024]{2,1,0:T(8,128)(2,1)} async-done(((bf16[128,16,1024]{2,1,0:T(8,128)(2,1)}), bf16[128,16,1024]{2,1,0:T(8,128)(2,1)}, u32[]{:S(2)}, u32[]{:S(2)}) %all-to-all-start) | async-done | bytes 4194336 | tf_op jit(solution)/shard_map/all_to_all | solution.py:271
  73.6 0.0 copy-done.1
  73.6 0.0 copy-done.2
  73.6 0.0 copy-done.3
  73.6 0.0 copy-done.4
  73.6 9.4 %sections.1 = bf16[128,16,512]{2,1,0:T(8,128)(2,1)} custom-call(bf16[128,16,1024]{2,1,0:T(8,128)(2,1)} %all-to-all-done.cells_ref, bf16[256,256]{1,0:T(8,128)(2,1)S(1)} %copy-done.1, bf16[256,256]{1,0:T(8,128)(2,1)S(1)} %copy-done.2, bf16[256,256]{1,0:T(8,128)(2,1)S(1)} %copy-done.1, bf16[256,256]{1,0:T(8,128)(2,1)S(1)} %copy-done.2, ...), custom_call_target="tpu_custom_call" | custom-call | tf_op jit(solution)/shard_map/sections/pallas_call | solution.py:277
  83.0 0.0 copy-start.6
  83.0 7.6 %all-to-all-start.1 = ((bf16[128,16,512]{2,1,0:T(8,128)(2,1)}), bf16[128,16,512]{2,1,0:T(8,128)(2,1)S(1)}, u32[]{:S(2)}, u32[]{:S(2)}) async-start(bf16[128,16,512]{2,1,0:T(8,128)(2,1)} %sections.1), calls=%async_computation.1 | async-start | bytes 4194304 | tf_op jit(solution)/shard_map/all_to_all | solution.py:312
  90.6 0.0 copy-done.6
  90.7 0.1 fusion.2
  90.7 0.1 maximum_convert_fusion
  90.9 0.1 copy.15
  91.0 2.2 %broadcast_select_fusion = bf16[4,64,128,4,4]{1,0,4,3,2:T(4,128)(2,1)} fusion(pred[4,4]{0,1:T(4,128)(4,1)S(1)} %iota_compare_fusion, bf16[64,128,4]{0,2,1:T(4,128)(2,1)S(1)} %copy.15), kind=kLoop, calls=%fused_computation | loop fusion | flops 524288 | bytes 1114128 | tf_op jit(solution)/shard_map/jit(_where)/select_n | solution.py:316
  93.2 0.0 copy-start.5
  93.2 4.4 %select_n.13 = bf16[256,2048]{0,1:T(8,128)(2,1)} reshape(bf16[4,64,128,4,4]{1,0,4,3,2:T(4,128)(2,1)} %broadcast_select_fusion) | data formatting | bytes 2097152 | tf_op jit(solution)/shard_map/jit(_where)/select_n | solution.py:316
  97.5 1.5 %copy.16.weights_ref = bf16[256,2048]{1,0:T(8,128)(2,1)S(1)} copy(bf16[256,2048]{0,1:T(8,128)(2,1)} %select_n.13) | data formatting | bytes 2097152 | tf_op jit(solution)/shard_map/jit(_where)/select_n | solution.py:316
  99.0 21.1 %all-to-all-done.1.power_ref = bf16[128,16,512]{2,1,0:T(8,128)(2,1)S(1)} async-done(((bf16[128,16,512]{2,1,0:T(8,128)(2,1)}), bf16[128,16,512]{2,1,0:T(8,128)(2,1)S(1)}, u32[]{:S(2)}, u32[]{:S(2)}) %all-to-all-start.1) | async-done | bytes 2097184 | tf_op jit(solution)/shard_map/all_to_all | solution.py:312
  120.1 0.0 copy-done.5
  120.1 2.1 %cepstra.1 = f32[2,8,64,128]{3,2,1,0:T(8,128)} custom-call(bf16[128,16,512]{2,1,0:T(8,128)(2,1)S(1)} %all-to-all-done.1.power_ref, bf16[256,2048]{1,0:T(8,128)(2,1)S(1)} %copy.16.weights_ref, f32[64,64]{1,0:T(8,128)S(1)} %copy-done.5), custom_call_target="tpu_custom_call" | custom-call | tf_op jit(solution)/shard_map/cepstra/pallas_call | solution.py:317
  (4 shorter events, 0.0 us)
Async XLA Ops:
  0.0 1.6 %copy-start = (bf16[1024,1024]{1,0:T(8,128)(2,1)S(1)}, bf16[1024,1024]{1,0:T(8,128)(2,1)}, u32[]{:S(2)}) copy-start(bf16[1024,1024]{1,0:T(8,128)(2,1)} %constant.28.clone.table_hbm) | copy-start | bytes 6291460
  9.4 64.2 %copy-start.1 = (bf16[256,256]{1,0:T(8,128)(2,1)S(1)}, bf16[256,256]{1,0:T(8,128)(2,1)}, u32[]{:S(2)}) copy-start(bf16[256,256]{1,0:T(8,128)(2,1)} %constant.29.clone.first_ref.third_ref) | copy-start | bytes 393220
  9.4 64.2 %copy-start.2 = (bf16[256,256]{1,0:T(8,128)(2,1)S(1)}, bf16[256,256]{1,0:T(8,128)(2,1)}, u32[]{:S(2)}) copy-start(bf16[256,256]{1,0:T(8,128)(2,1)} %constant.30.clone.second_ref.fourth_ref) | copy-start | bytes 393220
  9.4 64.2 %copy-start.3 = (f32[2,128,128]{2,1,0:T(8,128)S(1)}, f32[2,128,128]{2,1,0:T(8,128)}, u32[]{:S(2)}) copy-start(f32[2,128,128]{2,1,0:T(8,128)} %constant.31.clone.forward_ref) | copy-start | bytes 393220
  9.4 64.2 %copy-start.4 = (f32[2,128,128]{2,1,0:T(8,128)S(1)}, f32[2,128,128]{2,1,0:T(8,128)}, u32[]{:S(2)}) copy-start(f32[2,128,128]{2,1,0:T(8,128)} %constant.32.clone.inverse_ref) | copy-start | bytes 393220
  9.4 64.2 %all-to-all-start = ((bf16[128,16,1024]{2,1,0:T(8,128)(2,1)}), bf16[128,16,1024]{2,1,0:T(8,128)(2,1)}, u32[]{:S(2)}, u32[]{:S(2)}) async-start(bf16[128,16,1024]{2,1,0:T(8,128)(2,1)} %spectrum.1), calls=%async_computation | async-start | bytes 8388608 | tf_op jit(solution)/shard_map/all_to_all | solution.py:271
  83.0 7.6 %copy-start.6 = (s32[66]{0:T(128)S(1)}, s32[66]{0:T(128)}, u32[]{:S(2)}) copy-start(s32[66]{0:T(128)} %param.13) | copy-start | bytes 796
  83.0 37.1 %all-to-all-start.1 = ((bf16[128,16,512]{2,1,0:T(8,128)(2,1)}), bf16[128,16,512]{2,1,0:T(8,128)(2,1)S(1)}, u32[]{:S(2)}, u32[]{:S(2)}) async-start(bf16[128,16,512]{2,1,0:T(8,128)(2,1)} %sections.1), calls=%async_computation.1 | async-start | bytes 4194304 | tf_op jit(solution)/shard_map/all_to_all | solution.py:312
  93.2 26.9 %copy-start.5 = (f32[64,64]{1,0:T(8,128)S(1)}, f32[64,64]{1,0:T(8,128)}, u32[]{:S(2)}) copy-start(f32[64,64]{1,0:T(8,128)} %constant.33.clone.cosine_ref) | copy-start | bytes 49156

commit v4 on v3

--- a/solution.py
+++ b/solution.py
@@ -239,6 +239,7 @@
 
 
 VMEM_LIMIT = 48 * 1024 * 1024
+VMEM_WHOLE = 60 * 1024 * 1024
 
 
 def shards(traces, fan_mask, band_edges):
@@ -264,7 +265,7 @@
             pltpu.SemaphoreType.DMA((chunks, 2)),
             pltpu.SemaphoreType.DMA((chunks, parts)),
         ],
-        compiler_params=params,
+        compiler_params=pltpu.CompilerParams(vmem_limit_bytes=VMEM_WHOLE),
         name="spectrum",
     )(jnp.asarray(time_table(devices)), traces)
 

time: 123 us -> 121 us (0.984)
  local copies, waits for them, and re-layouts: 7.75 us -> 6.16 us
    unnamed x15 -> x13, local copies, waits for them, and re-layouts: 1.65 us -> 0.05 us
where the time goes in v4:
time: 121 us
  waiting for transfers between devices  72 us (60%)
  starting transfers between devices  19.6 us (16%)
  Pallas kernels  19.4 us (16%)
  local copies, waits for them, and re-layouts  6.16 us (5%)
  other arithmetic  3.52 us (3%)
    all_to_all x1, waiting for transfers between devices, shards(): lax.all_to_all(spectrum, axes, split_axis=0, concat_axis=0, tiled=True)  50.9 us
    all_to_all x1, waiting for transfers between devices, shards(): lax.all_to_all(power, axes, split_axis=0, concat_axis=0, tiled=True)  21.1 us
    all_to_all x1, starting transfers between devices, shards(): lax.all_to_all(spectrum, axes, split_axis=0, concat_axis=0, tiled=True)  12 us
    pallas_call x1, Pallas kernels, shards(): pl.pallas_call(functools.partial(sections_kernel, bins), grid=(HALF // 2,...  9.39 us
    pallas_call x1, Pallas kernels, shards(): pl.pallas_call(functools.partial(spectrum_kernel, devices, chunks, parts)...  7.92 us
    all_to_all x1, starting transfers between devices, shards(): lax.all_to_all(power, axes, split_axis=0, concat_axis=0, tiled=True)  7.61 us
    select_n x2, local copies, waits for them, and re-layouts, shards(): jnp.where(same, weights, jnp.zeros((), bf16))  5.83 us
  transfers between devices with their start and end apart: 2, of which 2 were waited for; matrix products, arithmetic and copies ran while one was open for 8% of the time, Pallas kernels for 0%

profile of v4, /device:TPU:1, one launch (start us, length us, event | category | flops | bytes accessed | tf_op | source)
XLA Modules:
  0.0 120.8 jit_solution(9764167278802866310)
XLA Ops:
  0.0 7.9 %spectrum.1 = bf16[128,16,1024]{2,1,0:T(8,128)(2,1)} custom-call(bf16[1024,1024]{1,0:T(8,128)(2,1)} %constant.28.clone.table_hbm, bf16[128,16384]{1,0:T(8,128)(2,1)} %traces_hbm.1), custom_call_target="tpu_custom_call" | custom-call | tf_op jit(solution)/shard_map/spectrum/pallas_call | solution.py:255
  7.9 0.0 copy-start
  7.9 0.0 copy-start.1
  8.0 0.0 copy-start.2
  8.0 0.0 copy-start.3
  8.0 12.0 %all-to-all-start = ((bf16[128,16,1024]{2,1,0:T(8,128)(2,1)}), bf16[128,16,1024]{2,1,0:T(8,128)(2,1)}, u32[]{:S(2)}, u32[]{:S(2)}) async-start(bf16[128,16,1024]{2,1,0:T(8,128)(2,1)} %spectrum.1), calls=%async_computation | async-start | bytes 8388608 | tf_op jit(solution)/shard_map/all_to_all | solution.py:272
  20.0 1.1 fusion.1
  21.1 0.1 copy.14
  21.3 50.9 %all-to-all-done.cells_ref = bf16[128,16,1024]{2,1,0:T(8,128)(2,1)} async-done(((bf16[128,16,1024]{2,1,0:T(8,128)(2,1)}), bf16[128,16,1024]{2,1,0:T(8,128)(2,1)}, u32[]{:S(2)}, u32[]{:S(2)}) %all-to-all-start) | async-done | bytes 4194336 | tf_op jit(solution)/shard_map/all_to_all | solution.py:272
  72.2 0.0 copy-done
  72.2 0.0 copy-done.1
  72.2 0.0 copy-done.2
  72.2 0.0 copy-done.3
  72.2 9.4 %sections.1 = bf16[128,16,512]{2,1,0:T(8,128)(2,1)} custom-call(bf16[128,16,1024]{2,1,0:T(8,128)(2,1)} %all-to-all-done.cells_ref, bf16[256,256]{1,0:T(8,128)(2,1)S(1)} %copy-done, bf16[256,256]{1,0:T(8,128)(2,1)S(1)} %copy-done.1, bf16[256,256]{1,0:T(8,128)(2,1)S(1)} %copy-done, bf16[256,256]{1,0:T(8,128)(2,1)S(1)} %copy-done.1, ...), custom_call_target="tpu_custom_call" | custom-call | tf_op jit(solution)/shard_map/sections/pallas_call | solution.py:278
  81.6 0.0 copy-start.5
  81.6 7.6 %all-to-all-start.1 = ((bf16[128,16,512]{2,1,0:T(8,128)(2,1)}), bf16[128,16,512]{2,1,0:T(8,128)(2,1)S(1)}, u32[]{:S(2)}, u32[]{:S(2)}) async-start(bf16[128,16,512]{2,1,0:T(8,128)(2,1)} %sections.1), calls=%async_computation.1 | async-start | bytes 4194304 | tf_op jit(solution)/shard_map/all_to_all | solution.py:313
  89.2 0.0 copy-done.5
  89.2 0.1 fusion.2
  89.3 0.1 maximum_convert_fusion
  89.4 0.1 copy.15
  89.6 2.2 %broadcast_select_fusion = bf16[4,64,128,4,4]{1,0,4,3,2:T(4,128)(2,1)} fusion(pred[4,4]{0,1:T(4,128)(4,1)S(1)} %iota_compare_fusion, bf16[64,128,4]{0,2,1:T(4,128)(2,1)S(1)} %copy.15), kind=kLoop, calls=%fused_computation | loop fusion | flops 524288 | bytes 1114128 | tf_op jit(solution)/shard_map/jit(_where)/select_n | solution.py:317
  91.8 0.0 copy-start.4
  91.8 4.4 %select_n.13 = bf16[256,2048]{0,1:T(8,128)(2,1)} reshape(bf16[4,64,128,4,4]{1,0,4,3,2:T(4,128)(2,1)} %broadcast_select_fusion) | data formatting | bytes 2097152 | tf_op jit(solution)/shard_map/jit(_where)/select_n | solution.py:317
  96.1 1.5 %copy.16.weights_ref = bf16[256,2048]{1,0:T(8,128)(2,1)S(1)} copy(bf16[256,2048]{0,1:T(8,128)(2,1)} %select_n.13) | data formatting | bytes 2097152 | tf_op jit(solution)/shard_map/jit(_where)/select_n | solution.py:317
  97.6 21.1 %all-to-all-done.1.power_ref = bf16[128,16,512]{2,1,0:T(8,128)(2,1)S(1)} async-done(((bf16[128,16,512]{2,1,0:T(8,128)(2,1)}), bf16[128,16,512]{2,1,0:T(8,128)(2,1)S(1)}, u32[]{:S(2)}, u32[]{:S(2)}) %all-to-all-start.1) | async-done | bytes 2097184 | tf_op jit(solution)/shard_map/all_to_all | solution.py:313
  118.7 0.0 copy-done.4
  118.7 2.1 %cepstra.1 = f32[2,8,64,128]{3,2,1,0:T(8,128)} custom-call(bf16[128,16,512]{2,1,0:T(8,128)(2,1)S(1)} %all-to-all-done.1.power_ref, bf16[256,2048]{1,0:T(8,128)(2,1)S(1)} %copy.16.weights_ref, f32[64,64]{1,0:T(8,128)S(1)} %copy-done.4), custom_call_target="tpu_custom_call" | custom-call | tf_op jit(solution)/shard_map/cepstra/pallas_call | solution.py:318
  (4 shorter events, 0.0 us)
Async XLA Ops:
  7.9 64.2 %copy-start = (bf16[256,256]{1,0:T(8,128)(2,1)S(1)}, bf16[256,256]{1,0:T(8,128)(2,1)}, u32[]{:S(2)}) copy-start(bf16[256,256]{1,0:T(8,128)(2,1)} %constant.29.clone.first_ref.third_ref) | copy-start | bytes 393220
  7.9 64.2 %copy-start.1 = (bf16[256,256]{1,0:T(8,128)(2,1)S(1)}, bf16[256,256]{1,0:T(8,128)(2,1)}, u32[]{:S(2)}) copy-start(bf16[256,256]{1,0:T(8,128)(2,1)} %constant.30.clone.second_ref.fourth_ref) | copy-start | bytes 393220
  8.0 64.2 %copy-start.2 = (f32[2,128,128]{2,1,0:T(8,128)S(1)}, f32[2,128,128]{2,1,0:T(8,128)}, u32[]{:S(2)}) copy-start(f32[2,128,128]{2,1,0:T(8,128)} %constant.31.clone.forward_ref) | copy-start | bytes 393220
  8.0 64.2 %copy-start.3 = (f32[2,128,128]{2,1,0:T(8,128)S(1)}, f32[2,128,128]{2,1,0:T(8,128)}, u32[]{:S(2)}) copy-start(f32[2,128,128]{2,1,0:T(8,128)} %constant.32.clone.inverse_ref) | copy-start | bytes 393220
  8.0 64.2 %all-to-all-start = ((bf16[128,16,1024]{2,1,0:T(8,128)(2,1)}), bf16[128,16,1024]{2,1,0:T(8,128)(2,1)}, u32[]{:S(2)}, u32[]{:S(2)}) async-start(bf16[128,16,1024]{2,1,0:T(8,128)(2,1)} %spectrum.1), calls=%async_computation | async-start | bytes 8388608 | tf_op jit(solution)/shard_map/all_to_all | solution.py:272
  81.6 7.6 %copy-start.5 = (s32[66]{0:T(128)S(1)}, s32[66]{0:T(128)}, u32[]{:S(2)}) copy-start(s32[66]{0:T(128)} %param.13) | copy-start | bytes 796
  81.6 37.1 %all-to-all-start.1 = ((bf16[128,16,512]{2,1,0:T(8,128)(2,1)}), bf16[128,16,512]{2,1,0:T(8,128)(2,1)S(1)}, u32[]{:S(2)}, u32[]{:S(2)}) async-start(bf16[128,16,512]{2,1,0:T(8,128)(2,1)} %sections.1), calls=%async_computation.1 | async-start | bytes 4194304 | tf_op jit(solution)/shard_map/all_to_all | solution.py:313
  91.8 26.9 %copy-start.4 = (f32[64,64]{1,0:T(8,128)S(1)}, f32[64,64]{1,0:T(8,128)}, u32[]{:S(2)}) copy-start(f32[64,64]{1,0:T(8,128)} %constant.33.clone.cosine_ref) | copy-start | bytes 49156

commit v5 on v4

--- a/solution.py
+++ b/solution.py
@@ -18,6 +18,7 @@
 NB = 64
 FRAMES = 16
 HALF = FRAMES // 2
+PIECES = 2
 
 energy_floor = 0.05
 
@@ -76,6 +77,7 @@
 
 def spectrum_kernel(
     devices,
+    piece,
     chunks,
     parts,
     table_hbm,
@@ -91,7 +93,7 @@
     rows = 2 * NF // devices
     height = 2 * NF // parts
     owners = devices // parts
-    frames = HALF // chunks
+    frames = HALF // PIECES // chunks
     width = frames * FLEN
     lanes = frames * N1
 
@@ -100,7 +102,7 @@
         return pltpu.make_async_copy(table_hbm.at[at], table.at[at], table_sem.at[j])
 
     def traces_copy(i, half):
-        at = pl.ds((half * chunks + i) * width, width)
+        at = pl.ds(((half * PIECES + piece) * chunks + i) * width, width)
         return pltpu.make_async_copy(
             traces_hbm.at[:, at], traces.at[i, half], traces_sem.at[i, half]
         )
@@ -150,6 +152,7 @@
 
 def sections_kernel(
     bins,
+    earlier,
     cells_ref,
     first_ref,
     second_ref,
@@ -158,13 +161,9 @@
     forward_ref,
     inverse_ref,
     mask_ref,
-    power_ref,
-    cells,
-    turned,
-    kept,
-    back,
-    power_rows,
+    *refs,
 ):
+    power_ref, cells, turned, kept, back, power_rows = refs[earlier:]
     rows = 4 * bins
     group = 16
     count = 4 * bins
@@ -252,55 +251,40 @@
     params = pltpu.CompilerParams(vmem_limit_bytes=VMEM_LIMIT)
 
     chunks, parts = 2, 2
-    spectrum = pl.pallas_call(
-        functools.partial(spectrum_kernel, devices, chunks, parts),
-        in_specs=[pl.BlockSpec(memory_space=pltpu.HBM)] * 2,
-        out_specs=pl.BlockSpec(memory_space=pltpu.HBM),
-        out_shape=jax.ShapeDtypeStruct((devices, rows, HALF * N1), bf16),
-        scratch_shapes=[
-            pltpu.VMEM((2 * NF, FLEN), bf16),
-            pltpu.VMEM((chunks, 2, N1, HALF // chunks * FLEN), bf16),
-            pltpu.VMEM((devices, rows, HALF * N1), bf16),
-            pltpu.SemaphoreType.DMA((parts,)),
-            pltpu.SemaphoreType.DMA((chunks, 2)),
-            pltpu.SemaphoreType.DMA((chunks, parts)),
-        ],
-        compiler_params=pltpu.CompilerParams(vmem_limit_bytes=VMEM_WHOLE),
-        name="spectrum",
-    )(jnp.asarray(time_table(devices)), traces)
-
-    cells = lax.all_to_all(spectrum, axes, split_axis=0, concat_axis=0, tiled=True)
+    lanes = HALF // PIECES * N1
+    table = jnp.asarray(time_table(devices))
+    cells = []
+    for piece in range(PIECES):
+        spectrum = pl.pallas_call(
+            functools.partial(spectrum_kernel, devices, piece, chunks, parts),
+            in_specs=[pl.BlockSpec(memory_space=pltpu.HBM)] * 2,
+            out_specs=pl.BlockSpec(memory_space=pltpu.HBM),
+            out_shape=jax.ShapeDtypeStruct((devices, rows, lanes), bf16),
+            scratch_shapes=[
+                pltpu.VMEM((2 * NF, FLEN), bf16),
+                pltpu.VMEM((chunks, 2, N1, HALF // PIECES // chunks * FLEN), bf16),
+                pltpu.VMEM((devices, rows, lanes), bf16),
+                pltpu.SemaphoreType.DMA((parts,)),
+                pltpu.SemaphoreType.DMA((chunks, 2)),
+                pltpu.SemaphoreType.DMA((chunks, parts)),
+            ],
+            compiler_params=pltpu.CompilerParams(vmem_limit_bytes=VMEM_WHOLE),
+            cost_estimate=pl.CostEstimate(
+                flops=4 * NF * FLEN * N1 * FRAMES // PIECES,
+                bytes_accessed=6 * 1024 * 1024,
+                transcendentals=0,
+            ),
+            name="spectrum",
+        )(table, traces)
+        cells.append(
+            lax.all_to_all(spectrum, axes, split_axis=0, concat_axis=0, tiled=True)
+        )
 
     mask = lax.dynamic_slice_in_dim(fan_mask, lax.axis_index("sub") * bins, bins, 0)
     mask = jnp.transpose(mask.reshape(bins, N1, N2), (0, 2, 1))
     mask = (mask > 0).astype(bf16)
 
-    power = pl.pallas_call(
-        functools.partial(sections_kernel, bins),
-        grid=(HALF // 2,),
-        in_specs=[
-            pl.BlockSpec((N2, rows, 2 * N1), lambda i: (0, 0, i)),
-            whole((2 * N2, 2 * N2)),
-            whole((2 * N1, 2 * N1)),
-            whole((2 * N1, 2 * N1)),
-            whole((2 * N2, 2 * N2)),
-            whole((2, N2, N1)),
-            whole((2, N2, N1)),
-            whole((bins, N2, N1)),
-        ],
-        out_specs=pl.BlockSpec((N2, rows, N1), lambda i: (0, 0, i)),
-        out_shape=jax.ShapeDtypeStruct((N2, rows, HALF // 2 * N1), bf16),
-        scratch_shapes=[
-            pltpu.VMEM((2 * N2, rows * N1), bf16),
-            pltpu.VMEM((rows * N2, 2 * N1), bf16),
-            pltpu.VMEM((rows * N2, 2 * N1), bf16),
-            pltpu.VMEM((2 * N2, rows * N1), bf16),
-            pltpu.VMEM((rows, N2, N1), bf16),
-        ],
-        compiler_params=params,
-        name="sections",
-    )(
-        cells,
+    tables = (
         jnp.asarray(left_table(N2, -1.0)),
         jnp.asarray(right_table(N1, -1.0)),
         jnp.asarray(right_table(N1, 1.0)),
@@ -309,6 +293,42 @@
         jnp.asarray(twiddle(1.0)),
         mask,
     )
+    steps = HALF // 2 // PIECES
+    power = None
+    for piece in range(PIECES):
+        earlier = () if power is None else (power,)
+        power = pl.pallas_call(
+            functools.partial(sections_kernel, bins, len(earlier)),
+            grid=(steps,),
+            in_specs=[
+                pl.BlockSpec((N2, rows, 2 * N1), lambda i: (0, 0, i)),
+                whole((2 * N2, 2 * N2)),
+                whole((2 * N1, 2 * N1)),
+                whole((2 * N1, 2 * N1)),
+                whole((2 * N2, 2 * N2)),
+                whole((2, N2, N1)),
+                whole((2, N2, N1)),
+                whole((bins, N2, N1)),
+            ]
+            + [pl.BlockSpec(memory_space=pltpu.HBM)] * len(earlier),
+            out_specs=pl.BlockSpec((N2, rows, N1), lambda i, at=piece * steps: (0, 0, i + at)),
+            out_shape=jax.ShapeDtypeStruct((N2, rows, HALF // 2 * N1), bf16),
+            scratch_shapes=[
+                pltpu.VMEM((2 * N2, rows * N1), bf16),
+                pltpu.VMEM((rows * N2, 2 * N1), bf16),
+                pltpu.VMEM((rows * N2, 2 * N1), bf16),
+                pltpu.VMEM((2 * N2, rows * N1), bf16),
+                pltpu.VMEM((rows, N2, N1), bf16),
+            ],
+            input_output_aliases={8: 0} if earlier else {},
+            compiler_params=params,
+            cost_estimate=pl.CostEstimate(
+                flops=4 * 2 * 4 * N1 * N1 * N1 * bins * FRAMES // PIECES,
+                bytes_accessed=3 * 1024 * 1024,
+                transcendentals=0,
+            ),
+            name="sections",
+        )(cells[piece], *tables, *earlier)
 
     returned = lax.all_to_all(power, axes, split_axis=0, concat_axis=0, tiled=True)
 

time: 121 us -> 127 us (1.050)
  local copies, waits for them, and re-layouts: 6.16 us -> 10.4 us
  waiting for transfers between devices: 72 us -> 67.9 us
  starting transfers between devices: 19.6 us -> 22.4 us
  Pallas kernels: 19.4 us -> 21.6 us
    all_to_all x1 -> x2, starting transfers between devices: 12 us -> 17.3 us  [shards(): lax.all_to_all(spectrum, axes, split_axis=0, concat_axis=0, tiled=True)]
    unnamed x13 -> x19, local copies, waits for them, and re-layouts: 0.05 us -> 4.31 us
    all_to_all x1 -> x2, waiting for transfers between devices: 50.9 us -> 46.8 us  [shards(): lax.all_to_all(spectrum, axes, split_axis=0, concat_axis=0, tiled=True)]
    all_to_all x1, starting transfers between devices: 7.61 us -> 5.15 us  [shards(): lax.all_to_all(power, axes, split_axis=0, concat_axis=0, tiled=True)]
    pallas_call x2 -> x4, Pallas kernels: 17.3 us -> 19.5 us  [the longest x2 10.5 us: shards(): pl.pallas_call(functools.partial(spectrum_kernel, devices, piece, chunks,...]
  transfers between devices with their start and end apart: 2 -> 3, of which waited for: 2 -> 3; matrix products, arithmetic and copies ran while one was open for 8% -> 8% of each run, Pallas kernels for 0% -> 7%
where the time goes in v5:
time: 127 us; the launch traced here: 126 us
  waiting for transfers between devices  67.9 us (53%)
  starting transfers between devices  22.4 us (18%)
  Pallas kernels  21.6 us (17%)
  local copies, waits for them, and re-layouts  10.4 us (8%)
  other arithmetic  3.5 us (3%)
    all_to_all x2, waiting for transfers between devices, shards(): lax.all_to_all(spectrum, axes, split_axis=0, concat_axis=0, tiled=True)  46.8 us
    all_to_all x1, waiting for transfers between devices, shards(): lax.all_to_all(power, axes, split_axis=0, concat_axis=0, tiled=True)  21.1 us
    all_to_all x2, starting transfers between devices, shards(): lax.all_to_all(spectrum, axes, split_axis=0, concat_axis=0, tiled=True)  17.3 us
    pallas_call x2, Pallas kernels, shards(): pl.pallas_call(functools.partial(spectrum_kernel, devices, piece, chunks,...  10.5 us
    pallas_call x2, Pallas kernels, shards(): pl.pallas_call(functools.partial(sections_kernel, bins, len(earlier)), gr...  9.09 us
    select_n x2, local copies, waits for them, and re-layouts, shards(): jnp.where(same, weights, jnp.zeros((), bf16))  5.83 us
    all_to_all x1, starting transfers between devices, shards(): lax.all_to_all(power, axes, split_axis=0, concat_axis=0, tiled=True)  5.15 us
    unnamed x19, local copies, waits for them, and re-layouts  4.31 us
  transfers between devices with their start and end apart: 3, of which 3 were waited for; matrix products, arithmetic and copies ran while one was open for 8% of the time, Pallas kernels for 7%

profile of v5, /device:TPU:1, one launch (start us, length us, event | category | flops | bytes accessed | tf_op | source)
XLA Modules:
  0.0 126.1 jit_solution(9652872285357530430)
XLA Ops:
  0.0 5.2 %spectrum.3 = bf16[128,16,512]{2,1,0:T(8,128)(2,1)} custom-call(bf16[1024,1024]{1,0:T(8,128)(2,1)} %constant.28.clone.table_hbm, bf16[128,16384]{1,0:T(8,128)(2,1)} %traces_hbm.3), custom_call_target="tpu_custom_call" | custom-call | flops 2147483648 | bytes 6291456 | tf_op jit(solution)/shard_map/spectrum/pallas_call | solution.py:258
  5.2 11.5 %all-to-all-start.1 = ((bf16[128,16,512]{2,1,0:T(8,128)(2,1)}), bf16[128,16,512]{2,1,0:T(8,128)(2,1)S(1)}, u32[]{:S(2)}, u32[]{:S(2)}) async-start(bf16[128,16,512]{2,1,0:T(8,128)(2,1)} %spectrum.3), calls=%async_computation.1 | async-start | bytes 4194304 | tf_op jit(solution)/shard_map/all_to_all | solution.py:280
  16.7 5.2 %spectrum.2 = bf16[128,16,512]{2,1,0:T(8,128)(2,1)} custom-call(bf16[1024,1024]{1,0:T(8,128)(2,1)} %constant.28.clone.table_hbm, bf16[128,16384]{1,0:T(8,128)(2,1)} %traces_hbm.3), custom_call_target="tpu_custom_call" | custom-call | flops 2147483648 | bytes 6291456 | tf_op jit(solution)/shard_map/spectrum/pallas_call | solution.py:258
  22.0 0.0 copy-start.4
  22.0 0.0 copy-start.5
  22.0 0.0 copy-start.6
  22.0 0.0 copy-start.7
  22.0 24.2 %all-to-all-done.1.cells_ref = bf16[128,16,512]{2,1,0:T(8,128)(2,1)S(1)} async-done(((bf16[128,16,512]{2,1,0:T(8,128)(2,1)}), bf16[128,16,512]{2,1,0:T(8,128)(2,1)S(1)}, u32[]{:S(2)}, u32[]{:S(2)}) %all-to-all-start.1) | async-done | bytes 2097184 | tf_op jit(solution)/shard_map/all_to_all | solution.py:280
  46.3 5.8 %all-to-all-start = ((bf16[128,16,512]{2,1,0:T(8,128)(2,1)}), bf16[128,16,512]{2,1,0:T(8,128)(2,1)}, u32[]{:S(2)}, u32[]{:S(2)}) async-start(bf16[128,16,512]{2,1,0:T(8,128)(2,1)} %spectrum.2), calls=%async_computation | async-start | bytes 4194304 | tf_op jit(solution)/shard_map/all_to_all | solution.py:280
  52.0 1.1 fusion.1
  53.2 0.1 copy.15
  53.3 0.0 copy-done.4
  53.3 0.0 copy-done.5
  53.4 0.0 copy-done.6
  53.4 0.0 copy-done.7
  53.4 4.0 %sections.2.refs_0_ = bf16[128,16,512]{2,1,0:T(8,128)(2,1)S(1)} custom-call(bf16[128,16,512]{2,1,0:T(8,128)(2,1)S(1)} %all-to-all-done.1.cells_ref, bf16[256,256]{1,0:T(8,128)(2,1)S(1)} %copy-done.4, bf16[256,256]{1,0:T(8,128)(2,1)S(1)} %copy-done.5, bf16[256,256]{1,0:T(8,128)(2,1)S(1)} %copy-done.4, bf16[256,256]{1,0:T(8,128)(2,1)S(1)} %copy-done.5, ...), custom_call_target="tpu_custom_call" | custom-call | flops 2147483648 | bytes 3145728 | tf_op jit(solution)/shard_map/sections/pallas_call | solution.py:300
  57.4 0.0 copy-start
  57.4 1.3 %copy-done = bf16[128,16,512]{2,1,0:T(8,128)(2,1)} copy-done((bf16[128,16,512]{2,1,0:T(8,128)(2,1)}, bf16[128,16,512]{2,1,0:T(8,128)(2,1)S(1)}, u32[]{:S(2)}) %copy-start) | copy-done | bytes 2097176
  58.7 22.6 %all-to-all-done.cells_ref = bf16[128,16,512]{2,1,0:T(8,128)(2,1)} async-done(((bf16[128,16,512]{2,1,0:T(8,128)(2,1)}), bf16[128,16,512]{2,1,0:T(8,128)(2,1)}, u32[]{:S(2)}, u32[]{:S(2)}) %all-to-all-start) | async-done | bytes 2097184 | tf_op jit(solution)/shard_map/all_to_all | solution.py:280
  81.3 0.0 copy-start.1
  81.3 1.6 %copy-done.1 = bf16[128,16,512]{2,1,0:T(8,128)(2,1)S(1)} copy-done((bf16[128,16,512]{2,1,0:T(8,128)(2,1)S(1)}, bf16[128,16,512]{2,1,0:T(8,128)(2,1)}, u32[]{:S(2)}) %copy-start.1) | copy-done | bytes 2097176
  82.9 5.1 %sections.3 = bf16[128,16,512]{2,1,0:T(8,128)(2,1)S(1)} custom-call(bf16[128,16,512]{2,1,0:T(8,128)(2,1)} %all-to-all-done.cells_ref, bf16[256,256]{1,0:T(8,128)(2,1)S(1)} %copy-done.4, bf16[256,256]{1,0:T(8,128)(2,1)S(1)} %copy-done.5, bf16[256,256]{1,0:T(8,128)(2,1)S(1)} %copy-done.4, ...), custom_call_target="tpu_custom_call", output_to_operand_aliasing={{}: (8, {})} | custom-call | flops 2147483648 | bytes 3145728 | tf_op jit(solution)/shard_map/sections/pallas_call | solution.py:300
  88.0 0.0 copy-start.2
  88.0 1.3 %copy-done.2 = bf16[128,16,512]{2,1,0:T(8,128)(2,1)} copy-done((bf16[128,16,512]{2,1,0:T(8,128)(2,1)}, bf16[128,16,512]{2,1,0:T(8,128)(2,1)S(1)}, u32[]{:S(2)}) %copy-start.2) | copy-done | bytes 2097176
  89.3 0.0 copy-start.8
  89.3 5.1 %all-to-all-start.2 = ((bf16[128,16,512]{2,1,0:T(8,128)(2,1)}), bf16[128,16,512]{2,1,0:T(8,128)(2,1)S(1)}, u32[]{:S(2)}, u32[]{:S(2)}) async-start(bf16[128,16,512]{2,1,0:T(8,128)(2,1)} %copy-done.2), calls=%async_computation.2 | async-start | bytes 4194304 | tf_op jit(solution)/shard_map/all_to_all | solution.py:333
  94.5 0.0 copy-done.8
  94.5 0.1 fusion.2
  94.6 0.1 maximum_convert_fusion
  94.7 0.1 copy.16
  94.9 2.2 %broadcast_select_fusion = bf16[4,64,128,4,4]{1,0,4,3,2:T(4,128)(2,1)} fusion(pred[4,4]{0,1:T(4,128)(4,1)S(1)} %iota_compare_fusion, bf16[64,128,4]{0,2,1:T(4,128)(2,1)S(1)} %copy.16), kind=kLoop, calls=%fused_computation | loop fusion | flops 524288 | bytes 1114128 | tf_op jit(solution)/shard_map/jit(_where)/select_n | solution.py:337
  97.0 0.0 copy-start.3
  97.0 4.4 %select_n.13 = bf16[256,2048]{0,1:T(8,128)(2,1)} reshape(bf16[4,64,128,4,4]{1,0,4,3,2:T(4,128)(2,1)} %broadcast_select_fusion) | data formatting | bytes 2097152 | tf_op jit(solution)/shard_map/jit(_where)/select_n | solution.py:337
  101.4 1.5 %copy.17.weights_ref = bf16[256,2048]{1,0:T(8,128)(2,1)S(1)} copy(bf16[256,2048]{0,1:T(8,128)(2,1)} %select_n.13) | data formatting | bytes 2097152 | tf_op jit(solution)/shard_map/jit(_where)/select_n | solution.py:337
  102.9 21.1 %all-to-all-done.2.power_ref = bf16[128,16,512]{2,1,0:T(8,128)(2,1)S(1)} async-done(((bf16[128,16,512]{2,1,0:T(8,128)(2,1)}), bf16[128,16,512]{2,1,0:T(8,128)(2,1)S(1)}, u32[]{:S(2)}, u32[]{:S(2)}) %all-to-all-start.2) | async-done | bytes 2097184 | tf_op jit(solution)/shard_map/all_to_all | solution.py:333
  124.0 0.0 copy-done.3
  124.0 2.1 %cepstra.1 = f32[2,8,64,128]{3,2,1,0:T(8,128)} custom-call(bf16[128,16,512]{2,1,0:T(8,128)(2,1)S(1)} %all-to-all-done.2.power_ref, bf16[256,2048]{1,0:T(8,128)(2,1)S(1)} %copy.17.weights_ref, f32[64,64]{1,0:T(8,128)S(1)} %copy-done.3), custom_call_target="tpu_custom_call" | custom-call | tf_op jit(solution)/shard_map/cepstra/pallas_call | solution.py:338
  (4 shorter events, 0.0 us)
Async XLA Ops:
  5.2 41.0 %all-to-all-start.1 = ((bf16[128,16,512]{2,1,0:T(8,128)(2,1)}), bf16[128,16,512]{2,1,0:T(8,128)(2,1)S(1)}, u32[]{:S(2)}, u32[]{:S(2)}) async-start(bf16[128,16,512]{2,1,0:T(8,128)(2,1)} %spectrum.3), calls=%async_computation.1 | async-start | bytes 4194304 | tf_op jit(solution)/shard_map/all_to_all | solution.py:280
  22.0 31.4 %copy-start.4 = (bf16[256,256]{1,0:T(8,128)(2,1)S(1)}, bf16[256,256]{1,0:T(8,128)(2,1)}, u32[]{:S(2)}) copy-start(bf16[256,256]{1,0:T(8,128)(2,1)} %constant.29.clone.first_ref.third_ref) | copy-start | bytes 393220
  22.0 31.4 %copy-start.5 = (bf16[256,256]{1,0:T(8,128)(2,1)S(1)}, bf16[256,256]{1,0:T(8,128)(2,1)}, u32[]{:S(2)}) copy-start(bf16[256,256]{1,0:T(8,128)(2,1)} %constant.30.clone.second_ref.fourth_ref) | copy-start | bytes 393220
  22.0 31.4 %copy-start.6 = (f32[2,128,128]{2,1,0:T(8,128)S(1)}, f32[2,128,128]{2,1,0:T(8,128)}, u32[]{:S(2)}) copy-start(f32[2,128,128]{2,1,0:T(8,128)} %constant.31.clone.forward_ref) | copy-start | bytes 393220
  22.0 31.4 %copy-start.7 = (f32[2,128,128]{2,1,0:T(8,128)S(1)}, f32[2,128,128]{2,1,0:T(8,128)}, u32[]{:S(2)}) copy-start(f32[2,128,128]{2,1,0:T(8,128)} %constant.32.clone.inverse_ref) | copy-start | bytes 393220
  46.3 35.1 %all-to-all-start = ((bf16[128,16,512]{2,1,0:T(8,128)(2,1)}), bf16[128,16,512]{2,1,0:T(8,128)(2,1)}, u32[]{:S(2)}, u32[]{:S(2)}) async-start(bf16[128,16,512]{2,1,0:T(8,128)(2,1)} %spectrum.2), calls=%async_computation | async-start | bytes 4194304 | tf_op jit(solution)/shard_map/all_to_all | solution.py:280
  57.4 1.3 %copy-start = (bf16[128,16,512]{2,1,0:T(8,128)(2,1)}, bf16[128,16,512]{2,1,0:T(8,128)(2,1)S(1)}, u32[]{:S(2)}) copy-start(bf16[128,16,512]{2,1,0:T(8,128)(2,1)S(1)} %sections.2.refs_0_) | copy-start | bytes 6291460
  81.3 1.6 %copy-start.1 = (bf16[128,16,512]{2,1,0:T(8,128)(2,1)S(1)}, bf16[128,16,512]{2,1,0:T(8,128)(2,1)}, u32[]{:S(2)}) copy-start(bf16[128,16,512]{2,1,0:T(8,128)(2,1)} %copy-done) | copy-start | bytes 6291460
  88.0 1.3 %copy-start.2 = (bf16[128,16,512]{2,1,0:T(8,128)(2,1)}, bf16[128,16,512]{2,1,0:T(8,128)(2,1)S(1)}, u32[]{:S(2)}) copy-start(bf16[128,16,512]{2,1,0:T(8,128)(2,1)S(1)} %sections.3) | copy-start | bytes 6291460
  89.3 5.2 %copy-start.8 = (s32[66]{0:T(128)S(1)}, s32[66]{0:T(128)}, u32[]{:S(2)}) copy-start(s32[66]{0:T(128)} %param.13) | copy-start | bytes 796
  89.3 34.7 %all-to-all-start.2 = ((bf16[128,16,512]{2,1,0:T(8,128)(2,1)}), bf16[128,16,512]{2,1,0:T(8,128)(2,1)S(1)}, u32[]{:S(2)}, u32[]{:S(2)}) async-start(bf16[128,16,512]{2,1,0:T(8,128)(2,1)} %copy-done.2), calls=%async_computation.2 | async-start | bytes 4194304 | tf_op jit(solution)/shard_map/all_to_all | solution.py:333
  97.0 27.0 %copy-start.3 = (f32[64,64]{1,0:T(8,128)S(1)}, f32[64,64]{1,0:T(8,128)}, u32[]{:S(2)}) copy-start(f32[64,64]{1,0:T(8,128)} %constant.33.clone.cosine_ref) | copy-start | bytes 49156

commit v6 on v4

--- a/solution.py
+++ b/solution.py
@@ -8,6 +8,7 @@
 from jax import lax
 from jax.experimental import pallas as pl
 from jax.experimental.pallas import tpu as pltpu
+from jax.sharding import Mesh
 from jax.sharding import PartitionSpec as P
 
 NCH = 16384
@@ -21,6 +22,15 @@
 
 energy_floor = 0.05
 
+PLACES = {"x": 4, "zl": 2, "y": 4, "zh": 2, "core": 2}
+ORDER = ("zl", "y", "core", "x", "zh")
+
+
+def listed():
+    names = tuple(PLACES)
+    devices = np.arange(math.prod(PLACES.values())).reshape(tuple(PLACES.values()))
+    return devices.transpose([names.index(name) for name in ORDER]).reshape(-1)
+
 
 def time_table(devices):
     bins = NF // devices
@@ -30,7 +40,7 @@
     phases = 2.0 * math.pi / FLEN * ((f[:, None] * t[None, :]) % FLEN)
     factor = (0.375 * FLEN) ** -0.5
     table = np.stack([np.cos(phases), -np.sin(phases)], axis=0) * (hann * factor)
-    table = table.reshape(2, devices, bins, FLEN).transpose(1, 0, 2, 3)
+    table = table.reshape(2, devices, bins, FLEN)[:, listed()].transpose(1, 0, 2, 3)
     return table.reshape(2 * NF, FLEN).astype(ml_dtypes.bfloat16)
 
 
@@ -65,9 +75,9 @@
     return (np.cos(phases) * weight[:, None]).astype(np.float32)
 
 
-def band_weights(band_edges):
+def band_weights(band_edges, freq):
     bounds = band_edges.astype(jnp.float32)
-    freq = jnp.arange(NF, dtype=jnp.int32).astype(jnp.float32)[None, :]
+    freq = freq.astype(jnp.float32)[None, :]
     low, middle, high = bounds[:-2, None], bounds[1:-1, None], bounds[2:, None]
     rising = (freq - low) / (middle - low)
     falling = (high - freq) / (high - middle)
@@ -243,10 +253,9 @@
 
 
 def shards(traces, fan_mask, band_edges):
-    axes = ("chan", "sub")
-    devices = lax.axis_size("chan") * lax.axis_size("sub")
-    sub_count = lax.axis_size("sub")
+    devices = math.prod(lax.axis_size(name) for name in PLACES)
     bins = NF // devices
+    order = np.concatenate([listed(), N2 + listed()])
     rows = 4 * bins
     bf16 = jnp.bfloat16
     params = pltpu.CompilerParams(vmem_limit_bytes=VMEM_LIMIT)
@@ -269,9 +278,9 @@
         name="spectrum",
     )(jnp.asarray(time_table(devices)), traces)
 
-    cells = lax.all_to_all(spectrum, axes, split_axis=0, concat_axis=0, tiled=True)
-
-    mask = lax.dynamic_slice_in_dim(fan_mask, lax.axis_index("sub") * bins, bins, 0)
+    cells = lax.all_to_all(spectrum, ORDER, split_axis=0, concat_axis=0, tiled=True)
+
+    mask = lax.dynamic_slice_in_dim(fan_mask, lax.axis_index(("zh", "core")) * bins, bins, 0)
     mask = jnp.transpose(mask.reshape(bins, N1, N2), (0, 2, 1))
     mask = (mask > 0).astype(bf16)
 
@@ -301,18 +310,19 @@
         name="sections",
     )(
         cells,
-        jnp.asarray(left_table(N2, -1.0)),
+        jnp.asarray(left_table(N2, -1.0)[:, order]),
         jnp.asarray(right_table(N1, -1.0)),
         jnp.asarray(right_table(N1, 1.0)),
-        jnp.asarray(left_table(N2, 1.0)),
+        jnp.asarray(left_table(N2, 1.0)[order]),
         jnp.asarray(twiddle(-1.0)),
         jnp.asarray(twiddle(1.0)),
         mask,
     )
 
-    returned = lax.all_to_all(power, axes, split_axis=0, concat_axis=0, tiled=True)
-
-    weights = band_weights(band_edges).reshape(1, NB, devices, 1, bins)
+    returned = lax.all_to_all(power, ORDER, split_axis=0, concat_axis=0, tiled=True)
+
+    freq = (listed()[:, None] * bins + np.arange(bins)).reshape(-1)
+    weights = band_weights(band_edges, jnp.asarray(freq)).reshape(1, NB, devices, 1, bins)
     same = jnp.eye(4, dtype=bool)[:, None, None, :, None]
     weights = jnp.where(same, weights, jnp.zeros((), bf16)).reshape(4 * NB, devices * rows)
     cepstra = pl.pallas_call(
@@ -327,6 +337,10 @@
 
 
 def solution(mesh):
-    in_specs = (P(("chan", "sub"), None), P("chan", None), P())
-    out_specs = P(None, None, ("chan", "sub"))
-    return jax.shard_map(shards, mesh=mesh, in_specs=in_specs, out_specs=out_specs, check_vma=False)
+    places = Mesh(mesh.devices.reshape(tuple(PLACES.values())), tuple(PLACES))
+    whole_axes = tuple(PLACES)
+    in_specs = (P(whole_axes, None), P(("x", "zl", "y"), None), P())
+    out_specs = P(None, None, whole_axes)
+    return jax.shard_map(
+        shards, mesh=places, in_specs=in_specs, out_specs=out_specs, check_vma=False
+    )

time: 121 us -> 118 us (0.975)
  waiting for transfers between devices: 72 us -> 69 us
    all_to_all x2, waiting for transfers between devices: 72 us -> 69 us  [the longest x1 48.7 us: shards(): lax.all_to_all(spectrum, ORDER, split_axis=0, concat_axis=0, tiled=True)]
where the time goes in v6:
time: 118 us; the launch traced here: 117 us
  waiting for transfers between devices  69 us (58%)
  Pallas kernels  19.4 us (16%)
  starting transfers between devices  19.2 us (16%)
  local copies, waits for them, and re-layouts  6.19 us (5%)
  other arithmetic  3.52 us (3%)
    all_to_all x1, waiting for transfers between devices, shards(): lax.all_to_all(spectrum, ORDER, split_axis=0, concat_axis=0, tiled=True)  48.7 us
    all_to_all x1, waiting for transfers between devices, shards(): lax.all_to_all(power, ORDER, split_axis=0, concat_axis=0, tiled=True)  20.3 us
    all_to_all x1, starting transfers between devices, shards(): lax.all_to_all(spectrum, ORDER, split_axis=0, concat_axis=0, tiled=True)  12 us
    pallas_call x1, Pallas kernels, shards(): pl.pallas_call(functools.partial(sections_kernel, bins), grid=(HALF // 2,...  9.41 us
    pallas_call x1, Pallas kernels, shards(): pl.pallas_call(functools.partial(spectrum_kernel, devices, chunks, parts)...  7.95 us
    all_to_all x1, starting transfers between devices, shards(): lax.all_to_all(power, ORDER, split_axis=0, concat_axis=0, tiled=True)  7.24 us
    select_n x2, local copies, waits for them, and re-layouts, shards(): jnp.where(same, weights, jnp.zeros((), bf16))  5.84 us
  transfers between devices with their start and end apart: 2, of which 2 were waited for; matrix products, arithmetic and copies ran while one was open for 8% of the time, Pallas kernels for 0%

profile of v6, /device:TPU:1, one launch (start us, length us, event | category | flops | bytes accessed | tf_op | source)
XLA Modules:
  0.0 117.5 jit_solution(1909476027878329125)
XLA Ops:
  0.0 7.9 %spectrum.1 = bf16[128,16,1024]{2,1,0:T(8,128)(2,1)} custom-call(bf16[1024,1024]{1,0:T(8,128)(2,1)} %constant.37.clone.table_hbm, bf16[128,16384]{1,0:T(8,128)(2,1)} %traces_hbm.1), custom_call_target="tpu_custom_call" | custom-call | tf_op jit(solution)/shard_map/spectrum/pallas_call | solution.py:264
  8.0 0.0 copy-start
  8.0 0.0 copy-start.1
  8.0 0.0 copy-start.2
  8.0 0.0 copy-start.3
  8.0 0.0 copy-start.4
  8.0 0.0 copy-start.5
  8.0 12.0 %all-to-all-start = ((bf16[128,16,1024]{2,1,0:T(8,128)(2,1)}), bf16[128,16,1024]{2,1,0:T(8,128)(2,1)}, u32[]{:S(2)}, u32[]{:S(2)}) async-start(bf16[128,16,1024]{2,1,0:T(8,128)(2,1)} %spectrum.1), calls=%async_computation | async-start | bytes 8388608 | tf_op jit(solution)/shard_map/all_to_all | solution.py:281
  20.0 1.1 fusion.1
  21.2 0.1 copy.15
  21.3 48.7 %all-to-all-done.cells_ref = bf16[128,16,1024]{2,1,0:T(8,128)(2,1)} async-done(((bf16[128,16,1024]{2,1,0:T(8,128)(2,1)}), bf16[128,16,1024]{2,1,0:T(8,128)(2,1)}, u32[]{:S(2)}, u32[]{:S(2)}) %all-to-all-start) | async-done | bytes 4194336 | tf_op jit(solution)/shard_map/all_to_all | solution.py:281
  70.0 0.0 copy-done
  70.0 0.0 copy-done.1
  70.0 0.0 copy-done.2
  70.0 0.0 copy-done.3
  70.0 0.0 copy-done.4
  70.0 0.0 copy-done.5
  70.0 9.4 %sections.1 = bf16[128,16,512]{2,1,0:T(8,128)(2,1)} custom-call(bf16[128,16,1024]{2,1,0:T(8,128)(2,1)} %all-to-all-done.cells_ref, bf16[256,256]{1,0:T(8,128)(2,1)S(1)} %copy-done, bf16[256,256]{1,0:T(8,128)(2,1)S(1)} %copy-done.1, bf16[256,256]{1,0:T(8,128)(2,1)S(1)} %copy-done.2, bf16[256,256]{1,0:T(8,128)(2,1)S(1)} %copy-done.3, ...), custom_call_target="tpu_custom_call" | custom-call | tf_op jit(solution)/shard_map/sections/pallas_call | solution.py:287
  79.5 0.0 copy-start.9
  79.5 0.0 copy-start.7
  79.5 0.0 copy-start.8
  79.5 7.2 %all-to-all-start.1 = ((bf16[128,16,512]{2,1,0:T(8,128)(2,1)}), bf16[128,16,512]{2,1,0:T(8,128)(2,1)S(1)}, u32[]{:S(2)}, u32[]{:S(2)}) async-start(bf16[128,16,512]{2,1,0:T(8,128)(2,1)} %sections.1), calls=%async_computation.1 | async-start | bytes 4194304 | tf_op jit(solution)/shard_map/all_to_all | solution.py:322
  86.7 0.0 copy-done.9
  86.7 0.1 fusion.5
  86.8 0.0 copy-done.7
  86.8 0.0 copy-done.8
  86.8 0.1 fusion.4
  86.9 0.1 copy.16
  87.1 2.2 %broadcast_select_fusion = bf16[4,64,128,4,4]{1,0,4,3,2:T(4,128)(2,1)} fusion(pred[4,4]{0,1:T(4,128)(4,1)S(1)} %iota_compare_fusion, bf16[64,128,4]{0,2,1:T(4,128)(2,1)S(1)} %copy.16), kind=kLoop, calls=%fused_computation | loop fusion | flops 524288 | bytes 1114128 | tf_op jit(solution)/shard_map/jit(_where)/select_n | solution.py:327
  89.3 0.0 copy-start.6
  89.3 4.4 %select_n.13 = bf16[256,2048]{0,1:T(8,128)(2,1)} reshape(bf16[4,64,128,4,4]{1,0,4,3,2:T(4,128)(2,1)} %broadcast_select_fusion) | data formatting | bytes 2097152 | tf_op jit(solution)/shard_map/jit(_where)/select_n | solution.py:327
  93.6 1.5 %copy.17.weights_ref = bf16[256,2048]{1,0:T(8,128)(2,1)S(1)} copy(bf16[256,2048]{0,1:T(8,128)(2,1)} %select_n.13) | data formatting | bytes 2097152 | tf_op jit(solution)/shard_map/jit(_where)/select_n | solution.py:327
  95.1 20.3 %all-to-all-done.1.power_ref = bf16[128,16,512]{2,1,0:T(8,128)(2,1)S(1)} async-done(((bf16[128,16,512]{2,1,0:T(8,128)(2,1)}), bf16[128,16,512]{2,1,0:T(8,128)(2,1)S(1)}, u32[]{:S(2)}, u32[]{:S(2)}) %all-to-all-start.1) | async-done | bytes 2097184 | tf_op jit(solution)/shard_map/all_to_all | solution.py:322
  115.4 0.0 copy-done.6
  115.4 2.1 %cepstra.1 = f32[2,8,64,128]{3,2,1,0:T(8,128)} custom-call(bf16[128,16,512]{2,1,0:T(8,128)(2,1)S(1)} %all-to-all-done.1.power_ref, bf16[256,2048]{1,0:T(8,128)(2,1)S(1)} %copy.17.weights_ref, f32[64,64]{1,0:T(8,128)S(1)} %copy-done.6), custom_call_target="tpu_custom_call" | custom-call | tf_op jit(solution)/shard_map/cepstra/pallas_call | solution.py:328
  (3 shorter events, 0.0 us)
Async XLA Ops:
  8.0 62.1 %copy-start = (bf16[256,256]{1,0:T(8,128)(2,1)S(1)}, bf16[256,256]{1,0:T(8,128)(2,1)}, u32[]{:S(2)}) copy-start(bf16[256,256]{1,0:T(8,128)(2,1)} %constant.38.clone.first_ref) | copy-start | bytes 393220
  8.0 62.0 %copy-start.1 = (bf16[256,256]{1,0:T(8,128)(2,1)S(1)}, bf16[256,256]{1,0:T(8,128)(2,1)}, u32[]{:S(2)}) copy-start(bf16[256,256]{1,0:T(8,128)(2,1)} %constant.39.clone.second_ref) | copy-start | bytes 393220
  8.0 62.0 %copy-start.2 = (bf16[256,256]{1,0:T(8,128)(2,1)S(1)}, bf16[256,256]{1,0:T(8,128)(2,1)}, u32[]{:S(2)}) copy-start(bf16[256,256]{1,0:T(8,128)(2,1)} %constant.40.clone.third_ref) | copy-start | bytes 393220
  8.0 62.0 %copy-start.3 = (bf16[256,256]{1,0:T(8,128)(2,1)S(1)}, bf16[256,256]{1,0:T(8,128)(2,1)}, u32[]{:S(2)}) copy-start(bf16[256,256]{1,0:T(8,128)(2,1)} %constant.41.clone.fourth_ref) | copy-start | bytes 393220
  8.0 62.0 %copy-start.4 = (f32[2,128,128]{2,1,0:T(8,128)S(1)}, f32[2,128,128]{2,1,0:T(8,128)}, u32[]{:S(2)}) copy-start(f32[2,128,128]{2,1,0:T(8,128)} %constant.42.clone.forward_ref) | copy-start | bytes 393220
  8.0 62.0 %copy-start.5 = (f32[2,128,128]{2,1,0:T(8,128)S(1)}, f32[2,128,128]{2,1,0:T(8,128)}, u32[]{:S(2)}) copy-start(f32[2,128,128]{2,1,0:T(8,128)} %constant.43.clone.inverse_ref) | copy-start | bytes 393220
  8.0 62.0 %all-to-all-start = ((bf16[128,16,1024]{2,1,0:T(8,128)(2,1)}), bf16[128,16,1024]{2,1,0:T(8,128)(2,1)}, u32[]{:S(2)}, u32[]{:S(2)}) async-start(bf16[128,16,1024]{2,1,0:T(8,128)(2,1)} %spectrum.1), calls=%async_computation | async-start | bytes 8388608 | tf_op jit(solution)/shard_map/all_to_all | solution.py:281
  79.5 7.3 %copy-start.9 = (s32[66]{0:T(128)S(1)}, s32[66]{0:T(128)}, u32[]{:S(2)}) copy-start(s32[66]{0:T(128)} %param.14) | copy-start | bytes 796
  79.5 7.3 %copy-start.7 = (f32[128,4]{0,1:T(4,128)S(1)}, f32[128,4]{0,1:T(4,128)}, u32[]{:S(2)}) copy-start(f32[128,4]{0,1:T(4,128)} %constant.49) | copy-start | bytes 6148
  79.5 7.4 %copy-start.8 = (f32[128,4]{0,1:T(4,128)S(1)}, f32[128,4]{0,1:T(4,128)}, u32[]{:S(2)}) copy-start(f32[128,4]{0,1:T(4,128)} %constant.48) | copy-start | bytes 6148
  79.5 35.9 %all-to-all-start.1 = ((bf16[128,16,512]{2,1,0:T(8,128)(2,1)}), bf16[128,16,512]{2,1,0:T(8,128)(2,1)S(1)}, u32[]{:S(2)}, u32[]{:S(2)}) async-start(bf16[128,16,512]{2,1,0:T(8,128)(2,1)} %sections.1), calls=%async_computation.1 | async-start | bytes 4194304 | tf_op jit(solution)/shard_map/all_to_all | solution.py:322
  89.3 26.1 %copy-start.6 = (f32[64,64]{1,0:T(8,128)S(1)}, f32[64,64]{1,0:T(8,128)}, u32[]{:S(2)}) copy-start(f32[64,64]{1,0:T(8,128)} %constant.45.clone.cosine_ref) | copy-start | bytes 49156

commit v7 on v6

v7 whole, which is shorter than its diff:
```python
import functools
import math

import jax
import jax.numpy as jnp
import ml_dtypes
import numpy as np
from jax import lax
from jax.experimental import pallas as pl
from jax.experimental.pallas import tpu as pltpu
from jax.sharding import Mesh
from jax.sharding import PartitionSpec as P

NCH = 16384
N1 = 128
N2 = 128
FLEN = 1024
NF = 512
NB = 64
FRAMES = 16
BLOCKS = 32
BINS = NF // BLOCKS
SHARES = 4
SHARE = FRAMES // SHARES
ROUND = 8
ROUNDS = -(-(BINS + 1) // ROUND)

energy_floor = 0.05

PLACES = {"x": 4, "zl": 2, "y": 4, "zh": 2, "core": 2}
ORDER = ("zl", "y", "core", "x", "zh")


def listed():
    names = tuple(PLACES)
    devices = np.arange(math.prod(PLACES.values())).reshape(tuple(PLACES.values()))
    return devices.transpose([names.index(name) for name in ORDER]).reshape(-1)


def time_table():
    t = np.arange(FLEN)
    f = np.arange(NF)
    hann = 0.5 - 0.5 * np.cos(2.0 * math.pi * t / FLEN)
    phases = 2.0 * math.pi / FLEN * ((f[:, None] * t[None, :]) % FLEN)
    factor = (0.375 * FLEN) ** -0.5
    table = np.stack([np.cos(phases), -np.sin(phases)], axis=0) * (hann * factor)
    table = table.reshape(2, BLOCKS, BINS, FLEN).transpose(1, 0, 2, 3)
    return table.reshape(2 * NF, FLEN).astype(ml_dtypes.bfloat16)


def dft_parts(length, sign):
    n = np.arange(length)
    phases = 2.0 * math.pi / length * ((n[:, None] * n[None, :]) % length)
    factor = length**-0.5
    return np.cos(phases) * factor, sign * np.sin(phases) * factor


def left_table(length, sign):
    re, im = dft_parts(length, sign)
    return np.block([[re, -im], [im, re]]).astype(ml_dtypes.bfloat16)


def right_table(length, sign):
    re, im = dft_parts(length, sign)
    return np.block([[re, im], [-im, re]]).astype(ml_dtypes.bfloat16)


def twiddle(sign):
    q = np.arange(N2)
    a = np.arange(N1)
    phases = 2.0 * math.pi / NCH * ((q[:, None] * a[None, :]) % NCH)
    return np.stack([np.cos(phases), sign * np.sin(phases)]).astype(np.float32)


def cosine_table():
    j = np.arange(NB)
    phases = math.pi / (2 * NB) * ((j[:, None] * (2 * j[None, :] + 1)) % (4 * NB))
    weight = np.where(j == 0, (1.0 / NB) ** 0.5, (2.0 / NB) ** 0.5)
    return (np.cos(phases) * weight[:, None]).astype(np.float32)


def band_weights(band_edges, freq):
    bounds = band_edges.astype(jnp.float32)
    freq = freq.astype(jnp.float32)[None, :]
    low, middle, high = bounds[:-2, None], bounds[1:-1, None], bounds[2:, None]
    rising = (freq - low) / (middle - low)
    falling = (high - freq) / (high - middle)
    return jnp.maximum(jnp.minimum(rising, falling), 0.0).astype(jnp.bfloat16)


def interval(band_edges, freq):
    below = jnp.sum((band_edges[None, :] <= freq[:, None]).astype(jnp.int32), axis=1)
    return jnp.minimum(below - 1, NB)


def spectrum_kernel(
    chunks,
    parts,
    table_hbm,
    traces_hbm,
    out_hbm,
    table,
    traces,
    out,
    table_sem,
    traces_sem,
    out_sem,
):
    rows = 2 * BINS
    height = 2 * NF // parts
    across = PLACES["x"] // parts
    lanes = SHARE * N1
    cores = PLACES["core"]
    width = SHARE * FLEN

    def table_copy(j):
        at = pl.ds(j * height, height)
        return pltpu.make_async_copy(table_hbm.at[at], table.at[at], table_sem.at[j])

    def traces_copy(i, core):
        at = pl.ds((i * cores + core) * width, width)
        return pltpu.make_async_copy(
            traces_hbm.at[:, at], traces.at[i, core], traces_sem.at[i, core]
        )

    def out_copy(i, j):
        at = (slice(None), slice(None), slice(None), pl.ds(j * across, across), i)
        return pltpu.make_async_copy(out.at[at], out_hbm.at[at], out_sem.at[i, j])

    traces_copy(0, 0).start()
    table_copy(0).start()
    traces_copy(0, 1).start()
    for j in range(1, parts):
        table_copy(j).start()
    for i in range(1, chunks):
        for core in range(cores):
            traces_copy(i, core).start()
    for i in range(chunks):
        for core in range(cores):
            traces_copy(i, core).wait()
        samples = jnp.concatenate(
            [
                traces[i, core, :, m * FLEN : (m + 1) * FLEN]
                for core in range(cores)
                for m in range(SHARE)
            ],
            axis=0,
        )
        for j in range(parts):
            if i == 0:
                table_copy(j).wait()
            part = lax.dot_general(
                table[j * height : (j + 1) * height, :],
                samples,
                (((1,), (1,)), ((), ())),
                preferred_element_type=jnp.float32,
            ).astype(jnp.bfloat16)
            for k in range(height // rows):
                block = j * (height // rows) + k
                x, zl, y = block // 8, block // 4 % 2, block % 4
                for core in range(cores):
                    out[zl, y, core, x, i] = part[
                        k * rows : (k + 1) * rows, core * lanes : (core + 1) * lanes
                    ]
            out_copy(i, j).start()
    for i in range(chunks):
        for j in range(parts):
            out_copy(i, j).wait()


def sections_kernel(
    cells_ref,
    first_ref,
    second_ref,
    third_ref,
    fourth_ref,
    forward_ref,
    inverse_ref,
    mask_ref,
    bands_ref,
    rounds_ref,
    sums_ref,
    rest_hbm,
    cells,
    turned,
    kept,
    back,
    power_rows,
    sums_f32,
    rest,
    rest_sem,
):
    group = 16
    step = 2
    bf16 = jnp.bfloat16
    dot = functools.partial(jnp.dot, preferred_element_type=jnp.float32)
    fwd_cos, fwd_sin = forward_ref[0], forward_ref[1]
    inv_cos, inv_sin = inverse_ref[0], inverse_ref[1]

    def band_sums(r):
        for m in range(2):
            for g in range(0, N2 // group, 2):
                power = jnp.concatenate(
                    [
                        power_rows[m, :, (g + i) * group : (g + i + 1) * group, :].reshape(
                            BINS * group, N1
                        )
                        for i in range(2)
                    ],
                    axis=1,
                )
                sums = dot(bands_ref[r], power)
                for i in range(2):
                    sums_f32[
                        (g + i) * group : (g + i + 1) * group, m * ROUND : (m + 1) * ROUND, :
                    ] = sums[:, i * N1 : (i + 1) * N1].reshape(group, ROUND, N1)

    for m in range(2):
        for g in range(N2 // group):
            for x in range(2):
                block = cells_ref[
                    g * group : (g + 1) * group,
                    x * BINS : (x + 1) * BINS,
                    m * N1 : (m + 1) * N1,
                ]
                block = jnp.swapaxes(block, 0, 1)
                for f in range(BINS):
                    cells[
                        x * N2 + g * group : x * N2 + (g + 1) * group, f * N1 : (f + 1) * N1
                    ] = block[f]
        for f0 in range(0, BINS, step):
            summed = dot(first_ref[...], cells[:, f0 * N1 : (f0 + step) * N1])
            for i in range(step):
                f = f0 + i
                re = summed[:N2, i * N1 : (i + 1) * N1]
                im = summed[N2:, i * N1 : (i + 1) * N1]
                turned[f * N2 : (f + 1) * N2, :N1] = (re * fwd_cos - im * fwd_sin).astype(bf16)
                turned[f * N2 : (f + 1) * N2, N1:] = (re * fwd_sin + im * fwd_cos).astype(bf16)
        for f0 in range(0, BINS, step):
            section = dot(turned[f0 * N2 : (f0 + step) * N2, :], second_ref[...]).astype(bf16)
            for i in range(step):
                f = f0 + i
                mask = mask_ref[f]
                for x in range(2):
                    kept[f * N2 : (f + 1) * N2, x * N1 : (x + 1) * N1] = (
                        section[i * N2 : (i + 1) * N2, x * N1 : (x + 1) * N1] * mask
                    )
        for f0 in range(0, BINS, step):
            summed = dot(kept[f0 * N2 : (f0 + step) * N2, :], third_ref[...])
            for i in range(step):
                f = f0 + i
                re = summed[i * N2 : (i + 1) * N2, :N1]
                im = summed[i * N2 : (i + 1) * N2, N1:]
                back[:N2, f * N1 : (f + 1) * N1] = (re * inv_cos - im * inv_sin).astype(bf16)
                back[N2:, f * N1 : (f + 1) * N1] = (re * inv_sin + im * inv_cos).astype(bf16)
        for f0 in range(0, BINS, step):
            filtered = dot(fourth_ref[...], back[:, f0 * N1 : (f0 + step) * N1])
            filtered = filtered.astype(bf16).astype(jnp.float32)
            power = filtered[:N2] * filtered[:N2] + filtered[N2:] * filtered[N2:]
            for i in range(step):
                power_rows[m, f0 + i] = power[:, i * N1 : (i + 1) * N1].astype(bf16)
    band_sums(0)
    sums_ref[...] = sums_f32[...].astype(bf16)
    at = pl.ds(pl.multiple_of(pl.program_id(0) * 2 * ROUND, 2 * ROUND), 2 * ROUND)
    for r in range(1, ROUNDS):

        @pl.when(rounds_ref[0] > r)
        def _():
            band_sums(r)
            rest[...] = sums_f32[...].astype(bf16)
            copy = pltpu.make_async_copy(rest, rest_hbm.at[r - 1, :, at, :], rest_sem)
            copy.start()
            copy.wait()


def shares_beside(received):
    sizes = tuple(PLACES[name] for name in ORDER)
    received = received.reshape(*sizes, SHARE * ROUND, N1)
    parts = [
        received[:, :, core, :, zh].reshape(BLOCKS * SHARE * ROUND, N1)
        for zh in range(PLACES["zh"])
        for core in range(PLACES["core"])
    ]
    return jnp.concatenate(parts, axis=1)


def band_places(firsts, r):
    band = firsts[:, None] + r * ROUND + jnp.arange(ROUND, dtype=jnp.int32)
    same = band[None, None, :, None, :] == jnp.arange(NB)[None, :, None, None, None]
    frames = jnp.eye(SHARE, dtype=bool)[:, None, None, :, None]
    return (same & frames).astype(jnp.bfloat16).reshape(SHARE * NB, BLOCKS * SHARE * ROUND)


def cepstra_kernel(sums_ref, places_ref, rest_ref, cosine_ref, out_ref):
    energy = jnp.dot(
        places_ref[...], shares_beside(sums_ref[...]), preferred_element_type=jnp.float32
    )
    logs = jnp.log(jnp.maximum(energy + rest_ref[...], energy_floor))
    for m in range(SHARE):
        cepstra = jnp.dot(
            cosine_ref[...],
            logs[m * NB : (m + 1) * NB],
            precision=lax.Precision.HIGHEST,
            preferred_element_type=jnp.float32,
        )
        for share in range(SHARES):
            out_ref[share * SHARE + m] = cepstra[:, share * N1 : (share + 1) * N1]


def whole(shape):
    return pl.BlockSpec(shape, lambda i: (0,) * len(shape))


VMEM_LIMIT = 48 * 1024 * 1024
VMEM_WHOLE = 60 * 1024 * 1024


def shards(traces, fan_mask, band_edges):
    devices = math.prod(lax.axis_size(name) for name in PLACES)
    sizes = tuple(PLACES[name] for name in ORDER)
    rows = 2 * BINS
    lanes = SHARE * N1
    order = np.concatenate([listed(), N2 + listed()])
    bf16 = jnp.bfloat16
    params = pltpu.CompilerParams(vmem_limit_bytes=VMEM_LIMIT)

    chunks, parts = PLACES["zh"], 2
    spectrum = pl.pallas_call(
        functools.partial(spectrum_kernel, chunks, parts),
        in_specs=[pl.BlockSpec(memory_space=pltpu.HBM)] * 2,
        out_specs=pl.BlockSpec(memory_space=pltpu.HBM),
        out_shape=jax.ShapeDtypeStruct((*sizes, rows, lanes), bf16),
        scratch_shapes=[
            pltpu.VMEM((2 * NF, FLEN), bf16),
            pltpu.VMEM((chunks, PLACES["core"], N1, SHARE * FLEN), bf16),
            pltpu.VMEM((*sizes, rows, lanes), bf16),
            pltpu.SemaphoreType.DMA((parts,)),
            pltpu.SemaphoreType.DMA((chunks, PLACES["core"])),
            pltpu.SemaphoreType.DMA((chunks, parts)),
        ],
        compiler_params=pltpu.CompilerParams(vmem_limit_bytes=VMEM_WHOLE),
        name="spectrum",
    )(jnp.asarray(time_table()), traces)
    spectrum = spectrum.reshape(devices, rows, lanes)

    cells = lax.all_to_all(spectrum, ORDER, split_axis=0, concat_axis=0, tiled=True)

    mask = jnp.transpose(fan_mask.reshape(BINS, N1, N2), (0, 2, 1))
    mask = (mask > 0).astype(bf16)

    blocks = np.arange(BLOCKS, dtype=np.int32).reshape(
        PLACES["x"], PLACES["zl"], PLACES["y"]
    )
    starts = jnp.asarray(blocks.transpose(1, 2, 0).reshape(-1) * BINS)
    firsts = interval(band_edges, starts) - 1
    touched = interval(band_edges, starts + BINS - 1) + 1 - firsts
    rounds = (jnp.max(touched) + ROUND - 1) // ROUND
    own = lax.axis_index(("x", "zl", "y"))
    weights = band_weights(band_edges, own * BINS + jnp.arange(BINS, dtype=jnp.int32))
    own_first = interval(band_edges, jnp.reshape(own * BINS, (1,))) - 1
    sent = own_first + jnp.arange(ROUNDS * ROUND, dtype=jnp.int32)
    chosen = sent[:, None] == jnp.arange(NB, dtype=jnp.int32)[None, :]
    weights = jnp.max(
        jnp.where(chosen[:, :, None], weights[None], jnp.zeros((), bf16)), axis=1
    )
    weights = weights.reshape(ROUNDS, 1, ROUND, BINS, 1)
    same = jnp.eye(16, dtype=bool)[None, :, None, None, :]
    bands = jnp.where(same, weights, jnp.zeros((), bf16)).reshape(
        ROUNDS, 16 * ROUND, BINS * 16
    )

    sums, rest = pl.pallas_call(
        sections_kernel,
        grid=(SHARE // 2,),
        in_specs=[
            pl.BlockSpec((N2, rows, 2 * N1), lambda i: (0, 0, i)),
            whole((2 * N2, 2 * N2)),
            whole((2 * N1, 2 * N1)),
            whole((2 * N1, 2 * N1)),
            whole((2 * N2, 2 * N2)),
            whole((2, N2, N1)),
            whole((2, N2, N1)),
            whole((BINS, N2, N1)),
            whole((ROUNDS, 16 * ROUND, BINS * 16)),
            pl.BlockSpec(memory_space=pltpu.SMEM),
        ],
        out_specs=[
            pl.BlockSpec((N2, 2 * ROUND, N1), lambda i: (0, i, 0)),
            pl.BlockSpec(memory_space=pltpu.HBM),
        ],
        out_shape=[
            jax.ShapeDtypeStruct((N2, SHARE * ROUND, N1), bf16),
            jax.ShapeDtypeStruct((ROUNDS - 1, N2, SHARE * ROUND, N1), bf16),
        ],
        scratch_shapes=[
            pltpu.VMEM((2 * N2, BINS * N1), bf16),
            pltpu.VMEM((BINS * N2, 2 * N1), bf16),
            pltpu.VMEM((BINS * N2, 2 * N1), bf16),
            pltpu.VMEM((2 * N2, BINS * N1), bf16),
            pltpu.VMEM((2, BINS, N2, N1), bf16),
            pltpu.VMEM((N2, 2 * ROUND, N1), jnp.float32),
            pltpu.VMEM((N2, 2 * ROUND, N1), bf16),
            pltpu.SemaphoreType.DMA,
        ],
        compiler_params=params,
        name="sections",
    )(
        cells,
        jnp.asarray(left_table(N2, -1.0)[:, order]),
        jnp.asarray(right_table(N1, -1.0)),
        jnp.asarray(right_table(N1, 1.0)),
        jnp.asarray(left_table(N2, 1.0)[order]),
        jnp.asarray(twiddle(-1.0)),
        jnp.asarray(twiddle(1.0)),
        mask,
        bands,
        jnp.reshape(rounds, (1,)),
    )

    def send(sums):
        return lax.all_to_all(sums, ORDER, split_axis=0, concat_axis=0, tiled=True)

    def further_round(r, energy):
        received = send(lax.dynamic_index_in_dim(rest, r - 1, 0, keepdims=False))
        return energy + jnp.dot(
            band_places(firsts, r), shares_beside(received), preferred_element_type=jnp.float32
        )

    further = lax.fori_loop(
        1, rounds, further_round, jnp.zeros((SHARE * NB, SHARES * N1), jnp.float32)
    )
    return pl.pallas_call(
        cepstra_kernel,
        in_specs=[pl.BlockSpec(memory_space=pltpu.VMEM)] * 4,
        out_specs=pl.BlockSpec(memory_space=pltpu.VMEM),
        out_shape=jax.ShapeDtypeStruct((FRAMES, NB, N1), jnp.float32),
        compiler_params=params,
        name="cepstra",
    )(send(sums), band_places(firsts, 0), further, jnp.asarray(cosine_table()))


def solution(mesh):
    places = Mesh(mesh.devices.reshape(tuple(PLACES.values())), tuple(PLACES))
    whole_axes = tuple(PLACES)
    in_specs = (P(whole_axes, None), P(("x", "zl", "y"), None), P())
    out_specs = P(None, None, whole_axes)
    return jax.shard_map(
        shards, mesh=places, in_specs=in_specs, out_specs=out_specs, check_vma=False
    )
```

time: 118 us -> 107 us (0.907)
  waiting for transfers between devices: 69 us -> 59.6 us
  local copies, waits for them, and re-layouts: 6.19 us -> 3.84 us
  between operations: 0.17 us -> 1.65 us
    select_n x2 -> x0, local copies, waits for them, and re-layouts: 5.84 us -> none  [shards(): jnp.where(same, weights, jnp.zeros((), bf16))]
    all_to_all x1, waiting for transfers between devices: 48.7 us -> 43.6 us  [shards(): lax.all_to_all(spectrum, ORDER, split_axis=0, concat_axis=0, tiled=True)]
    all_to_all x1, waiting for transfers between devices: 20.3 us -> 16 us  [send(): return lax.all_to_all(sums, ORDER, split_axis=0, concat_axis=0, tiled=True)]
    broadcast_in_dim x0 -> x5, local copies, waits for them, and re-layouts: none -> 2.52 us  [the longest x4 2.47 us: shards(): jnp.where(same, weights, jnp.zeros((), bf16))]
    select_n x1, other arithmetic: 2.18 us -> 0.02 us  [shards(): jnp.where(same, weights, jnp.zeros((), bf16))]
  transfers between devices with their start and end apart: 2 -> 2, of which waited for: 2 -> 2; matrix products, arithmetic and copies ran while one was open for 8% -> 6% of each run, Pallas kernels for 0% -> 0%
where the time goes in v7:
time: 107 us
  waiting for transfers between devices  59.6 us (56%)
  Pallas kernels  19.6 us (18%)
  starting transfers between devices  19.2 us (18%)
  local copies, waits for them, and re-layouts  3.84 us (4%)
  other arithmetic  2.82 us (3%)
  between operations  1.65 us (2%)
    all_to_all x1, waiting for transfers between devices, shards(): lax.all_to_all(spectrum, ORDER, split_axis=0, concat_axis=0, tiled=True)  43.6 us
    all_to_all x1, waiting for transfers between devices, send(): return lax.all_to_all(sums, ORDER, split_axis=0, concat_axis=0, tiled=True)  16 us
    all_to_all x1, starting transfers between devices, shards(): lax.all_to_all(spectrum, ORDER, split_axis=0, concat_axis=0, tiled=True)  12 us
    pallas_call x1, Pallas kernels, shards(): pl.pallas_call(sections_kernel, grid=(SHARE // 2,), in_specs=[pl.BlockSpe...  9.79 us
    pallas_call x1, Pallas kernels, shards(): pl.pallas_call(functools.partial(spectrum_kernel, chunks, parts), in_spec...  8.01 us
    all_to_all x1, starting transfers between devices, send(): return lax.all_to_all(sums, ORDER, split_axis=0, concat_axis=0, tiled=True)  7.24 us
    broadcast_in_dim x4, local copies, waits for them, and re-layouts, shards(): jnp.where(same, weights, jnp.zeros((), bf16))  2.47 us
  transfers between devices with their start and end apart: 2, of which 2 were waited for; matrix products, arithmetic and copies ran while one was open for 6% of the time, Pallas kernels for 0%

profile of v7, /device:TPU:1, one launch (start us, length us, event | category | flops | bytes accessed | tf_op | source)
XLA Modules:
  0.0 106.9 jit_solution(7379991389339818870)
XLA Ops:
  0.0 8.0 %spectrum.1 = bf16[2,4,2,4,2,32,512]{6,5,4,3,2,1,0:T(8,128)(2,1)} custom-call(bf16[1024,1024]{1,0:T(8,128)(2,1)} %constant.123.clone.table_hbm, bf16[128,16384]{1,0:T(8,128)(2,1)} %traces_hbm.1), custom_call_target="tpu_custom_call" | custom-call | tf_op jit(solution)/shard_map/spectrum/pallas_call | solution.py:328
  8.0 0.0 copy-start.8
  8.0 0.0 copy-start.9
  8.0 0.0 copy-start.10
  8.1 0.0 copy-start.7
  8.1 12.0 %all-to-all-start.1 = ((bf16[128,32,512]{2,1,0:T(8,128)(2,1)}), bf16[128,32,512]{2,1,0:T(8,128)(2,1)}, u32[]{:S(2)}, u32[]{:S(2)}) async-start(bf16[128,32,512]{2,1,0:T(8,128)(2,1)} %bitcast.39), calls=%async_computation.1 | async-start | bytes 8388608 | tf_op jit(solution)/shard_map/all_to_all | solution.py:346
  20.1 0.0 copy-done.8
  20.1 0.0 copy-done.9
  20.1 0.0 copy-done.10
  20.1 0.2 convert_reduce_fusion
  20.3 0.6 minimum_add_fusion
  21.6 0.0 copy-done.7
  21.6 0.1 fusion.8
  21.7 0.1 copy.17
  21.8 0.3 copy.15
  22.1 0.6 fusion.12
  23.4 0.1 fusion.11
  23.5 0.1 iota_compare_fusion.3
  23.6 0.1 maximum_convert_fusion
  23.6 0.1 select_reduce_fusion
  23.8 0.0 copy-start
  23.8 0.0 copy-start.1
  23.8 0.0 copy-start.2
  23.8 0.0 copy-start.3
  23.8 0.0 copy-start.4
  23.8 0.0 copy-start.5
  23.8 0.4 broadcast_in_dim.82
  24.3 1.5 %broadcast_in_dim.83 = bf16[3,128,256]{2,1,0:T(8,128)(2,1)S(1)} reshape(bf16[3,16,8,16,16]{4,3,2,1,0:T(8,128)(2,1)S(1)} %broadcast_in_dim.82) | data formatting | bytes 393216 | tf_op jit(solution)/shard_map/jit(_where)/broadcast_in_dim | solution.py:368
  25.8 0.1 broadcast_in_dim.55
  25.9 0.5 broadcast_in_dim.56
  26.4 43.6 %all-to-all-done.1.cells_ref = bf16[128,32,512]{2,1,0:T(8,128)(2,1)} async-done(((bf16[128,32,512]{2,1,0:T(8,128)(2,1)}), bf16[128,32,512]{2,1,0:T(8,128)(2,1)}, u32[]{:S(2)}, u32[]{:S(2)}) %all-to-all-start.1) | async-done | bytes 4194336 | tf_op jit(solution)/shard_map/all_to_all | solution.py:346
  70.0 0.0 copy-done
  70.0 0.0 copy-done.1
  70.0 0.0 copy-done.2
  70.1 0.0 copy-done.3
  70.1 0.0 copy-done.4
  70.1 9.8 %sections.1 = (bf16[128,32,128]{2,1,0:T(8,128)(2,1)}, bf16[2,128,32,128]{3,2,1,0:T(8,128)(2,1)}) custom-call(bf16[128,32,512]{2,1,0:T(8,128)(2,1)} %all-to-all-done.1.cells_ref, bf16[256,256]{1,0:T(8,128)(2,1)S(1)} %copy-done, bf16[256,256]{1,0:T(8,128)(2,1)S(1)} %copy-done.1, bf16[256,256]{1,0:T(8,128)(2,1)S(1)} %copy-done.2, ...), custom_call_target="tpu_custom_call" | custom-call | tf_op jit(solution)/shard_map/sections/pallas_call | solution.py:372
  79.9 0.1 broadcast_in_dim.85
  79.9 0.2 while.14
  80.1 7.2 %all-to-all-start.2 = ((bf16[128,32,128]{2,1,0:T(8,128)(2,1)}), bf16[128,32,128]{2,1,0:T(8,128)(2,1)S(1)}, u32[]{:S(2)}, u32[]{:S(2)}) async-start(bf16[128,32,128]{2,1,0:T(8,128)(2,1)} %get-tuple-element.115), calls=%async_computation.2 | async-start | bytes 2097152 | tf_op jit(solution)/shard_map/all_to_all | solution.py:421
  87.4 0.0 copy-start.6
  87.4 0.1 iota_add_fusion.1
  87.5 0.1 iota_compare_fusion.2
  87.6 0.7 and_convert_fusion
  88.3 0.7 reshape.258
  88.9 0.2 copy.16.places_ref
  89.1 16.0 %all-to-all-done.2.sums_ref = bf16[128,32,128]{2,1,0:T(8,128)(2,1)S(1)} async-done(((bf16[128,32,128]{2,1,0:T(8,128)(2,1)}), bf16[128,32,128]{2,1,0:T(8,128)(2,1)S(1)}, u32[]{:S(2)}, u32[]{:S(2)}) %all-to-all-start.2) | async-done | bytes 1048608 | tf_op jit(solution)/shard_map/all_to_all | solution.py:421
  105.1 1.8 %cepstra.1 = f32[16,64,128]{2,1,0:T(8,128)} custom-call(bf16[128,32,128]{2,1,0:T(8,128)(2,1)S(1)} %all-to-all-done.2.sums_ref, bf16[256,1024]{1,0:T(8,128)(2,1)S(1)} %copy.16.places_ref, f32[256,512]{1,0:T(8,128)S(1)} %get-tuple-element.117.rest_ref, f32[64,64]{1,0:T(8,128)S(1)} %copy-done.6), custom_call_target="tpu_custom_call" | custom-call | tf_op jit(solution)/shard_map/cepstra/pallas_call | solution.py:432
  (7 shorter events, 0.1 us)
Async XLA Ops:
  8.0 12.0 %copy-start.8 = (s32[66]{0:T(128)S(1)}, s32[66]{0:T(128)}, u32[]{:S(2)}) copy-start(s32[66]{0:T(128)} %param.16) | copy-start | bytes 796
  8.0 12.0 %copy-start.9 = (s32[32]{0:T(128)S(1)}, s32[32]{0:T(128)}, u32[]{:S(2)}) copy-start(s32[32]{0:T(128)} %constant.124.clone) | copy-start | bytes 388
  8.0 12.0 %copy-start.10 = (s32[32]{0:T(128)S(1)}, s32[32]{0:T(128)}, u32[]{:S(2)}) copy-start(s32[32]{0:T(128)} %constant.133) | copy-start | bytes 388
  8.1 13.5 %copy-start.7 = (s32[16,16384]{1,0:T(8,128)S(1)}, s32[16,16384]{1,0:T(8,128)}, u32[]{:S(2)}) copy-start(s32[16,16384]{1,0:T(8,128)} %param.15) | copy-start | bytes 3145732
  8.1 62.0 %all-to-all-start.1 = ((bf16[128,32,512]{2,1,0:T(8,128)(2,1)}), bf16[128,32,512]{2,1,0:T(8,128)(2,1)}, u32[]{:S(2)}, u32[]{:S(2)}) async-start(bf16[128,32,512]{2,1,0:T(8,128)(2,1)} %bitcast.39), calls=%async_computation.1 | async-start | bytes 8388608 | tf_op jit(solution)/shard_map/all_to_all | solution.py:346
  23.8 46.3 %copy-start = (bf16[256,256]{1,0:T(8,128)(2,1)S(1)}, bf16[256,256]{1,0:T(8,128)(2,1)}, u32[]{:S(2)}) copy-start(bf16[256,256]{1,0:T(8,128)(2,1)} %constant.125.clone.first_ref) | copy-start | bytes 393220
  23.8 46.3 %copy-start.1 = (bf16[256,256]{1,0:T(8,128)(2,1)S(1)}, bf16[256,256]{1,0:T(8,128)(2,1)}, u32[]{:S(2)}) copy-start(bf16[256,256]{1,0:T(8,128)(2,1)} %constant.126.clone.second_ref) | copy-start | bytes 393220
  23.8 46.3 %copy-start.2 = (bf16[256,256]{1,0:T(8,128)(2,1)S(1)}, bf16[256,256]{1,0:T(8,128)(2,1)}, u32[]{:S(2)}) copy-start(bf16[256,256]{1,0:T(8,128)(2,1)} %constant.127.clone.third_ref) | copy-start | bytes 393220
  23.8 46.2 %copy-start.3 = (bf16[256,256]{1,0:T(8,128)(2,1)S(1)}, bf16[256,256]{1,0:T(8,128)(2,1)}, u32[]{:S(2)}) copy-start(bf16[256,256]{1,0:T(8,128)(2,1)} %constant.128.clone.fourth_ref) | copy-start | bytes 393220
  23.8 46.2 %copy-start.4 = (f32[2,128,128]{2,1,0:T(8,128)S(1)}, f32[2,128,128]{2,1,0:T(8,128)}, u32[]{:S(2)}) copy-start(f32[2,128,128]{2,1,0:T(8,128)} %constant.129.clone.forward_ref) | copy-start | bytes 393220
  23.8 46.2 %copy-start.5 = (f32[2,128,128]{2,1,0:T(8,128)S(1)}, f32[2,128,128]{2,1,0:T(8,128)}, u32[]{:S(2)}) copy-start(f32[2,128,128]{2,1,0:T(8,128)} %constant.130.clone.inverse_ref) | copy-start | bytes 393220
  80.1 25.0 %all-to-all-start.2 = ((bf16[128,32,128]{2,1,0:T(8,128)(2,1)}), bf16[128,32,128]{2,1,0:T(8,128)(2,1)S(1)}, u32[]{:S(2)}, u32[]{:S(2)}) async-start(bf16[128,32,128]{2,1,0:T(8,128)(2,1)} %get-tuple-element.115), calls=%async_computation.2 | async-start | bytes 2097152 | tf_op jit(solution)/shard_map/all_to_all | solution.py:421
  87.4 17.7 %copy-start.6 = (f32[64,64]{1,0:T(8,128)S(1)}, f32[64,64]{1,0:T(8,128)}, u32[]{:S(2)}) copy-start(f32[64,64]{1,0:T(8,128)} %constant.131.clone.cosine_ref) | copy-start | bytes 49156

commit v8 on v7

--- a/solution.py
+++ b/solution.py
@@ -296,15 +296,22 @@
         places_ref[...], shares_beside(sums_ref[...]), preferred_element_type=jnp.float32
     )
     logs = jnp.log(jnp.maximum(energy + rest_ref[...], energy_floor))
+    width = SHARES * N1
+    logs = jnp.concatenate([logs[m * NB : (m + 1) * NB] for m in range(SHARE)], axis=1)
+    bf16 = jnp.bfloat16
+    dot = functools.partial(jnp.dot, preferred_element_type=jnp.float32)
+    high = logs.astype(bf16)
+    low = (logs - high.astype(jnp.float32)).astype(bf16)
+    cosine = cosine_ref[...]
+    cosine_high = cosine.astype(bf16)
+    cosine_low = (cosine - cosine_high.astype(jnp.float32)).astype(bf16)
+    left = jnp.concatenate([cosine_high, cosine_low, cosine_high], axis=1)
+    right = jnp.concatenate([high, high, low], axis=0)
+    cepstra = dot(left, right)
     for m in range(SHARE):
-        cepstra = jnp.dot(
-            cosine_ref[...],
-            logs[m * NB : (m + 1) * NB],
-            precision=lax.Precision.HIGHEST,
-            preferred_element_type=jnp.float32,
-        )
         for share in range(SHARES):
-            out_ref[share * SHARE + m] = cepstra[:, share * N1 : (share + 1) * N1]
+            at = m * width + share * N1
+            out_ref[share * SHARE + m] = cepstra[:, at : at + N1]
 
 
 def whole(shape):

time: 107 us -> 107 us (level)
  no operation moved by 1% of the time
where the time goes in v8:
time: 107 us
  waiting for transfers between devices  59.6 us (56%)
  Pallas kernels  19.3 us (18%)
  starting transfers between devices  19.2 us (18%)
  local copies, waits for them, and re-layouts  3.84 us (4%)
  other arithmetic  2.82 us (3%)
  between operations  1.65 us (2%)
    all_to_all x1, waiting for transfers between devices, shards(): lax.all_to_all(spectrum, ORDER, split_axis=0, concat_axis=0, tiled=True)  43.6 us
    all_to_all x1, waiting for transfers between devices, send(): return lax.all_to_all(sums, ORDER, split_axis=0, concat_axis=0, tiled=True)  16 us
    all_to_all x1, starting transfers between devices, shards(): lax.all_to_all(spectrum, ORDER, split_axis=0, concat_axis=0, tiled=True)  12 us
    pallas_call x1, Pallas kernels, shards(): pl.pallas_call(sections_kernel, grid=(SHARE // 2,), in_specs=[pl.BlockSpe...  9.79 us
    pallas_call x1, Pallas kernels, shards(): pl.pallas_call(functools.partial(spectrum_kernel, chunks, parts), in_spec...  8.01 us
    all_to_all x1, starting transfers between devices, send(): return lax.all_to_all(sums, ORDER, split_axis=0, concat_axis=0, tiled=True)  7.24 us
    broadcast_in_dim x4, local copies, waits for them, and re-layouts, shards(): jnp.where(same, weights, jnp.zeros((), bf16))  2.47 us
  transfers between devices with their start and end apart: 2, of which 2 were waited for; matrix products, arithmetic and copies ran while one was open for 6% of the time, Pallas kernels for 0%

profile of v8, /device:TPU:1, one launch (start us, length us, event | category | flops | bytes accessed | tf_op | source)
XLA Modules:
  0.0 106.6 jit_solution(5883955730437260322)
XLA Ops:
  0.0 8.0 %spectrum.1 = bf16[2,4,2,4,2,32,512]{6,5,4,3,2,1,0:T(8,128)(2,1)} custom-call(bf16[1024,1024]{1,0:T(8,128)(2,1)} %constant.123.clone.table_hbm, bf16[128,16384]{1,0:T(8,128)(2,1)} %traces_hbm.1), custom_call_target="tpu_custom_call" | custom-call | tf_op jit(solution)/shard_map/spectrum/pallas_call | solution.py:335
  8.0 0.0 copy-start.8
  8.0 0.0 copy-start.9
  8.0 0.0 copy-start.10
  8.1 0.0 copy-start.7
  8.1 12.0 %all-to-all-start.1 = ((bf16[128,32,512]{2,1,0:T(8,128)(2,1)}), bf16[128,32,512]{2,1,0:T(8,128)(2,1)}, u32[]{:S(2)}, u32[]{:S(2)}) async-start(bf16[128,32,512]{2,1,0:T(8,128)(2,1)} %bitcast.39), calls=%async_computation.1 | async-start | bytes 8388608 | tf_op jit(solution)/shard_map/all_to_all | solution.py:353
  20.1 0.0 copy-done.8
  20.1 0.0 copy-done.9
  20.1 0.0 copy-done.10
  20.1 0.2 convert_reduce_fusion
  20.3 0.6 minimum_add_fusion
  21.6 0.0 copy-done.7
  21.6 0.1 fusion.8
  21.7 0.1 copy.17
  21.8 0.3 copy.15
  22.1 0.6 fusion.12
  23.4 0.1 fusion.11
  23.5 0.1 iota_compare_fusion.3
  23.6 0.1 maximum_convert_fusion
  23.6 0.1 select_reduce_fusion
  23.8 0.0 copy-start
  23.8 0.0 copy-start.1
  23.8 0.0 copy-start.2
  23.8 0.0 copy-start.3
  23.8 0.0 copy-start.4
  23.8 0.0 copy-start.5
  23.8 0.4 broadcast_in_dim.82
  24.3 1.5 %broadcast_in_dim.83 = bf16[3,128,256]{2,1,0:T(8,128)(2,1)S(1)} reshape(bf16[3,16,8,16,16]{4,3,2,1,0:T(8,128)(2,1)S(1)} %broadcast_in_dim.82) | data formatting | bytes 393216 | tf_op jit(solution)/shard_map/jit(_where)/broadcast_in_dim | solution.py:375
  25.8 0.1 broadcast_in_dim.55
  25.9 0.5 broadcast_in_dim.56
  26.4 43.6 %all-to-all-done.1.cells_ref = bf16[128,32,512]{2,1,0:T(8,128)(2,1)} async-done(((bf16[128,32,512]{2,1,0:T(8,128)(2,1)}), bf16[128,32,512]{2,1,0:T(8,128)(2,1)}, u32[]{:S(2)}, u32[]{:S(2)}) %all-to-all-start.1) | async-done | bytes 4194336 | tf_op jit(solution)/shard_map/all_to_all | solution.py:353
  70.0 0.0 copy-done
  70.0 0.0 copy-done.1
  70.0 0.0 copy-done.2
  70.1 0.0 copy-done.3
  70.1 0.0 copy-done.4
  70.1 9.8 %sections.1 = (bf16[128,32,128]{2,1,0:T(8,128)(2,1)}, bf16[2,128,32,128]{3,2,1,0:T(8,128)(2,1)}) custom-call(bf16[128,32,512]{2,1,0:T(8,128)(2,1)} %all-to-all-done.1.cells_ref, bf16[256,256]{1,0:T(8,128)(2,1)S(1)} %copy-done, bf16[256,256]{1,0:T(8,128)(2,1)S(1)} %copy-done.1, bf16[256,256]{1,0:T(8,128)(2,1)S(1)} %copy-done.2, ...), custom_call_target="tpu_custom_call" | custom-call | tf_op jit(solution)/shard_map/sections/pallas_call | solution.py:379
  79.9 0.1 broadcast_in_dim.85
  79.9 0.2 while.14
  80.1 7.2 %all-to-all-start.2 = ((bf16[128,32,128]{2,1,0:T(8,128)(2,1)}), bf16[128,32,128]{2,1,0:T(8,128)(2,1)S(1)}, u32[]{:S(2)}, u32[]{:S(2)}) async-start(bf16[128,32,128]{2,1,0:T(8,128)(2,1)} %get-tuple-element.115), calls=%async_computation.2 | async-start | bytes 2097152 | tf_op jit(solution)/shard_map/all_to_all | solution.py:428
  87.4 0.0 copy-start.6
  87.4 0.1 iota_add_fusion.1
  87.5 0.1 iota_compare_fusion.2
  87.6 0.7 and_convert_fusion
  88.3 0.7 reshape.258
  88.9 0.2 copy.16.places_ref
  89.1 16.0 %all-to-all-done.2.sums_ref = bf16[128,32,128]{2,1,0:T(8,128)(2,1)S(1)} async-done(((bf16[128,32,128]{2,1,0:T(8,128)(2,1)}), bf16[128,32,128]{2,1,0:T(8,128)(2,1)S(1)}, u32[]{:S(2)}, u32[]{:S(2)}) %all-to-all-start.2) | async-done | bytes 1048608 | tf_op jit(solution)/shard_map/all_to_all | solution.py:428
  105.1 1.5 %cepstra.1 = f32[16,64,128]{2,1,0:T(8,128)} custom-call(bf16[128,32,128]{2,1,0:T(8,128)(2,1)S(1)} %all-to-all-done.2.sums_ref, bf16[256,1024]{1,0:T(8,128)(2,1)S(1)} %copy.16.places_ref, f32[256,512]{1,0:T(8,128)S(1)} %get-tuple-element.117.rest_ref, f32[64,64]{1,0:T(8,128)S(1)} %copy-done.6), custom_call_target="tpu_custom_call" | custom-call | tf_op jit(solution)/shard_map/cepstra/pallas_call | solution.py:439
  (7 shorter events, 0.1 us)
Async XLA Ops:
  8.0 12.0 %copy-start.8 = (s32[66]{0:T(128)S(1)}, s32[66]{0:T(128)}, u32[]{:S(2)}) copy-start(s32[66]{0:T(128)} %param.16) | copy-start | bytes 796
  8.0 12.0 %copy-start.9 = (s32[32]{0:T(128)S(1)}, s32[32]{0:T(128)}, u32[]{:S(2)}) copy-start(s32[32]{0:T(128)} %constant.124.clone) | copy-start | bytes 388
  8.0 12.0 %copy-start.10 = (s32[32]{0:T(128)S(1)}, s32[32]{0:T(128)}, u32[]{:S(2)}) copy-start(s32[32]{0:T(128)} %constant.133) | copy-start | bytes 388
  8.1 13.5 %copy-start.7 = (s32[16,16384]{1,0:T(8,128)S(1)}, s32[16,16384]{1,0:T(8,128)}, u32[]{:S(2)}) copy-start(s32[16,16384]{1,0:T(8,128)} %param.15) | copy-start | bytes 3145732
  8.1 62.0 %all-to-all-start.1 = ((bf16[128,32,512]{2,1,0:T(8,128)(2,1)}), bf16[128,32,512]{2,1,0:T(8,128)(2,1)}, u32[]{:S(2)}, u32[]{:S(2)}) async-start(bf16[128,32,512]{2,1,0:T(8,128)(2,1)} %bitcast.39), calls=%async_computation.1 | async-start | bytes 8388608 | tf_op jit(solution)/shard_map/all_to_all | solution.py:353
  23.8 46.3 %copy-start = (bf16[256,256]{1,0:T(8,128)(2,1)S(1)}, bf16[256,256]{1,0:T(8,128)(2,1)}, u32[]{:S(2)}) copy-start(bf16[256,256]{1,0:T(8,128)(2,1)} %constant.125.clone.first_ref) | copy-start | bytes 393220
  23.8 46.3 %copy-start.1 = (bf16[256,256]{1,0:T(8,128)(2,1)S(1)}, bf16[256,256]{1,0:T(8,128)(2,1)}, u32[]{:S(2)}) copy-start(bf16[256,256]{1,0:T(8,128)(2,1)} %constant.126.clone.second_ref) | copy-start | bytes 393220
  23.8 46.3 %copy-start.2 = (bf16[256,256]{1,0:T(8,128)(2,1)S(1)}, bf16[256,256]{1,0:T(8,128)(2,1)}, u32[]{:S(2)}) copy-start(bf16[256,256]{1,0:T(8,128)(2,1)} %constant.127.clone.third_ref) | copy-start | bytes 393220
  23.8 46.2 %copy-start.3 = (bf16[256,256]{1,0:T(8,128)(2,1)S(1)}, bf16[256,256]{1,0:T(8,128)(2,1)}, u32[]{:S(2)}) copy-start(bf16[256,256]{1,0:T(8,128)(2,1)} %constant.128.clone.fourth_ref) | copy-start | bytes 393220
  23.8 46.2 %copy-start.4 = (f32[2,128,128]{2,1,0:T(8,128)S(1)}, f32[2,128,128]{2,1,0:T(8,128)}, u32[]{:S(2)}) copy-start(f32[2,128,128]{2,1,0:T(8,128)} %constant.129.clone.forward_ref) | copy-start | bytes 393220
  23.8 46.2 %copy-start.5 = (f32[2,128,128]{2,1,0:T(8,128)S(1)}, f32[2,128,128]{2,1,0:T(8,128)}, u32[]{:S(2)}) copy-start(f32[2,128,128]{2,1,0:T(8,128)} %constant.130.clone.inverse_ref) | copy-start | bytes 393220
  80.1 25.0 %all-to-all-start.2 = ((bf16[128,32,128]{2,1,0:T(8,128)(2,1)}), bf16[128,32,128]{2,1,0:T(8,128)(2,1)S(1)}, u32[]{:S(2)}, u32[]{:S(2)}) async-start(bf16[128,32,128]{2,1,0:T(8,128)(2,1)} %get-tuple-element.115), calls=%async_computation.2 | async-start | bytes 2097152 | tf_op jit(solution)/shard_map/all_to_all | solution.py:428
  87.4 17.7 %copy-start.6 = (f32[64,64]{1,0:T(8,128)S(1)}, f32[64,64]{1,0:T(8,128)}, u32[]{:S(2)}) copy-start(f32[64,64]{1,0:T(8,128)} %constant.131.clone.cosine_ref) | copy-start | bytes 49156

commit v9 on v8

--- a/solution.py
+++ b/solution.py
@@ -260,8 +260,8 @@
             for i in range(step):
                 power_rows[m, f0 + i] = power[:, i * N1 : (i + 1) * N1].astype(bf16)
     band_sums(0)
-    sums_ref[...] = sums_f32[...].astype(bf16)
     at = pl.ds(pl.multiple_of(pl.program_id(0) * 2 * ROUND, 2 * ROUND), 2 * ROUND)
+    sums_ref[:, at, :] = sums_f32[...].astype(bf16)
     for r in range(1, ROUNDS):
 
         @pl.when(rounds_ref[0] > r)
@@ -392,7 +392,7 @@
             pl.BlockSpec(memory_space=pltpu.SMEM),
         ],
         out_specs=[
-            pl.BlockSpec((N2, 2 * ROUND, N1), lambda i: (0, i, 0)),
+            pl.BlockSpec(memory_space=pltpu.VMEM),
             pl.BlockSpec(memory_space=pltpu.HBM),
         ],
         out_shape=[

time: 107 us -> 107 us (level)
  no operation moved by 1% of the time
where the time goes in v9:
time: 107 us
  waiting for transfers between devices  59.6 us (56%)
  Pallas kernels  19.4 us (18%)
  starting transfers between devices  19.2 us (18%)
  local copies, waits for them, and re-layouts  3.84 us (4%)
  other arithmetic  2.82 us (3%)
  between operations  1.65 us (2%)
    all_to_all x1, waiting for transfers between devices, shards(): lax.all_to_all(spectrum, ORDER, split_axis=0, concat_axis=0, tiled=True)  43.6 us
    all_to_all x1, waiting for transfers between devices, send(): return lax.all_to_all(sums, ORDER, split_axis=0, concat_axis=0, tiled=True)  16 us
    all_to_all x1, starting transfers between devices, shards(): lax.all_to_all(spectrum, ORDER, split_axis=0, concat_axis=0, tiled=True)  12 us
    pallas_call x1, Pallas kernels, shards(): pl.pallas_call(sections_kernel, grid=(SHARE // 2,), in_specs=[pl.BlockSpe...  9.92 us
    pallas_call x1, Pallas kernels, shards(): pl.pallas_call(functools.partial(spectrum_kernel, chunks, parts), in_spec...  8.01 us
    all_to_all x1, starting transfers between devices, send(): return lax.all_to_all(sums, ORDER, split_axis=0, concat_axis=0, tiled=True)  7.24 us
    broadcast_in_dim x4, local copies, waits for them, and re-layouts, shards(): jnp.where(same, weights, jnp.zeros((), bf16))  2.47 us
  transfers between devices with their start and end apart: 2, of which 2 were waited for; matrix products, arithmetic and copies ran while one was open for 6% of the time, Pallas kernels for 0%

profile of v9, /device:TPU:1, one launch (start us, length us, event | category | flops | bytes accessed | tf_op | source)
XLA Modules:
  0.0 106.7 jit_solution(6310009257329101897)
XLA Ops:
  0.0 8.0 %spectrum.1 = bf16[2,4,2,4,2,32,512]{6,5,4,3,2,1,0:T(8,128)(2,1)} custom-call(bf16[1024,1024]{1,0:T(8,128)(2,1)} %constant.123.clone.table_hbm, bf16[128,16384]{1,0:T(8,128)(2,1)} %traces_hbm.1), custom_call_target="tpu_custom_call" | custom-call | tf_op jit(solution)/shard_map/spectrum/pallas_call | solution.py:335
  8.0 0.0 copy-start.8
  8.0 0.0 copy-start.9
  8.0 0.0 copy-start.10
  8.1 0.0 copy-start.7
  8.1 12.0 %all-to-all-start.1 = ((bf16[128,32,512]{2,1,0:T(8,128)(2,1)}), bf16[128,32,512]{2,1,0:T(8,128)(2,1)}, u32[]{:S(2)}, u32[]{:S(2)}) async-start(bf16[128,32,512]{2,1,0:T(8,128)(2,1)} %bitcast.39), calls=%async_computation.1 | async-start | bytes 8388608 | tf_op jit(solution)/shard_map/all_to_all | solution.py:353
  20.1 0.0 copy-done.8
  20.1 0.0 copy-done.9
  20.1 0.0 copy-done.10
  20.1 0.2 convert_reduce_fusion
  20.3 0.6 minimum_add_fusion
  21.6 0.0 copy-done.7
  21.6 0.1 fusion.8
  21.7 0.1 copy.17
  21.8 0.3 copy.15
  22.1 0.6 fusion.12
  23.4 0.1 fusion.11
  23.5 0.1 iota_compare_fusion.3
  23.6 0.1 maximum_convert_fusion
  23.6 0.1 select_reduce_fusion
  23.8 0.0 copy-start
  23.8 0.0 copy-start.1
  23.8 0.0 copy-start.2
  23.8 0.0 copy-start.3
  23.8 0.0 copy-start.4
  23.8 0.0 copy-start.5
  23.8 0.4 broadcast_in_dim.82
  24.3 1.5 %broadcast_in_dim.83 = bf16[3,128,256]{2,1,0:T(8,128)(2,1)S(1)} reshape(bf16[3,16,8,16,16]{4,3,2,1,0:T(8,128)(2,1)S(1)} %broadcast_in_dim.82) | data formatting | bytes 393216 | tf_op jit(solution)/shard_map/jit(_where)/broadcast_in_dim | solution.py:375
  25.8 0.1 broadcast_in_dim.55
  25.9 0.5 broadcast_in_dim.56
  26.4 43.6 %all-to-all-done.1.cells_ref = bf16[128,32,512]{2,1,0:T(8,128)(2,1)} async-done(((bf16[128,32,512]{2,1,0:T(8,128)(2,1)}), bf16[128,32,512]{2,1,0:T(8,128)(2,1)}, u32[]{:S(2)}, u32[]{:S(2)}) %all-to-all-start.1) | async-done | bytes 4194336 | tf_op jit(solution)/shard_map/all_to_all | solution.py:353
  70.0 0.0 copy-done
  70.0 0.0 copy-done.1
  70.0 0.0 copy-done.2
  70.1 0.0 copy-done.3
  70.1 0.0 copy-done.4
  70.1 9.9 %sections.1 = (bf16[128,32,128]{2,1,0:T(8,128)(2,1)}, bf16[2,128,32,128]{3,2,1,0:T(8,128)(2,1)}) custom-call(bf16[128,32,512]{2,1,0:T(8,128)(2,1)} %all-to-all-done.1.cells_ref, bf16[256,256]{1,0:T(8,128)(2,1)S(1)} %copy-done, bf16[256,256]{1,0:T(8,128)(2,1)S(1)} %copy-done.1, bf16[256,256]{1,0:T(8,128)(2,1)S(1)} %copy-done.2, ...), custom_call_target="tpu_custom_call" | custom-call | tf_op jit(solution)/shard_map/sections/pallas_call | solution.py:379
  80.0 0.1 broadcast_in_dim.85
  80.1 0.2 while.14
  80.3 7.2 %all-to-all-start.2 = ((bf16[128,32,128]{2,1,0:T(8,128)(2,1)}), bf16[128,32,128]{2,1,0:T(8,128)(2,1)S(1)}, u32[]{:S(2)}, u32[]{:S(2)}) async-start(bf16[128,32,128]{2,1,0:T(8,128)(2,1)} %get-tuple-element.115), calls=%async_computation.2 | async-start | bytes 2097152 | tf_op jit(solution)/shard_map/all_to_all | solution.py:428
  87.5 0.0 copy-start.6
  87.5 0.1 iota_add_fusion.1
  87.6 0.1 iota_compare_fusion.2
  87.7 0.7 and_convert_fusion
  88.4 0.7 reshape.258
  89.1 0.2 copy.16.places_ref
  89.3 16.0 %all-to-all-done.2.sums_ref = bf16[128,32,128]{2,1,0:T(8,128)(2,1)S(1)} async-done(((bf16[128,32,128]{2,1,0:T(8,128)(2,1)}), bf16[128,32,128]{2,1,0:T(8,128)(2,1)S(1)}, u32[]{:S(2)}, u32[]{:S(2)}) %all-to-all-start.2) | async-done | bytes 1048608 | tf_op jit(solution)/shard_map/all_to_all | solution.py:428
  105.2 1.5 %cepstra.1 = f32[16,64,128]{2,1,0:T(8,128)} custom-call(bf16[128,32,128]{2,1,0:T(8,128)(2,1)S(1)} %all-to-all-done.2.sums_ref, bf16[256,1024]{1,0:T(8,128)(2,1)S(1)} %copy.16.places_ref, f32[256,512]{1,0:T(8,128)S(1)} %get-tuple-element.117.rest_ref, f32[64,64]{1,0:T(8,128)S(1)} %copy-done.6), custom_call_target="tpu_custom_call" | custom-call | tf_op jit(solution)/shard_map/cepstra/pallas_call | solution.py:439
  (7 shorter events, 0.1 us)
Async XLA Ops:
  8.0 12.0 %copy-start.8 = (s32[66]{0:T(128)S(1)}, s32[66]{0:T(128)}, u32[]{:S(2)}) copy-start(s32[66]{0:T(128)} %param.16) | copy-start | bytes 796
  8.0 12.0 %copy-start.9 = (s32[32]{0:T(128)S(1)}, s32[32]{0:T(128)}, u32[]{:S(2)}) copy-start(s32[32]{0:T(128)} %constant.124.clone) | copy-start | bytes 388
  8.0 12.0 %copy-start.10 = (s32[32]{0:T(128)S(1)}, s32[32]{0:T(128)}, u32[]{:S(2)}) copy-start(s32[32]{0:T(128)} %constant.133) | copy-start | bytes 388
  8.1 13.5 %copy-start.7 = (s32[16,16384]{1,0:T(8,128)S(1)}, s32[16,16384]{1,0:T(8,128)}, u32[]{:S(2)}) copy-start(s32[16,16384]{1,0:T(8,128)} %param.15) | copy-start | bytes 3145732
  8.1 62.0 %all-to-all-start.1 = ((bf16[128,32,512]{2,1,0:T(8,128)(2,1)}), bf16[128,32,512]{2,1,0:T(8,128)(2,1)}, u32[]{:S(2)}, u32[]{:S(2)}) async-start(bf16[128,32,512]{2,1,0:T(8,128)(2,1)} %bitcast.39), calls=%async_computation.1 | async-start | bytes 8388608 | tf_op jit(solution)/shard_map/all_to_all | solution.py:353
  23.8 46.3 %copy-start = (bf16[256,256]{1,0:T(8,128)(2,1)S(1)}, bf16[256,256]{1,0:T(8,128)(2,1)}, u32[]{:S(2)}) copy-start(bf16[256,256]{1,0:T(8,128)(2,1)} %constant.125.clone.first_ref) | copy-start | bytes 393220
  23.8 46.3 %copy-start.1 = (bf16[256,256]{1,0:T(8,128)(2,1)S(1)}, bf16[256,256]{1,0:T(8,128)(2,1)}, u32[]{:S(2)}) copy-start(bf16[256,256]{1,0:T(8,128)(2,1)} %constant.126.clone.second_ref) | copy-start | bytes 393220
  23.8 46.3 %copy-start.2 = (bf16[256,256]{1,0:T(8,128)(2,1)S(1)}, bf16[256,256]{1,0:T(8,128)(2,1)}, u32[]{:S(2)}) copy-start(bf16[256,256]{1,0:T(8,128)(2,1)} %constant.127.clone.third_ref) | copy-start | bytes 393220
  23.8 46.2 %copy-start.3 = (bf16[256,256]{1,0:T(8,128)(2,1)S(1)}, bf16[256,256]{1,0:T(8,128)(2,1)}, u32[]{:S(2)}) copy-start(bf16[256,256]{1,0:T(8,128)(2,1)} %constant.128.clone.fourth_ref) | copy-start | bytes 393220
  23.8 46.2 %copy-start.4 = (f32[2,128,128]{2,1,0:T(8,128)S(1)}, f32[2,128,128]{2,1,0:T(8,128)}, u32[]{:S(2)}) copy-start(f32[2,128,128]{2,1,0:T(8,128)} %constant.129.clone.forward_ref) | copy-start | bytes 393220
  23.8 46.2 %copy-start.5 = (f32[2,128,128]{2,1,0:T(8,128)S(1)}, f32[2,128,128]{2,1,0:T(8,128)}, u32[]{:S(2)}) copy-start(f32[2,128,128]{2,1,0:T(8,128)} %constant.130.clone.inverse_ref) | copy-start | bytes 393220
  80.3 25.0 %all-to-all-start.2 = ((bf16[128,32,128]{2,1,0:T(8,128)(2,1)}), bf16[128,32,128]{2,1,0:T(8,128)(2,1)S(1)}, u32[]{:S(2)}, u32[]{:S(2)}) async-start(bf16[128,32,128]{2,1,0:T(8,128)(2,1)} %get-tuple-element.115), calls=%async_computation.2 | async-start | bytes 2097152 | tf_op jit(solution)/shard_map/all_to_all | solution.py:428
  87.5 17.7 %copy-start.6 = (f32[64,64]{1,0:T(8,128)S(1)}, f32[64,64]{1,0:T(8,128)}, u32[]{:S(2)}) copy-start(f32[64,64]{1,0:T(8,128)} %constant.131.clone.cosine_ref) | copy-start | bytes 49156

commit v10 on v8

--- a/solution.py
+++ b/solution.py
@@ -191,7 +191,7 @@
     rest_sem,
 ):
     group = 16
-    step = 2
+    step = 4
     bf16 = jnp.bfloat16
     dot = functools.partial(jnp.dot, preferred_element_type=jnp.float32)
     fwd_cos, fwd_sin = forward_ref[0], forward_ref[1]

time: 107 us -> 107 us (level)
  no operation moved by 1% of the time
where the time goes in v10:
time: 107 us
  waiting for transfers between devices  59.6 us (56%)
  Pallas kernels  19.4 us (18%)
  starting transfers between devices  19.2 us (18%)
  local copies, waits for them, and re-layouts  3.84 us (4%)
  other arithmetic  2.82 us (3%)
  between operations  1.65 us (2%)
    all_to_all x1, waiting for transfers between devices, shards(): lax.all_to_all(spectrum, ORDER, split_axis=0, concat_axis=0, tiled=True)  43.6 us
    all_to_all x1, waiting for transfers between devices, send(): return lax.all_to_all(sums, ORDER, split_axis=0, concat_axis=0, tiled=True)  16 us
    all_to_all x1, starting transfers between devices, shards(): lax.all_to_all(spectrum, ORDER, split_axis=0, concat_axis=0, tiled=True)  12 us
    pallas_call x1, Pallas kernels, shards(): pl.pallas_call(sections_kernel, grid=(SHARE // 2,), in_specs=[pl.BlockSpe...  9.92 us
    pallas_call x1, Pallas kernels, shards(): pl.pallas_call(functools.partial(spectrum_kernel, chunks, parts), in_spec...  8.01 us
    all_to_all x1, starting transfers between devices, send(): return lax.all_to_all(sums, ORDER, split_axis=0, concat_axis=0, tiled=True)  7.24 us
    broadcast_in_dim x4, local copies, waits for them, and re-layouts, shards(): jnp.where(same, weights, jnp.zeros((), bf16))  2.47 us
  transfers between devices with their start and end apart: 2, of which 2 were waited for; matrix products, arithmetic and copies ran while one was open for 6% of the time, Pallas kernels for 0%

profile of v10, /device:TPU:1, one launch (start us, length us, event | category | flops | bytes accessed | tf_op | source)
XLA Modules:
  0.0 106.7 jit_solution(7601665259686182400)
XLA Ops:
  0.0 8.0 %spectrum.1 = bf16[2,4,2,4,2,32,512]{6,5,4,3,2,1,0:T(8,128)(2,1)} custom-call(bf16[1024,1024]{1,0:T(8,128)(2,1)} %constant.123.clone.table_hbm, bf16[128,16384]{1,0:T(8,128)(2,1)} %traces_hbm.1), custom_call_target="tpu_custom_call" | custom-call | tf_op jit(solution)/shard_map/spectrum/pallas_call | solution.py:335
  8.0 0.0 copy-start.8
  8.0 0.0 copy-start.9
  8.0 0.0 copy-start.10
  8.1 0.0 copy-start.7
  8.1 12.0 %all-to-all-start.1 = ((bf16[128,32,512]{2,1,0:T(8,128)(2,1)}), bf16[128,32,512]{2,1,0:T(8,128)(2,1)}, u32[]{:S(2)}, u32[]{:S(2)}) async-start(bf16[128,32,512]{2,1,0:T(8,128)(2,1)} %bitcast.39), calls=%async_computation.1 | async-start | bytes 8388608 | tf_op jit(solution)/shard_map/all_to_all | solution.py:353
  20.1 0.0 copy-done.8
  20.1 0.0 copy-done.9
  20.1 0.0 copy-done.10
  20.1 0.2 convert_reduce_fusion
  20.3 0.6 minimum_add_fusion
  21.6 0.0 copy-done.7
  21.6 0.1 fusion.8
  21.7 0.1 copy.17
  21.8 0.3 copy.15
  22.1 0.6 fusion.12
  23.4 0.1 fusion.11
  23.5 0.1 iota_compare_fusion.3
  23.6 0.1 maximum_convert_fusion
  23.6 0.1 select_reduce_fusion
  23.8 0.0 copy-start
  23.8 0.0 copy-start.1
  23.8 0.0 copy-start.2
  23.8 0.0 copy-start.3
  23.8 0.0 copy-start.4
  23.8 0.0 copy-start.5
  23.8 0.4 broadcast_in_dim.82
  24.3 1.5 %broadcast_in_dim.83 = bf16[3,128,256]{2,1,0:T(8,128)(2,1)S(1)} reshape(bf16[3,16,8,16,16]{4,3,2,1,0:T(8,128)(2,1)S(1)} %broadcast_in_dim.82) | data formatting | bytes 393216 | tf_op jit(solution)/shard_map/jit(_where)/broadcast_in_dim | solution.py:375
  25.8 0.1 broadcast_in_dim.55
  25.9 0.5 broadcast_in_dim.56
  26.4 43.6 %all-to-all-done.1.cells_ref = bf16[128,32,512]{2,1,0:T(8,128)(2,1)} async-done(((bf16[128,32,512]{2,1,0:T(8,128)(2,1)}), bf16[128,32,512]{2,1,0:T(8,128)(2,1)}, u32[]{:S(2)}, u32[]{:S(2)}) %all-to-all-start.1) | async-done | bytes 4194336 | tf_op jit(solution)/shard_map/all_to_all | solution.py:353
  70.0 0.0 copy-done
  70.0 0.0 copy-done.1
  70.0 0.0 copy-done.2
  70.1 0.0 copy-done.3
  70.1 9.9 %sections.1 = (bf16[128,32,128]{2,1,0:T(8,128)(2,1)}, bf16[2,128,32,128]{3,2,1,0:T(8,128)(2,1)}) custom-call(bf16[128,32,512]{2,1,0:T(8,128)(2,1)} %all-to-all-done.1.cells_ref, bf16[256,256]{1,0:T(8,128)(2,1)S(1)} %copy-done, bf16[256,256]{1,0:T(8,128)(2,1)S(1)} %copy-done.1, bf16[256,256]{1,0:T(8,128)(2,1)S(1)} %copy-done.2, ...), custom_call_target="tpu_custom_call" | custom-call | tf_op jit(solution)/shard_map/sections/pallas_call | solution.py:379
  80.0 0.1 broadcast_in_dim.85
  80.1 0.2 while.14
  80.3 7.2 %all-to-all-start.2 = ((bf16[128,32,128]{2,1,0:T(8,128)(2,1)}), bf16[128,32,128]{2,1,0:T(8,128)(2,1)S(1)}, u32[]{:S(2)}, u32[]{:S(2)}) async-start(bf16[128,32,128]{2,1,0:T(8,128)(2,1)} %get-tuple-element.115), calls=%async_computation.2 | async-start | bytes 2097152 | tf_op jit(solution)/shard_map/all_to_all | solution.py:428
  87.5 0.0 copy-start.6
  87.5 0.1 iota_add_fusion.1
  87.6 0.1 iota_compare_fusion.2
  87.7 0.7 and_convert_fusion
  88.4 0.7 reshape.258
  89.1 0.2 copy.16.places_ref
  89.3 16.0 %all-to-all-done.2.sums_ref = bf16[128,32,128]{2,1,0:T(8,128)(2,1)S(1)} async-done(((bf16[128,32,128]{2,1,0:T(8,128)(2,1)}), bf16[128,32,128]{2,1,0:T(8,128)(2,1)S(1)}, u32[]{:S(2)}, u32[]{:S(2)}) %all-to-all-start.2) | async-done | bytes 1048608 | tf_op jit(solution)/shard_map/all_to_all | solution.py:428
  105.2 0.0 copy-done.6
  105.2 1.5 %cepstra.1 = f32[16,64,128]{2,1,0:T(8,128)} custom-call(bf16[128,32,128]{2,1,0:T(8,128)(2,1)S(1)} %all-to-all-done.2.sums_ref, bf16[256,1024]{1,0:T(8,128)(2,1)S(1)} %copy.16.places_ref, f32[256,512]{1,0:T(8,128)S(1)} %get-tuple-element.117.rest_ref, f32[64,64]{1,0:T(8,128)S(1)} %copy-done.6), custom_call_target="tpu_custom_call" | custom-call | tf_op jit(solution)/shard_map/cepstra/pallas_call | solution.py:439
  (7 shorter events, 0.1 us)
Async XLA Ops:
  8.0 12.0 %copy-start.8 = (s32[66]{0:T(128)S(1)}, s32[66]{0:T(128)}, u32[]{:S(2)}) copy-start(s32[66]{0:T(128)} %param.16) | copy-start | bytes 796
  8.0 12.0 %copy-start.9 = (s32[32]{0:T(128)S(1)}, s32[32]{0:T(128)}, u32[]{:S(2)}) copy-start(s32[32]{0:T(128)} %constant.124.clone) | copy-start | bytes 388
  8.0 12.0 %copy-start.10 = (s32[32]{0:T(128)S(1)}, s32[32]{0:T(128)}, u32[]{:S(2)}) copy-start(s32[32]{0:T(128)} %constant.133) | copy-start | bytes 388
  8.1 13.5 %copy-start.7 = (s32[16,16384]{1,0:T(8,128)S(1)}, s32[16,16384]{1,0:T(8,128)}, u32[]{:S(2)}) copy-start(s32[16,16384]{1,0:T(8,128)} %param.15) | copy-start | bytes 3145732
  8.1 62.0 %all-to-all-start.1 = ((bf16[128,32,512]{2,1,0:T(8,128)(2,1)}), bf16[128,32,512]{2,1,0:T(8,128)(2,1)}, u32[]{:S(2)}, u32[]{:S(2)}) async-start(bf16[128,32,512]{2,1,0:T(8,128)(2,1)} %bitcast.39), calls=%async_computation.1 | async-start | bytes 8388608 | tf_op jit(solution)/shard_map/all_to_all | solution.py:353
  23.8 46.3 %copy-start = (bf16[256,256]{1,0:T(8,128)(2,1)S(1)}, bf16[256,256]{1,0:T(8,128)(2,1)}, u32[]{:S(2)}) copy-start(bf16[256,256]{1,0:T(8,128)(2,1)} %constant.125.clone.first_ref) | copy-start | bytes 393220
  23.8 46.3 %copy-start.1 = (bf16[256,256]{1,0:T(8,128)(2,1)S(1)}, bf16[256,256]{1,0:T(8,128)(2,1)}, u32[]{:S(2)}) copy-start(bf16[256,256]{1,0:T(8,128)(2,1)} %constant.126.clone.second_ref) | copy-start | bytes 393220
  23.8 46.3 %copy-start.2 = (bf16[256,256]{1,0:T(8,128)(2,1)S(1)}, bf16[256,256]{1,0:T(8,128)(2,1)}, u32[]{:S(2)}) copy-start(bf16[256,256]{1,0:T(8,128)(2,1)} %constant.127.clone.third_ref) | copy-start | bytes 393220
  23.8 46.2 %copy-start.3 = (bf16[256,256]{1,0:T(8,128)(2,1)S(1)}, bf16[256,256]{1,0:T(8,128)(2,1)}, u32[]{:S(2)}) copy-start(bf16[256,256]{1,0:T(8,128)(2,1)} %constant.128.clone.fourth_ref) | copy-start | bytes 393220
  23.8 46.2 %copy-start.4 = (f32[2,128,128]{2,1,0:T(8,128)S(1)}, f32[2,128,128]{2,1,0:T(8,128)}, u32[]{:S(2)}) copy-start(f32[2,128,128]{2,1,0:T(8,128)} %constant.129.clone.forward_ref) | copy-start | bytes 393220
  23.8 46.2 %copy-start.5 = (f32[2,128,128]{2,1,0:T(8,128)S(1)}, f32[2,128,128]{2,1,0:T(8,128)}, u32[]{:S(2)}) copy-start(f32[2,128,128]{2,1,0:T(8,128)} %constant.130.clone.inverse_ref) | copy-start | bytes 393220
  80.3 25.0 %all-to-all-start.2 = ((bf16[128,32,128]{2,1,0:T(8,128)(2,1)}), bf16[128,32,128]{2,1,0:T(8,128)(2,1)S(1)}, u32[]{:S(2)}, u32[]{:S(2)}) async-start(bf16[128,32,128]{2,1,0:T(8,128)(2,1)} %get-tuple-element.115), calls=%async_computation.2 | async-start | bytes 2097152 | tf_op jit(solution)/shard_map/all_to_all | solution.py:428
  87.5 17.7 %copy-start.6 = (f32[64,64]{1,0:T(8,128)S(1)}, f32[64,64]{1,0:T(8,128)}, u32[]{:S(2)}) copy-start(f32[64,64]{1,0:T(8,128)} %constant.131.clone.cosine_ref) | copy-start | bytes 49156
